TPU v7x, 32 devices: a whole 2x2x4 slice. The times are simulated.
32 devices in a mesh: mp: 2 (over x), vocab: 8 (over z, core), rows: 2 (over y).
Axes of the slice: x: 2, y: 2, z: 4, core: 2. Of those that a mesh axis runs over, the one named last changes fastest.
Arguments:
- hidden: bfloat16 [2, 512, 4096], P('mp', None, 'rows')
- norm_gain: bfloat16 [2, 4096], P('mp', 'rows'), may hold values from 0.5 to 1.5
- head_weights: bfloat16 [2, 4096, 12288], P('mp', 'rows', 'vocab')
- pair_source: int32 [32], P('vocab'), may hold values from 0 to 23, as said below
- pair_target: int32 [32], P('vocab'), may hold values from 0 to 23, as said below
- pair_count: int32 [8], P('vocab'), may hold values from 2 to 4, as said below
- pair_weight: bfloat16 [32, 512, 512], P('vocab'), may hold values from 0.00019454956 to 0.00390625
- next_token: int32 [512], P(('mp', 'rows')), may hold values from 0 to 12287
Outputs:
- ensemble_logp: float32 [512, 12288], P(('mp', 'rows'), 'vocab')
- target_nll: float32 [512], P(('mp', 'rows'))
Inputs may be any that keep to these rules, and one draw needn't show every extreme that they name: `pair_target`: slot p targets one of the blocks of its own shard, (p // 4) * 3 to (p // 4) * 3 + 2. `pair_source`: slot p's source block lies from (p // 4) * 3 - 3 to (p // 4) * 3 + 2 * 3 - 1; slot 0 of every shard but the first and the last takes the block just below the shard's own, slot 1 of every shard but the last the block just above. The live slots of a shard are its first pair_count ones.
All inputs are finite; a program needn't handle non-finite values.
Results may differ from a plain program's by a relative error of at most 0.0003.
Values may be sent and summed in bfloat16 or wider, within the bound.
No kernel may reach another device: no remote copies, remote signals or barrier semaphores. Data moves between devices by JAX's collectives and lax.ppermute only.
A program may use at most 128 MiB of HBM per device.

v0:
```python
import jax
import jax.numpy as jnp
from jax import lax
from jax.sharding import PartitionSpec as P


def with_halo(block, sides, width):
    for axis, dim in sides:
        count = lax.axis_size(axis)
        forward = [(i, i + 1) for i in range(count - 1)]
        backward = [(target, source) for source, target in forward]
        low = lax.ppermute(
            lax.slice_in_dim(block, block.shape[dim] - width, None, axis=dim), axis, forward
        )
        high = lax.ppermute(lax.slice_in_dim(block, 0, width, axis=dim), axis, backward)
        block = jnp.concatenate([low, block, high], axis=dim)
    return block


def on_device(
    hidden, norm_gain, head_weights, pair_source, pair_target, pair_count, pair_weight, next_token
):
    model_count = lax.axis_size("mp")
    row_groups = lax.axis_size("rows")
    rows_all = hidden.shape[1]
    feat_local = hidden.shape[2]
    features = feat_local * row_groups
    half_rows = rows_all // row_groups
    quarter = half_rows // model_count
    head_local = head_weights[0]
    shard_cols = head_local.shape[1]
    block_cols = pair_weight.shape[1]
    blocks_dev = shard_cols // block_cols
    reordered = hidden[0].reshape(model_count, row_groups, quarter, feat_local)
    reordered = jnp.transpose(reordered, (1, 0, 2, 3)).reshape(rows_all, feat_local)
    own_rows = reordered.astype(jnp.float32)
    squares = lax.psum(jnp.sum(own_rows * own_rows, axis=1), "rows")
    row_scale = lax.rsqrt(squares / features + 1e-05)
    normed = own_rows * row_scale[:, None] * norm_gain[0].astype(jnp.float32)[None, :]
    head_wide = head_local.astype(jnp.float32)
    logits = lax.psum_scatter(
        jnp.dot(
            normed, head_wide, preferred_element_type=jnp.float32, precision=lax.Precision.HIGHEST
        ),
        "rows",
        scatter_dimension=0,
        tiled=True,
    )
    row_peak = lax.pmax(jnp.max(logits, axis=1), "vocab")
    row_total = lax.psum(jnp.sum(jnp.exp(logits - row_peak[:, None]), axis=1), "vocab")
    grouped = logits.reshape(model_count, quarter, shard_cols)
    peak_group = row_peak.reshape(model_count, quarter)
    total_group = row_total.reshape(model_count, quarter)
    padded = with_halo(grouped, (("vocab", 2),), shard_cols)
    received, peak_pair, total_pair = (
        lax.all_to_all(padded, "mp", split_axis=0, concat_axis=0, tiled=True),
        lax.all_to_all(peak_group, "mp", split_axis=0, concat_axis=0, tiled=True),
        lax.all_to_all(total_group, "mp", split_axis=0, concat_axis=0, tiled=True),
    )
    llama_part = received[0][:, shard_cols : 2 * shard_cols]
    qwen_part = received[1]
    llama_logp = llama_part - peak_pair[0][:, None] - jnp.log(total_pair[0])[:, None]
    qwen_prob = (jnp.exp(qwen_part - peak_pair[1][:, None]) / total_pair[1][:, None]).astype(
        jnp.bfloat16
    )
    vocab_index = lax.axis_index("vocab")
    source_local = pair_source - (vocab_index * blocks_dev - blocks_dev)
    target_local = pair_target - vocab_index * blocks_dev
    blocks = qwen_prob.reshape(quarter, 3 * blocks_dev, block_cols)
    picked_blocks = jnp.take(blocks, source_local, axis=1)
    contribution = jnp.einsum(
        "qsk,skn->sqn", picked_blocks, pair_weight, preferred_element_type=jnp.float32
    )
    live_slot = jnp.arange(pair_source.shape[0]) < pair_count[0]
    selector = (
        (target_local[:, None] == jnp.arange(blocks_dev)[None, :]) & live_slot[:, None]
    ).astype(jnp.float32)
    mapped = jnp.einsum(
        "sqn,sb->qbn", contribution, selector, precision=lax.Precision.HIGHEST
    ).reshape(quarter, shard_cols)
    mixed = jnp.logaddexp(jnp.maximum(llama_logp, -50.0), jnp.log(mapped))
    columns = vocab_index * shard_cols + jnp.arange(shard_cols, dtype=jnp.int32)
    on_target = next_token[:, None] == columns[None, :]
    picked = jnp.sum(jnp.where(on_target, mixed, 0.0), axis=1)
    row_mass, picked = lax.psum((jnp.sum(mapped, axis=1), picked), "vocab")
    log_norm = jnp.log1p(row_mass)
    return (mixed - log_norm[:, None], log_norm - picked)


def solution(mesh):
    in_specs = (
        P("mp", None, "rows"),
        P("mp", "rows"),
        P("mp", "rows", "vocab"),
        P("vocab"),
        P("vocab"),
        P("vocab"),
        P("vocab", None, None),
        P(("mp", "rows")),
    )
    out_specs = (P(("mp", "rows"), "vocab"), P(("mp", "rows")))
    return jax.shard_map(
        on_device, mesh=mesh, in_specs=in_specs, out_specs=out_specs, check_vma=False
    )
```

profile of v0, /device:TPU:0, one launch (start us, length us, event | category | flops | bytes accessed | tf_op | source)
XLA Modules:
  0.0 245.5 jit_solution(11256388552762011196)
XLA Ops:
  7.2 2.2 fusion.4
  9.4 5.9 %psum.28 = f32[512]{0:T(512)S(1)} all-reduce(f32[512]{0:T(512)S(1)} %bitcast.69), channel_id=1, replica_groups=mesh['mp'=2,'vocab'=8,'rows'=2] {'rows'}, use_global_device_ids=true, to_apply=%region_1.0 | all-reduce | flops 512 | bytes 4096 | tf_op jit(solution)/shard_map/psum | solution.py:37
  16.1 2.2 fusion.5
  20.0 11.6 %fusion = f32[512,1536]{1,0:T(8,128)} fusion(f32[512,2048]{1,0:T(8,128)S(1)} %bitcast.67, bf16[1,2048,1536]{2,1,0:T(8,128)(2,1)S(1)} %bitcast.73), kind=kOutput, calls=%fused_computation.1 | convolution fusion | flops 19327352832 | bytes 13631488 | tf_op jit(solution)/shard_map/dot_general | solution.py:42
  31.6 45.3 %reduce-scatter.2.cloned.1.call-done = f32[256,1536]{1,0:T(8,128)} async-done(((f32[512,1536]{1,0:T(8,128)}), f32[256,1536]{1,0:T(8,128)}) %reduce-scatter.2.cloned.1.call-update) | async-done | bytes 1572880 | tf_op jit(solution)/shard_map/reduce_scatter | solution.py:41
  76.9 3.1 %copy.37 = f32[2,128,1536]{1,2,0:T(8,128)} copy(f32[2,128,1536]{2,1,0:T(8,128)} %bitcast.63) | data formatting | bytes 3145728 | tf_op jit(solution)/shard_map/reshape | solution.py:51
  81.2 4.3 %collective-permute-start = (f32[2,128,1536]{1,2,0:T(8,128)}, f32[2,128,1536]{1,2,0:T(8,128)}, u32[]{:S(2)}, u32[]{:S(2)}) collective-permute-start(f32[2,128,1536]{1,2,0:T(8,128)} %copy.37), channel_id=1, source_target_pairs={{0,2},{2,4},{4,6},{6,8},{8,10},{10,12},{12,14},{1,3},{3,5},{5,7},{... | collective-permute-start | bytes 4718600 | tf_op jit(solution)/shard_map/ppermute | solution.py:12
  85.5 1.6 reduce_max.9
  87.0 23.8 %pmax.7 = f32[256]{0:T(256)} all-reduce(f32[256]{0:T(256)S(1)} %reduce_max.9), channel_id=1, replica_groups=mesh['mp'=2,'vocab'=8,'rows'=2] {'vocab'}, use_global_device_ids=true, to_apply=%region_4.0 | all-reduce | flops 256 | bytes 2048 | tf_op jit(solution)/shard_map/pmax | solution.py:49
  110.8 1.8 exponential_reduce_fusion
  112.6 15.8 %psum.29 = f32[2,1,128]{2,1,0:T(1,128)S(1)} all-reduce(f32[2,1,128]{2,1,0:T(1,128)S(1)} %bitcast.71), channel_id=1, replica_groups=mesh['mp'=2,'vocab'=8,'rows'=2] {'vocab'}, use_global_device_ids=true, to_apply=%region_6.0 | all-reduce | flops 256 | bytes 2048 | tf_op jit(solution)/shard_map/psum | solution.py:50
  128.4 6.3 %all_to_all.23 = f32[2,1,128]{2,1,0:T(1,128)S(1)} all-to-all(f32[2,1,128]{2,1,0:T(1,128)S(1)} %psum.29), channel_id=1, replica_groups=mesh['mp'=2,'vocab'=8,'rows'=2] {'mp'}, dimensions={0} | all-to-all | bytes 2048 | tf_op jit(solution)/shard_map/all_to_all | solution.py:58
  134.6 3.2 %all-to-all-start.1 = ((f32[2,1,128]{2,1,0:T(1,128)}), f32[2,1,128]{2,1,0:T(1,128)S(1)}, u32[]{:S(2)}, u32[]{:S(2)}) async-start(f32[2,1,128]{2,1,0:T(1,128)} %bitcast.10), calls=%async_computation.2 | async-start | bytes 2048 | tf_op jit(solution)/shard_map/all_to_all | solution.py:57
  137.9 4.8 %pad_maximum_fusion = f32[2,128,4608]{1,2,0:T(8,128)} fusion(f32[2,128,1536]{1,2,0:T(8,128)} %collective-permute-done.1, f32[2,128,1536]{1,2,0:T(8,128)} %copy.37, f32[2,128,1536]{1,2,0:T(8,128)} %collective-permute-done), kind=kLoop, calls=%fused_computation.3 | loop fusion | flops 2359296 | bytes 9437184 | tf_op jit(solution)/shard_map/concatenate | solution.py:16
  142.7 6.1 %all-to-all-start = ((f32[2,128,4608]{1,2,0:T(8,128)}), f32[2,128,4608]{1,2,0:T(8,128)}, u32[]{:S(2)}, u32[]{:S(2)}) async-start(f32[2,128,4608]{1,2,0:T(8,128)} %pad_maximum_fusion), calls=%async_computation.1 | async-start | bytes 9437184 | tf_op jit(solution)/shard_map/all_to_all | solution.py:56
  149.6 49.0 %all-to-all-done = f32[2,128,4608]{1,2,0:T(8,128)} async-done(((f32[2,128,4608]{1,2,0:T(8,128)}), f32[2,128,4608]{1,2,0:T(8,128)}, u32[]{:S(2)}, u32[]{:S(2)}) %all-to-all-start) | async-done | bytes 4718624 | tf_op jit(solution)/shard_map/all_to_all | solution.py:56
  198.5 4.8 %slice_bitcast_fusion = (f32[128,4608]{0,1:T(8,128)}, f32[1,128,4608]{1,2,0:T(8,128)}) fusion(f32[2,128,4608]{1,2,0:T(8,128)} %all-to-all-done), kind=kLoop, calls=%fused_computation.9 | loop fusion | bytes 9437184 | tf_op jit(solution)/shard_map/squeeze | solution.py:60
  203.3 3.2 %copy.40 = f32[128,9,512]{2,0,1:T(8,128)} copy(f32[128,9,512]{0,2,1:T(8,128)} %bitcast.64) | data formatting | bytes 4718592 | tf_op jit(solution)/shard_map/squeeze | solution.py:61
  206.5 2.1 divide_convert_fusion
  211.5 3.1 %log_bitcast_fusion = (f32[128,3,512]{2,1,0:T(4,128)}, f32[128]{0:T(128)S(1)}) fusion(f32[4,128,512]{2,1,0:T(8,128)S(1)} %fusion.12, s32[4]{0:T(128)S(1)} %broadcast_subtract_fusion.1, pred[4]{0:T(512)(128)(4,1)S(1)} %iota_compare_fusion.1), kind=kOutput, calls=%fused_computation.14 | convolution fusion | flops 9633688 | bytes 1835540 | tf_op jit(solution)/shard_map/sqn,sb->qbn/dot_general | solution.py:78
  216.2 1.9 select_reduce_fusion
  218.1 15.2 %all-reduce = (f32[128]{0:T(128)S(1)}, f32[128]{0:T(128)S(1)}) all-reduce(f32[128]{0:T(128)S(1)} %get-tuple-element.17, f32[128]{0:T(128)S(1)} %select_reduce_fusion), channel_id=1, replica_groups=mesh['mp'=2,'vocab'=8,'rows'=2] {'vocab'}, use_global_device_ids=true, to_apply=%region_8.9 | all-reduce | flops 256 | bytes 2048 | tf_op jit(solution)/shard_map/psum | solution.py:85
  233.7 2.7 %broadcast_subtract_fusion = f32[128,1536]{0,1:T(8,128)} fusion(f32[128]{0:T(128)S(1)} %get-tuple-element.23, f32[128,3,512]{0,2,1:T(8,128)S(1)} %copy.42, f32[128]{0:T(128)S(1)} %get-tuple-element.20, f32[128]{0:T(128)S(1)} %get-tuple-element.18, f32[128,4608]{0,1:T(8,128)} %get-tuple-element.14), kind=kLoop, calls=%fused_computation.28 | loop fusion | flops 2359296 | bytes 2360832 | tf_op jit(solution)/shard_map/sub | solution.py:87
  236.4 2.3 copy.43
  (35 shorter events, 8.8 us)
Async XLA Ops:
  7.2 202.8 %copy-start = (bf16[4,512,512]{2,1,0:T(8,128)(2,1)S(1)}, bf16[4,512,512]{2,1,0:T(8,128)(2,1)}, u32[]{:S(2)}) copy-start(bf16[4,512,512]{2,1,0:T(8,128)(2,1)} %param.14) | copy-start | bytes 6291460
  7.2 69.7 %reduce-scatter.2.cloned.1.call-start = ((), (), s32[]{:S(2)}) async-start(), calls=%async_computation.4 | async-start | bytes 4718592 | tf_op jit(solution)/shard_map/reduce_scatter | solution.py:41
  16.0 2.8 %slice-start = ((s8[6291456]{0:T(1024)(128)(4,1)}), s8[4194304]{0:T(1024)(128)(4,1)S(1)}, s32[]{:S(2)}) async-start(s8[6291456]{0:T(1024)(128)(4,1)} %bitcast.72), calls=%async_computation.5 | async-start | bytes 8388608
  18.3 1.7 slice-start.1
  79.9 57.9 %collective-permute-start.1 = (f32[2,128,1536]{1,2,0:T(8,128)}, f32[2,128,1536]{1,2,0:T(8,128)}, u32[]{:S(2)}, u32[]{:S(2)}) collective-permute-start(f32[2,128,1536]{1,2,0:T(8,128)} %copy.37), channel_id=1, source_target_pairs={{2,0},{4,2},{6,4},{8,6},{10,8},{12,10},{14,12},{3,1},{5,3},{7,5},{... | collective-permute-start | bytes 4718600 | tf_op jit(solution)/shard_map/ppermute | solution.py:15
  81.2 56.6 %collective-permute-start = (f32[2,128,1536]{1,2,0:T(8,128)}, f32[2,128,1536]{1,2,0:T(8,128)}, u32[]{:S(2)}, u32[]{:S(2)}) collective-permute-start(f32[2,128,1536]{1,2,0:T(8,128)} %copy.37), channel_id=1, source_target_pairs={{0,2},{2,4},{4,6},{6,8},{8,10},{10,12},{12,14},{1,3},{3,5},{5,7},{... | collective-permute-start | bytes 4718600 | tf_op jit(solution)/shard_map/ppermute | solution.py:12
  134.6 8.0 %all-to-all-start.1 = ((f32[2,1,128]{2,1,0:T(1,128)}), f32[2,1,128]{2,1,0:T(1,128)S(1)}, u32[]{:S(2)}, u32[]{:S(2)}) async-start(f32[2,1,128]{2,1,0:T(1,128)} %bitcast.10), calls=%async_computation.2 | async-start | bytes 2048 | tf_op jit(solution)/shard_map/all_to_all | solution.py:57
  142.6 6.8 %copy-start.2 = (s32[4]{0:T(128)S(1)}, s32[4]{0:T(128)}, u32[]{:S(2)}) copy-start(s32[4]{0:T(128)} %param.11) | copy-start | bytes 52
  142.6 6.9 %copy-start.3 = (s32[4]{0:T(128)S(1)}, s32[4]{0:T(128)}, u32[]{:S(2)}) copy-start(s32[4]{0:T(128)} %param.12) | copy-start | bytes 52
  142.7 55.9 %all-to-all-start = ((f32[2,128,4608]{1,2,0:T(8,128)}), f32[2,128,4608]{1,2,0:T(8,128)}, u32[]{:S(2)}, u32[]{:S(2)}) async-start(f32[2,128,4608]{1,2,0:T(8,128)} %pad_maximum_fusion), calls=%async_computation.1 | async-start | bytes 9437184 | tf_op jit(solution)/shard_map/all_to_all | solution.py:56
  211.5 4.7 %copy-start.1 = (s32[128]{0:T(128)S(1)}, s32[128]{0:T(128)}, u32[]{:S(2)}) copy-start(s32[128]{0:T(128)} %param.15) | copy-start | bytes 1540
Sparse Core Ops, SparseCore 0:
  31.7 45.0 reduce-scatter.1
where the time goes:
time: 246 us
  waiting for transfers between devices  94.3 us (38%)
  blocking collectives  66.8 us (27%)
  other arithmetic  20.5 us (8%)
  local copies, waits for them, and re-layouts  17.9 us (7%)
  matrix products  16.2 us (7%)
  starting transfers between devices  14.9 us (6%)
  between operations  14.9 us (6%)
    all_to_all x1, waiting for transfers between devices, on_device(): lax.all_to_all(padded, 'mp', split_axis=0, concat_axis=0, tiled=True)  49 us
    reduce_scatter x1, waiting for transfers between devices, on_device(): lax.psum_scatter(jnp.dot(normed, head_wide, preferred_element_type=jnp.fl...  45.3 us
    pmax x1, blocking collectives, on_device(): row_peak = lax.pmax(jnp.max(logits, axis=1), 'vocab')  23.8 us
    psum x1, blocking collectives, on_device(): lax.psum(jnp.sum(jnp.exp(logits - row_peak[:, None]), axis=1), 'vocab')  15.8 us
    psum x1, blocking collectives, on_device(): row_mass, picked = lax.psum((jnp.sum(mapped, axis=1), picked), 'vocab')  15.2 us
    dot_general x1, matrix products, on_device(): jnp.dot(normed, head_wide, preferred_element_type=jnp.float32, precision=...  11.6 us
    all_to_all x1, blocking collectives, on_device(): lax.all_to_all(total_group, 'mp', split_axis=0, concat_axis=0, tiled=True)  6.26 us
    all_to_all x1, starting transfers between devices, on_device(): lax.all_to_all(padded, 'mp', split_axis=0, concat_axis=0, tiled=True)  6.13 us
  transfers between devices with their start and end apart: 5, of which 2 were waited for; matrix products, arithmetic and copies ran while one was open for 3% of the time, Pallas kernels for 0%

commit v1 on v0

v1 whole, which is shorter than its diff:
```python
import functools

import jax
import jax.numpy as jnp
from jax import lax
from jax.experimental import pallas as pl
from jax.experimental.pallas import tpu as pltpu
from jax.sharding import PartitionSpec as P

LANES = 128
EXTRA = 16
CODE = 512
HEAD_COPIES = 4
TOP = 32767.0
LEAST = 1e-30
FLOOR = 1.9287498479639178e-22
VMEM = 16 * 1024 * 1024

f32, bf16, i32, i16 = jnp.float32, jnp.bfloat16, jnp.int32, jnp.int16


def params():
    return pltpu.CompilerParams(vmem_limit_bytes=VMEM)


def exponent(value):
    return jnp.ceil(jnp.log2(jnp.maximum(value, LEAST)))


def columns_to_lanes(values, rows):
    lanes = lax.broadcasted_iota(i32, (rows, LANES), 1)
    out = jnp.zeros((rows, LANES), f32)
    for place, value in enumerate(values):
        out = jnp.where(lanes == place, value, out)
    return out


def split_exact(gained):
    high = gained.astype(bf16)
    return high, (gained - high.astype(f32)).astype(bf16)


def encode(values, power):
    size = jnp.sqrt(jnp.abs(values) * jnp.exp2(-power)) * TOP
    code = jnp.minimum(size + 0.5, TOP).astype(i32)
    return jnp.where(values < 0, -code, code).astype(i16)


def decode(codes, power):
    wide = codes.astype(i32).astype(f32)
    return wide * jnp.abs(wide) * (jnp.exp2(power) * (1.0 / (TOP * TOP)))


def encode_scalar(value):
    power = exponent(value)
    mantissa = jnp.maximum(value, LEAST) * jnp.exp2(-power) * 16384.0
    first = jnp.floor(mantissa)
    return power, first, jnp.floor((mantissa - first) * 16384.0)


def decode_scalar(power, first, second):
    return (first + second * (1.0 / 16384.0)) * (1.0 / 16384.0) * jnp.exp2(power)


def prepare(hidden, gain, left_ref, at):
    rows = hidden.shape[0]
    values = hidden.astype(f32)
    high, low = split_exact(values * gain)
    left_ref[pl.ds(at, rows), :] = high
    left_ref[pl.ds(at + rows, rows), :] = low
    return jnp.sum(values * values, axis=1, keepdims=True)


def put_codes(out_ref, both, first):
    rows = both.shape[0] // 2
    part = both[:rows] + both[rows:]
    power = exponent(jnp.max(jnp.abs(part), axis=1, keepdims=True))
    codes = encode(part, power)
    for k in range(part.shape[1] // LANES):
        out_ref[pl.ds((first // LANES + k) * rows, rows), :] = codes[:, k * LANES : (k + 1) * LANES]
    return power


def put_extra(out_ref, powers, squares):
    rows = squares.shape[0]
    extra = columns_to_lanes(powers + list(encode_scalar(squares)), rows)
    body = out_ref.shape[0] - EXTRA
    out_ref[pl.ds(body, EXTRA), :] = jnp.transpose(extra)[:EXTRA].astype(i32).astype(i16)


def first_kernel(kinds, rows, quarter_ref, hidden_ref, gain_ref, head_ref, *refs):
    count = len(kinds)
    left_refs, square_refs, head_out = refs[:count], refs[count : 2 * count], refs[2 * count]
    held, gain_held, sems, gain_sem, head_sems = refs[2 * count + 1 :]
    copies = []
    for place, which in enumerate(kinds):
        at = pl.ds(pl.multiple_of(quarter_ref[which] * rows, rows), rows)
        copies.append(pltpu.make_async_copy(hidden_ref.at[at, :], held.at[place], sems.at[place]))
    gain_copy = pltpu.make_async_copy(gain_ref, gain_held, gain_sem)
    deep = head_ref.shape[0] // HEAD_COPIES
    spans = [pl.ds(k * deep, deep) for k in range(HEAD_COPIES)]
    head_copies = [
        pltpu.make_async_copy(head_ref.at[at, :], head_out.at[at, :], head_sems.at[k])
        for k, at in enumerate(spans)
    ]
    gain_copy.start()
    for copy in copies + head_copies:
        copy.start()
    gain_copy.wait()
    gain = gain_held[...].astype(f32)
    for place, copy in enumerate(copies):
        copy.wait()
        squares = prepare(held[place], gain, left_refs[place], 0)
        square_refs[place][...] = jnp.broadcast_to(squares, (rows, LANES))
    for copy in head_copies:
        copy.wait()


def first_prep(quarters, hidden, gain, head, kinds):
    rows, feats, count = hidden.shape[0] // 4, hidden.shape[1], len(kinds)
    hbm = pl.BlockSpec(memory_space=pltpu.HBM)
    outs = pl.pallas_call(
        functools.partial(first_kernel, kinds, rows),
        in_specs=[pl.BlockSpec(memory_space=pltpu.SMEM), hbm, hbm, hbm],
        out_shape=[jax.ShapeDtypeStruct((2 * rows, feats), bf16)] * count
        + [jax.ShapeDtypeStruct((rows, LANES), f32)] * count
        + [jax.ShapeDtypeStruct(head.shape, head.dtype)],
        scratch_shapes=[
            pltpu.VMEM((count, rows, feats), bf16),
            pltpu.VMEM(gain.shape, bf16),
            pltpu.SemaphoreType.DMA((count,)),
            pltpu.SemaphoreType.DMA,
            pltpu.SemaphoreType.DMA((HEAD_COPIES,)),
        ],
        compiler_params=params(),
        cost_estimate=pl.CostEstimate(
            flops=8 * count * rows * feats, bytes_accessed=2 * head.size, transcendentals=0
        ),
        name="first_prep",
    )(quarters, hidden, gain, head)
    return outs[:count], outs[count : 2 * count], outs[2 * count]


def encode_kernel(count, both_ref, *refs):
    square_refs, outs = refs[:count], refs[count:]
    rows, cols = both_ref.shape[0] // count // 2, both_ref.shape[1]
    for place, out_ref in enumerate(outs):
        powers = []
        for first in range(0, cols, CODE):
            both = both_ref[pl.ds(2 * place * rows, 2 * rows), pl.ds(first, CODE)]
            powers.append(put_codes(out_ref, both, first))
        put_extra(out_ref, powers, square_refs[place][:, :1])


def encode_parts(both, squares):
    count = len(squares)
    rows, cols = both.shape[0] // count // 2, both.shape[1]
    return pl.pallas_call(
        functools.partial(encode_kernel, count),
        out_shape=[jax.ShapeDtypeStruct((cols // LANES * rows + EXTRA, LANES), i16)] * count,
        compiler_params=params(),
        cost_estimate=pl.CostEstimate(
            flops=20 * count * rows * cols, bytes_accessed=10 * count * rows * cols, transcendentals=count * rows * cols
        ),
        name="encode_parts",
    )(both, *squares)


def product(left, head):
    return jnp.dot(left, head, preferred_element_type=f32)


def side_kernel(width, blocks, own_which, meta_ref, quarter_ref, token_ref, hidden_ref, gain_ref, w_ref, near_ref, own_ref, far_ref, left_ref, squares_ref, held, gain_held, w_held, sum_ref, sem, gain_sem, w_sems):
    rows = token_ref.shape[1]
    slots = w_ref.shape[0]
    at = pl.ds(pl.multiple_of(quarter_ref[own_which] * rows, rows), rows)
    hidden_copy = pltpu.make_async_copy(hidden_ref.at[at, :], held, sem)
    gain_copy = pltpu.make_async_copy(gain_ref, gain_held, gain_sem)
    w_copies = [pltpu.make_async_copy(w_ref.at[k], w_held.at[k], w_sems.at[k]) for k in range(slots)]
    gain_copy.start()
    hidden_copy.start()
    for copy in w_copies:
        copy.start()
    shard = meta_ref[1]
    near_at = jnp.where(shard % 2 == 0, 2, 0)
    token = jnp.transpose(jnp.broadcast_to(token_ref[...].astype(f32), (8, rows)))[:, :1].astype(i32)
    place = lax.broadcasted_iota(i32, (rows, width), 1)
    sum_ref[...] = jnp.zeros_like(sum_ref)
    gain_copy.wait()
    hidden_copy.wait()
    squares = prepare(held[...], gain_held[...].astype(f32), left_ref, 0)
    squares_ref[...] = jnp.broadcast_to(squares, (rows, LANES))
    for slot in range(slots):
        w_copies[slot].wait()

        @pl.when(slot < meta_ref[2 + 2 * slots])
        def _():
            source = jnp.clip(meta_ref[2 + slot] - (shard - 1) * blocks, 0, 3 * blocks - 1)
            hits = (token - meta_ref[2 + slots + slot] * width == place).astype(bf16)
            left = jnp.concatenate([hits, jnp.ones((EXTRA, width), bf16)], axis=0)
            found = lax.dot_general(
                left, w_held[slot], (((1,), (1,)), ((), ())), preferred_element_type=f32
            )
            at = pl.ds(pl.multiple_of(source % blocks * width, width), width)
            sum_ref[source // blocks, :, at] += found

    order = lax.broadcasted_iota(i32, (EXTRA, 1), 0)
    for out_ref, k in ((near_ref, near_at), (own_ref, 1), (far_ref, 2 - near_at)):
        out_ref[pl.ds(0, rows), :] = sum_ref[k, pl.ds(0, rows), :].astype(bf16)
        sums = sum_ref[k, pl.ds(rows, EXTRA), :]
        first = sums.astype(bf16).astype(f32)
        second = (sums - first).astype(bf16).astype(f32)
        third = sums - first - second
        parts = jnp.where(order == 0, first, jnp.where(order == 1, second, jnp.where(order == 2, third, 0.0)))
        out_ref[pl.ds(rows, EXTRA), :] = parts.astype(bf16)


def side_parts(meta, quarters, token, hidden, gain, weights, width, cols):
    rows, feats = token.shape[1], hidden.shape[1]
    smem = pl.BlockSpec(memory_space=pltpu.SMEM)
    hbm = pl.BlockSpec(memory_space=pltpu.HBM)
    outs = pl.pallas_call(
        functools.partial(side_kernel, width, cols // width, 0),
        in_specs=[smem, smem, pl.BlockSpec(memory_space=pltpu.VMEM), hbm, hbm, hbm],
        out_shape=[jax.ShapeDtypeStruct((rows + EXTRA, cols), bf16)] * 3
        + [jax.ShapeDtypeStruct((2 * rows, feats), bf16), jax.ShapeDtypeStruct((rows, LANES), f32)],
        scratch_shapes=[
            pltpu.VMEM((rows, feats), bf16),
            pltpu.VMEM(gain.shape, bf16),
            pltpu.VMEM(weights.shape, bf16),
            pltpu.VMEM((3, rows + EXTRA, cols), f32),
            pltpu.SemaphoreType.DMA,
            pltpu.SemaphoreType.DMA,
            pltpu.SemaphoreType.DMA((weights.shape[0],)),
        ],
        compiler_params=params(),
        cost_estimate=pl.CostEstimate(flops=1, bytes_accessed=1, transcendentals=0),
        name="side_parts",
    )(meta, quarters, token, hidden, gain, weights)
    return outs[:3], outs[3], outs[4]


def extras(ref, rows):
    tile = ref[pl.ds(ref.shape[0] - EXTRA, EXTRA), :].astype(i32).astype(f32)
    wide = jnp.transpose(tile)
    groups = (ref.shape[0] - EXTRA) // rows * LANES // CODE
    at = [wide[:, j : j + 1] for j in range(groups + 3)]
    return at[:groups], decode_scalar(*at[groups:])


def model_logits(mine, features, own_ref, squares_ref, cy_ref, cx_ref, cd_ref, out_ref):
    rows = squares_ref.shape[0]
    cols = own_ref.shape[1]

    def run(scale, at_slab):
        for slab in range(cols // LANES):
            out_ref[:, pl.ds(slab * LANES, LANES)] = at_slab(slab) * scale

    @pl.when(mine)
    def _():
        power_y, squares_y = extras(cy_ref, rows)

        def at_slab(slab):
            at = pl.ds(slab * LANES, LANES)
            own = own_ref[pl.ds(0, rows), at] + own_ref[pl.ds(rows, rows), at]
            return own + decode(cy_ref[pl.ds(slab * rows, rows), :], power_y[slab * LANES // CODE])

        run(lax.rsqrt((squares_ref[:, :1] + squares_y) / features + 1e-05), at_slab)

    @pl.when(jnp.logical_not(mine))
    def _():
        power_x, squares_x = extras(cx_ref, rows)
        power_d, squares_d = extras(cd_ref, rows)

        def at_slab(slab):
            part, group = pl.ds(slab * rows, rows), slab * LANES // CODE
            return decode(cx_ref[part, :], power_x[group]) + decode(cd_ref[part, :], power_d[group])

        run(lax.rsqrt((squares_x + squares_d) / features + 1e-05), at_slab)

    peak = jnp.full((rows, LANES), -jnp.inf, f32)
    for slab in range(cols // LANES):
        peak = jnp.maximum(peak, out_ref[:, pl.ds(slab * LANES, LANES)])
    return jnp.max(peak, axis=1, keepdims=True)


def qwen_kernel(width, blocks, features, meta_ref, own_ref, squares_ref, cy_ref, cx_ref, cd_ref, u_ref, stats_ref, q_ref):
    rows = squares_ref.shape[0]
    body = blocks * width
    peak = model_logits(meta_ref[0] == 1, features, own_ref, squares_ref, cy_ref, cx_ref, cd_ref, q_ref)
    total = jnp.zeros((rows, 1), f32)
    for j in range(blocks):
        at = pl.ds(j * width, width)
        qwen = jnp.exp(q_ref[:, at] - peak)
        u_ref[:, at] = qwen.astype(bf16)
        total += jnp.sum(qwen, axis=1, keepdims=True)
    first = peak.astype(bf16).astype(f32)
    second = (peak - first).astype(bf16).astype(f32)
    third = peak - first - second
    u_ref[:, body:] = columns_to_lanes([first, second, third], rows).astype(bf16)
    stats_ref[...] = columns_to_lanes([peak, total], rows)


def join_qwen(meta, own, squares, codes, width, features):
    rows, cols = own.shape[0] // 2, own.shape[1]
    whole = pl.BlockSpec(memory_space=pltpu.VMEM)
    return pl.pallas_call(
        functools.partial(qwen_kernel, width, cols // width, features),
        in_specs=[pl.BlockSpec(memory_space=pltpu.SMEM)] + [whole] * 5,
        out_shape=[
            jax.ShapeDtypeStruct((rows, cols + LANES), bf16),
            jax.ShapeDtypeStruct((rows, LANES), f32),
        ],
        scratch_shapes=[pltpu.VMEM((rows, cols), f32)],
        compiler_params=params(),
        cost_estimate=pl.CostEstimate(flops=1, bytes_accessed=8 * 1024 * 1024, transcendentals=0),
        name="join_qwen",
    )(meta, own, squares, *codes)


def llama_kernel(width, blocks, features, meta_ref, own_ref, squares_ref, cy_ref, cx_ref, cd_ref, token_ref, u_ref, near_ref, mine_ref, far_ref, before_ref, e_ref, stats_ref):
    rows = squares_ref.shape[0]
    body = blocks * width
    columns_refs = (near_ref, mine_ref, far_ref)
    peak = model_logits(meta_ref[0] == 0, features, own_ref, squares_ref, cy_ref, cx_ref, cd_ref, e_ref)
    total = jnp.zeros((rows, 1), f32)
    mass = jnp.zeros((rows, 1), f32)
    pick_e = jnp.zeros((rows, 1), f32)
    pick_m = jnp.zeros((rows, 1), f32)
    token = jnp.transpose(jnp.broadcast_to(token_ref[...].astype(f32), (8, rows)))
    token = token[:, :1].astype(i32) - meta_ref[1] * body
    for j in range(blocks):
        at = pl.ds(j * width, width)
        llama = jnp.exp(e_ref[:, at] - peak)
        e_ref[:, at] = llama
        total += jnp.sum(llama, axis=1, keepdims=True)
        hit = lax.broadcasted_iota(i32, (rows, width), 1) + j * width == token
        pick_e += jnp.sum(jnp.where(hit, llama, 0.0), axis=1, keepdims=True)
        held = u_ref[:, at].astype(f32)
        columns = functools.reduce(jnp.add, [ref[pl.ds(0, rows), at].astype(f32) for ref in columns_refs])
        pick_m += jnp.sum(held * columns, axis=1, keepdims=True)
        sums = functools.reduce(jnp.add, [ref[pl.ds(rows, EXTRA), at].astype(f32) for ref in columns_refs])
        mass += jnp.sum(held * jnp.sum(sums, axis=0, keepdims=True), axis=1, keepdims=True)
    before = before_ref[...]
    stats = columns_to_lanes([peak, total, before[:, 0:1], before[:, 1:2], mass, pick_e, pick_m], rows)
    stats_ref[...] = jnp.transpose(stats)[:8]


def join_llama(meta, own, squares, codes, token, u, columns, stats, width, features):
    rows, cols = own.shape[0] // 2, own.shape[1]
    whole = pl.BlockSpec(memory_space=pltpu.VMEM)
    return pl.pallas_call(
        functools.partial(llama_kernel, width, cols // width, features),
        in_specs=[pl.BlockSpec(memory_space=pltpu.SMEM)] + [whole] * 11,
        out_shape=[jax.ShapeDtypeStruct((rows, cols), f32), jax.ShapeDtypeStruct((8, rows), f32)],
        compiler_params=params(),
        cost_estimate=pl.CostEstimate(flops=1, bytes_accessed=8 * 1024 * 1024, transcendentals=0),
        name="join_llama",
    )(meta, own, squares, *codes, token, u, *columns, stats)


def map_kernel(width, blocks, shards, meta_ref, u_ref, near_ref, far_ref, w_ref, m_ref, top_ref, all_ref, scale_ref):
    rows = u_ref.shape[0]
    body = blocks * width
    shard = meta_ref[1]
    slots = w_ref.shape[0]
    near_at = jnp.where(shard % 2 == 0, 2, 0)

    def peak_of(ref):
        lanes = ref[:, body:].astype(f32)
        return lanes[:, 0:1] + lanes[:, 1:2] + lanes[:, 2:3]

    own_peak = peak_of(u_ref)
    near_peak = peak_of(near_ref)
    far_peak = jnp.where((shard > 0) & (shard < shards - 1), peak_of(far_ref), own_peak)
    top = jnp.maximum(jnp.maximum(near_peak, far_peak), own_peak)
    for k, ref, peak in ((near_at, near_ref, near_peak), (1, u_ref, own_peak), (2 - near_at, far_ref, far_peak)):
        all_ref[k] = ref[:, :body]
        scale_ref[k] = jnp.broadcast_to(jnp.exp(peak - top), (rows, LANES))
    m_ref[...] = jnp.zeros_like(m_ref)
    for slot in range(slots):

        @pl.when(slot < meta_ref[2 + 2 * slots])
        def _():
            source = jnp.clip(meta_ref[2 + slot] - (shard - 1) * blocks, 0, 3 * blocks - 1)
            target = jnp.clip(meta_ref[2 + slots + slot] - shard * blocks, 0, blocks - 1)
            inside = pl.multiple_of(source % blocks * width, width)
            picked = all_ref[source // blocks, :, pl.ds(inside, width)]
            term = jnp.dot(picked, w_ref[slot], preferred_element_type=f32)
            at = pl.ds(pl.multiple_of(target * width, width), width)
            m_ref[:, at] += term * scale_ref[source // blocks][:, :1]

    top_ref[...] = jnp.broadcast_to(top, (rows, LANES))


def map_parts(meta, u, near, far, weights, width, shards):
    rows, cols = u.shape[0], u.shape[1] - LANES
    blocks = cols // width
    whole = pl.BlockSpec(memory_space=pltpu.VMEM)
    return pl.pallas_call(
        functools.partial(map_kernel, width, blocks, shards),
        in_specs=[pl.BlockSpec(memory_space=pltpu.SMEM)] + [whole] * 4,
        out_shape=[jax.ShapeDtypeStruct((rows, cols), f32), jax.ShapeDtypeStruct((rows, LANES), f32)],
        scratch_shapes=[pltpu.VMEM((3, rows, cols), bf16), pltpu.VMEM((3, rows, LANES), f32)],
        compiler_params=params(),
        cost_estimate=pl.CostEstimate(
            flops=2 * rows * weights.size, bytes_accessed=2 * weights.size, transcendentals=0
        ),
        name="map_parts",
    )(meta, u, near, far, weights)


def finish_kernel(pieces, *refs):
    stats_refs, (e_ref, m_ref, m_top_ref, out_ref, nll_ref) = refs[:pieces], refs[pieces:]
    stats = [ref[k : k + 8, :] for ref in stats_refs for k in range(0, ref.shape[0], 8)]
    shards = range(len(stats))
    row = lambda s, k: stats[s][k : k + 1, :]
    top_l = functools.reduce(jnp.maximum, [row(s, 0) for s in shards])
    top_q = functools.reduce(jnp.maximum, [row(s, 2) for s in shards])
    sum_l = functools.reduce(jnp.add, [row(s, 1) * jnp.exp(row(s, 0) - top_l) for s in shards])
    sum_q = functools.reduce(jnp.add, [row(s, 3) * jnp.exp(row(s, 2) - top_q) for s in shards])
    part_l = [jnp.exp(row(s, 0) - top_l) / sum_l for s in shards]
    part_q = [jnp.exp(row(s, 2) - top_q) / sum_q for s in shards]
    mass = functools.reduce(jnp.add, [row(s, 4) * part_q[s] for s in shards])
    pick_e = functools.reduce(jnp.add, [row(s, 5) * part_l[s] for s in shards])
    pick_m = functools.reduce(jnp.add, [row(s, 6) * part_q[s] for s in shards])
    log_norm = jnp.log1p(mass)
    nll_ref[...] = log_norm - jnp.log(jnp.maximum(pick_e, FLOOR) + pick_m)
    tile = jnp.concatenate([part_l[0], top_q, 1.0 / sum_q, log_norm, jnp.zeros((4, log_norm.shape[1]), f32)], axis=0)
    turned = jnp.transpose(tile)
    a, top, share, c = (turned[:, i : i + 1] for i in range(4))
    b = jnp.exp(m_top_ref[:, :1] - top) * share
    out_ref[...] = jnp.log(jnp.maximum(e_ref[...] * a, FLOOR) + m_ref[...] * b) - c


def finish(pieces, e, m, m_top):
    rows, cols = e.shape
    return pl.pallas_call(
        functools.partial(finish_kernel, len(pieces)),
        out_shape=[
            jax.ShapeDtypeStruct((rows, cols), f32),
            jax.ShapeDtypeStruct((1, rows), f32),
        ],
        compiler_params=params(),
        cost_estimate=pl.CostEstimate(
            flops=20 * rows * cols, bytes_accessed=12 * rows * cols, transcendentals=2 * rows * cols
        ),
        name="finish",
    )(*pieces, e, m, m_top)


def gather_pieces(own, shards):
    pieces, step = [own], 1
    while step < shards:
        radix = 4 if step > 1 and 4 * step <= shards else 2
        sent = pieces[0] if len(pieces) == 1 else jnp.concatenate(pieces, axis=0)
        for turn in range(1, radix):
            pieces.append(lax.ppermute(sent, "vocab", [(i, i ^ (turn * step)) for i in range(shards)]))
        step *= radix
    return pieces


def on_device(
    hidden, norm_gain, head_weights, pair_source, pair_target, pair_count, pair_weight, next_token
):
    shards = lax.axis_size("vocab")
    row_groups = lax.axis_size("rows")
    hidden, head = hidden[0], head_weights[0]
    token = next_token[None, :]
    held_hidden = pltpu.with_memory_space_constraint(hidden, pltpu.HBM)
    held_weight = pltpu.with_memory_space_constraint(pair_weight, pltpu.HBM)
    held_gain = pltpu.with_memory_space_constraint(norm_gain, pltpu.HBM)
    head = pltpu.with_memory_space_constraint(head, pltpu.HBM)
    width = pair_weight.shape[1]
    features = hidden.shape[1] * row_groups
    model, shard, side = (lax.axis_index(name).astype(i32) for name in ("mp", "vocab", "rows"))
    mine = 2 * model + side
    quarters = jnp.stack([mine, mine ^ 1, mine ^ 2, mine ^ 3])
    meta = jnp.concatenate([jnp.stack([model, shard]), pair_source, pair_target, pair_count])

    inside = [(i, i ^ 1) for i in range(shards)]
    across = [(i, i + 1 if i % 2 else i - 1) for i in range(1, shards - 1)]
    lefts, squares, head = first_prep(quarters, held_hidden, held_gain, head, (3, 1, 2))
    (to_d,) = encode_parts(product(lefts[0], head), squares[:1])
    from_d = lax.ppermute(to_d, ("mp", "rows"), [(0, 3), (1, 2), (2, 1), (3, 0)])
    left_y, _ = lax.optimization_barrier((lefts[1], to_d))
    (to_y,) = encode_parts(product(left_y, head), squares[1:2])
    from_y = lax.ppermute(to_y, "rows", [(0, 1), (1, 0)])
    left_x, _ = lax.optimization_barrier((lefts[2], to_y))
    (to_x,) = encode_parts(product(left_x, head), squares[2:])
    from_x = lax.ppermute(to_x, "mp", [(0, 1), (1, 0)])
    early, _ = lax.optimization_barrier((meta, to_x))
    (to_near, columns, to_far), left_own, squares_own = side_parts(
        early, quarters, token, held_hidden, held_gain, held_weight, width, head.shape[1]
    )
    far_columns = lax.ppermute(to_far, "vocab", across)
    near_columns = lax.ppermute(to_near, "vocab", inside)
    own = product(left_own, head)

    codes = (from_y, from_x, from_d)
    u, stats = join_qwen(meta, own, squares_own, codes, width, features)
    far = lax.ppermute(u, "vocab", across)
    near = lax.ppermute(u, "vocab", inside)
    e, stats = join_llama(
        meta, own, squares_own, codes, token, u, (near_columns, columns, far_columns), stats, width, features
    )
    m, m_top = map_parts(meta, u, near, far, pair_weight, width, shards)
    out, nll = finish(gather_pieces(stats, shards), e, m, m_top)
    return out, nll[0]


def solution(mesh):
    in_specs = (
        P("mp", None, "rows"),
        P("mp", "rows"),
        P("mp", "rows", "vocab"),
        P("vocab"),
        P("vocab"),
        P("vocab"),
        P("vocab", None, None),
        P(("mp", "rows")),
    )
    out_specs = (P(("mp", "rows"), "vocab"), P(("mp", "rows")))
    return jax.shard_map(
        on_device, mesh=mesh, in_specs=in_specs, out_specs=out_specs, check_vma=False
    )
```

time: 246 us -> 46.6 us (0.19)
  waiting for transfers between devices: 94.3 us -> 4.33 us
  blocking collectives: 66.8 us -> 0 us
  other arithmetic: 20.5 us -> 0.08 us
  local copies, waits for them, and re-layouts: 17.9 us -> 0.1 us
  Pallas kernels: 0 us -> 16.7 us
  between operations: 14.9 us -> 1.44 us
  matrix products: 16.2 us -> 9.9 us
    all_to_all x2 -> x0, waiting for transfers between devices: 49 us -> none  [the longest x1 49 us: on_device(): lax.all_to_all(padded, 'mp', split_axis=0, concat_axis=0, tiled=True)]
    reduce_scatter x1 -> x0, waiting for transfers between devices: 45.3 us -> none  [on_device(): lax.psum_scatter(jnp.dot(normed, head_wide, preferred_element_type=jnp.fl...]
    psum x3 -> x0, blocking collectives: 36.8 us -> none  [the longest x1 15.8 us: on_device(): lax.psum(jnp.sum(jnp.exp(logits - row_peak[:, None]), axis=1), 'vocab')]
    pmax x1 -> x0, blocking collectives: 23.8 us -> none  [on_device(): row_peak = lax.pmax(jnp.max(logits, axis=1), 'vocab')]
    pallas_call x0 -> x9, Pallas kernels: none -> 16.7 us  [the longest x1 4.32 us: first_prep(): pl.pallas_call(functools.partial(first_kernel, kinds, rows), in_specs=[pl...]
    all_to_all x2 -> x0, starting transfers between devices: 9.32 us -> none  [the longest x1 6.13 us: on_device(): lax.all_to_all(padded, 'mp', split_axis=0, concat_axis=0, tiled=True)]
    squeeze x2 -> x0, local copies, waits for them, and re-layouts: 7.96 us -> none  [the longest x1 4.8 us: on_device(): llama_part = received[0][:, shard_cols:2 * shard_cols]]
    ppermute x2 -> x11, starting transfers between devices: 5.55 us -> 13.5 us  [the longest x4 4.46 us: gather_pieces(): lax.ppermute(sent, 'vocab', [(i, i ^ turn * step) for i in range(shards)])]
  transfers between devices with their start and end apart: 5 -> 11, of which waited for: 2 -> 4; matrix products, arithmetic and copies ran while one was open for 3% -> 18% of each run, Pallas kernels for 0% -> 23%
where the time goes in v1:
time: 46.6 us; the launch traced here: 46 us
  Pallas kernels  16.7 us (36%)
  starting transfers between devices  13.5 us (29%)
  matrix products  9.9 us (21%)
  waiting for transfers between devices  4.33 us (9%)
  between operations  1.44 us (3%)
    dot_general x4, matrix products, product(): return jnp.dot(left, head, preferred_element_type=f32)  9.9 us
    ppermute x4, starting transfers between devices, gather_pieces(): lax.ppermute(sent, 'vocab', [(i, i ^ turn * step) for i in range(shards)])  4.46 us
    pallas_call x1, Pallas kernels, first_prep(): pl.pallas_call(functools.partial(first_kernel, kinds, rows), in_specs=[pl...  4.32 us
    pallas_call x1, Pallas kernels, side_parts(): pl.pallas_call(functools.partial(side_kernel, width, cols // width, 0), i...  4.03 us
    ppermute x1, starting transfers between devices, on_device(): lax.ppermute(to_d, ('mp', 'rows'), [(0, 3), (1, 2), (2, 1), (3, 0)])  3.95 us
    ppermute x1, starting transfers between devices, on_device(): near = lax.ppermute(u, 'vocab', inside)  2.98 us
    pallas_call x3, Pallas kernels, encode_parts(): pl.pallas_call(functools.partial(encode_kernel, count), out_shape=[jax.Sh...  2.14 us
    ppermute x4, waiting for transfers between devices, gather_pieces(): lax.ppermute(sent, 'vocab', [(i, i ^ turn * step) for i in range(shards)])  2.13 us
  transfers between devices with their start and end apart: 11, of which 4 were waited for; matrix products, arithmetic and copies ran while one was open for 18% of the time, Pallas kernels for 23%

profile of v1, /device:TPU:0, one launch (start us, length us, event | category | flops | bytes accessed | tf_op | source)
XLA Modules:
  0.0 46.0 jit_solution(17434046853671818041)
XLA Ops:
  0.7 4.3 %first_prep.1 = (bf16[256,2048]{1,0:T(8,128)(2,1)S(1)}, bf16[256,2048]{1,0:T(8,128)(2,1)S(1)}, bf16[256,2048]{1,0:T(8,128)(2,1)S(1)}, f32[128,128]{1,0:T(8,128)S...) custom-call(s32[4]{0:T(128)S(1)} %pad_add_fusion.quarter_ref, ...), custom_call_target="tpu_custom_call" | custom-call | flops 6291456 | bytes 6291456 | tf_op jit(solution)/shard_map/first_prep/pallas_call | solution.py:122
  5.1 1.8 %fusion.both_ref = f32[256,1536]{1,0:T(8,128)S(1)} fusion(bf16[256,2048]{1,0:T(8,128)(2,1)S(1)} %get-tuple-element.27, bf16[2048,1536]{1,0:T(8,128)(2,1)S(1)} %get-tuple-element.28), kind=kOutput, calls=%fused_computation.3 | convolution fusion | flops 1610612736 | bytes 8912896 | tf_op jit(solution)/shard_map/dot_general | solution.py:170
  6.8 0.7 %encode_parts.3 = s16[1552,128]{1,0:T(8,128)(2,1)S(1)} custom-call(f32[256,1536]{1,0:T(8,128)S(1)} %fusion.both_ref, f32[128,128]{1,0:T(8,128)S(1)} %get-tuple-element.29.refs_0_), custom_call_target="tpu_custom_call" | custom-call | flops 3932160 | bytes 1966080 | tf_op jit(solution)/shard_map/encode_parts/pallas_call | solution.py:158
  7.6 3.9 %collective-permute-start.2 = (s16[1552,128]{1,0:T(8,128)(2,1)S(1)}, s16[1552,128]{1,0:T(8,128)(2,1)S(1)}, u32[]{:S(2)}, u32[]{:S(2)}) collective-permute-start(s16[1552,128]{1,0:T(8,128)(2,1)S(1)} %encode_parts.3), channel_id=1, source_target_pairs={{0,17},{1,16},{16,1},{17,0},{2,19},{3,18},{18,3},{19,2},{4,21},{5,... | collective-permute-start | bytes 1191944 | tf_op jit(solution)/shard_map/ppermute | solution.py:485
  11.5 1.8 %fusion.1.both_ref = f32[256,1536]{1,0:T(8,128)S(1)} fusion(bf16[256,2048]{1,0:T(8,128)(2,1)S(1)} %get-tuple-element.30, bf16[2048,1536]{1,0:T(8,128)(2,1)S(1)} %get-tuple-element.28), kind=kOutput, calls=%fused_computation.4 | convolution fusion | flops 1610612736 | bytes 8912896 | tf_op jit(solution)/shard_map/dot_general | solution.py:170
  13.3 0.7 %encode_parts.4 = s16[1552,128]{1,0:T(8,128)(2,1)S(1)} custom-call(f32[256,1536]{1,0:T(8,128)S(1)} %fusion.1.both_ref, f32[128,128]{1,0:T(8,128)S(1)} %get-tuple-element.31.refs_0_), custom_call_target="tpu_custom_call" | custom-call | flops 3932160 | bytes 1966080 | tf_op jit(solution)/shard_map/encode_parts/pallas_call | solution.py:158
  14.0 0.5 %collective-permute-start = (s16[1552,128]{1,0:T(8,128)(2,1)S(1)}, s16[1552,128]{1,0:T(8,128)(2,1)S(1)}, u32[]{:S(2)}, u32[]{:S(2)}) collective-permute-start(s16[1552,128]{1,0:T(8,128)(2,1)S(1)} %encode_parts.4), channel_id=1, source_target_pairs={{0,1},{1,0},{2,3},{3,2},{4,5},{5,4},{6,7},{7,6},{8,9},{9,8},{10,11... | collective-permute-start | bytes 1191944 | tf_op jit(solution)/shard_map/ppermute | solution.py:488
  14.5 1.8 %fusion.2.both_ref = f32[256,1536]{1,0:T(8,128)S(1)} fusion(bf16[256,2048]{1,0:T(8,128)(2,1)S(1)} %get-tuple-element.32, bf16[2048,1536]{1,0:T(8,128)(2,1)S(1)} %get-tuple-element.28), kind=kOutput, calls=%fused_computation.5 | convolution fusion | flops 1610612736 | bytes 8912896 | tf_op jit(solution)/shard_map/dot_general | solution.py:170
  16.3 0.7 %encode_parts.5 = s16[1552,128]{1,0:T(8,128)(2,1)S(1)} custom-call(f32[256,1536]{1,0:T(8,128)S(1)} %fusion.2.both_ref, f32[128,128]{1,0:T(8,128)S(1)} %get-tuple-element.33.refs_0_), custom_call_target="tpu_custom_call" | custom-call | flops 3932160 | bytes 1966080 | tf_op jit(solution)/shard_map/encode_parts/pallas_call | solution.py:158
  17.9 4.0 %side_parts.1 = (bf16[144,1536]{1,0:T(8,128)(2,1)S(1)}, bf16[144,1536]{1,0:T(8,128)(2,1)S(1)}, bf16[144,1536]{1,0:T(8,128)(2,1)S(1)}, bf16[256,2048]{1,0:T(8,128)(2,1)S(1)}, f32[128,128]{1,0:T(8,128)S(1)}) custom-call(s32[11]{0:T(128)S(1)} %concatenate.6.meta_ref, s32[4]{0:T(128)S(1)} %pad_add_fusion.quarter_ref, s32[1,128]{1,0:T(1,128)S(1)} %bitcast.18, ...), custom_call_target="tpu_custom_call" | custom-call | flops 1 | bytes 1 | tf_op jit(solution)/shard_map/side_parts/pallas_call | solution.py:222
  22.0 0.7 %collective-permute-start.4 = (bf16[144,1536]{1,0:T(8,128)(2,1)S(1)}, bf16[144,1536]{1,0:T(8,128)(2,1)S(1)}, u32[]{:S(2)}, u32[]{:S(2)}) collective-permute-start(bf16[144,1536]{1,0:T(8,128)(2,1)S(1)} %get-tuple-element.40), channel_id=1, source_target_pairs={{2,4},{4,2},{6,8},{8,6},{10,12},{12,10},{3,5},{5,3},{7,9},{9,7},{1... | collective-permute-start | bytes 1327112 | tf_op jit(solution)/shard_map/ppermute | solution.py:496
  22.7 4.6 %fusion.3.own_ref = f32[256,1536]{1,0:T(8,128)S(1)} fusion(bf16[256,2048]{1,0:T(8,128)(2,1)S(1)} %get-tuple-element.35, bf16[2048,1536]{1,0:T(8,128)(2,1)} %copy-done.2), kind=kOutput, calls=%fused_computation.6 | convolution fusion | flops 1610612736 | bytes 8912896 | tf_op jit(solution)/shard_map/dot_general | solution.py:170
  27.3 1.9 %collective-permute-done.cy_ref = s16[1552,128]{1,0:T(8,128)(2,1)S(1)} collective-permute-done((s16[1552,128]{1,0:T(8,128)(2,1)S(1)}, s16[1552,128]{1,0:T(8,128)(2,1)S(1)}, u32[]{:S(2)}, u32[]{:S(2)}) %collective-permute-start) | collective-permute-done | bytes 397344 | tf_op jit(solution)/shard_map/ppermute | solution.py:488
  29.5 1.4 %join_qwen.1 = (bf16[128,1664]{1,0:T(8,128)(2,1)S(1)}, f32[128,128]{1,0:T(8,128)S(1)}) custom-call(s32[11]{0:T(128)S(1)} %concatenate.6.meta_ref, f32[256,1536]{1,0:T(8,128)S(1)} %fusion.3.own_ref, f32[128,128]{1,0:T(8,128)S(1)} %get-tuple-element.36.squares_ref, s16[1552,128]{1,0:T(8,128)(2,1)S(1)} %collective-permute-done.cy_ref, ...), custom_call_target="tpu_custom_call" | custom-call | flops 1 | bytes 8388608 | tf_op jit(solution)/shard_map/join_qwen/pallas_call | solution.py:307
  30.9 0.7 %collective-permute-start.10 = (bf16[128,1664]{1,0:T(8,128)(2,1)S(1)}, bf16[128,1664]{1,0:T(8,128)(2,1)S(1)}, u32[]{:S(2)}, u32[]{:S(2)}) collective-permute-start(bf16[128,1664]{1,0:T(8,128)(2,1)S(1)} %get-tuple-element.37.u_ref), channel_id=1, source_target_pairs={{2,4},{4,2},{6,8},{8,6},{10,12},{12,10},{3,5},{5,3},{7,9},{9,7},{1... | collective-permute-start | bytes 1277960 | tf_op jit(solution)/shard_map/ppermute | solution.py:502
  31.6 3.0 %collective-permute-start.9 = (bf16[128,1664]{1,0:T(8,128)(2,1)S(1)}, bf16[128,1664]{1,0:T(8,128)(2,1)S(1)}, u32[]{:S(2)}, u32[]{:S(2)}) collective-permute-start(bf16[128,1664]{1,0:T(8,128)(2,1)S(1)} %get-tuple-element.37.u_ref), channel_id=1, source_target_pairs={{0,2},{2,0},{4,6},{6,4},{8,10},{10,8},{12,14},{14,12},{1,3},{3,1},... | collective-permute-start | bytes 1277960 | tf_op jit(solution)/shard_map/ppermute | solution.py:503
  34.6 1.7 %join_llama.1 = (f32[128,1536]{1,0:T(8,128)S(1)}, f32[8,128]{1,0:T(8,128)S(1)}) custom-call(s32[11]{0:T(128)S(1)} %concatenate.6.meta_ref, f32[256,1536]{1,0:T(8,128)S(1)} %fusion.3.own_ref, f32[128,128]{1,0:T(8,128)S(1)} %get-tuple-element.36.squares_ref, s16[1552,128]{1,0:T(8,128)(2,1)S(1)} %collective-permute-done.cy_ref, ...), custom_call_target="tpu_custom_call" | custom-call | flops 1 | bytes 8388608 | tf_op jit(solution)/shard_map/join_llama/pallas_call | solution.py:352
  36.3 1.1 %collective-permute-done.5.refs_1_ = f32[8,128]{1,0:T(8,128)S(1)} collective-permute-done((f32[8,128]{1,0:T(8,128)S(1)}, f32[8,128]{1,0:T(8,128)S(1)}, u32[]{:S(2)}, u32[]{:S(2)}) %collective-permute-start.5) | collective-permute-done | bytes 4128 | tf_op jit(solution)/shard_map/ppermute | solution.py:458
  37.5 2.7 %collective-permute-start.8 = (f32[16,128]{1,0:T(8,128)S(1)}, f32[16,128]{1,0:T(8,128)S(1)}, u32[]{:S(2)}, u32[]{:S(2)}) collective-permute-start(f32[16,128]{1,0:T(8,128)S(1)} %constant_dynamic-update-slice_fusion), channel_id=1, source_target_pairs={{0,12},{2,14},{4,8},{6,10},{8,4},{10,6},{12,0},{14,2},{1,13},{3,15... | collective-permute-start | bytes 24584 | tf_op jit(solution)/shard_map/ppermute | solution.py:458
  40.2 0.4 collective-permute-start.7
  40.6 1.3 %collective-permute-start.6 = (f32[16,128]{1,0:T(8,128)S(1)}, f32[16,128]{1,0:T(8,128)S(1)}, u32[]{:S(2)}, u32[]{:S(2)}) collective-permute-start(f32[16,128]{1,0:T(8,128)S(1)} %constant_dynamic-update-slice_fusion), channel_id=1, source_target_pairs={{0,4},{2,6},{4,0},{6,2},{8,12},{10,14},{12,8},{14,10},{1,5},{3,7},... | collective-permute-start | bytes 24584 | tf_op jit(solution)/shard_map/ppermute | solution.py:458
  41.9 1.8 %map_parts.1 = (f32[128,1536]{1,0:T(8,128)S(1)}, f32[128,128]{1,0:T(8,128)S(1)}) custom-call(s32[11]{0:T(128)S(1)} %concatenate.6.meta_ref, bf16[128,1664]{1,0:T(8,128)(2,1)S(1)} %get-tuple-element.37.u_ref, bf16[128,1664]{1,0:T(8,128)(2,1)S(1)} %collective-permute-done.9.near_ref, bf16[128,1664]{1,0:T(8,128)(2,1)S(1)} %collective-permute-done.10.far_ref, ...), custom_call_target="tpu_custom_call" | custom-call | flops 268435456 | bytes 2097152 | tf_op jit(solution)/shard_map/map_parts/pallas_call | solution.py:400
  43.7 1.0 %collective-permute-done.7.refs_3_ = f32[16,128]{1,0:T(8,128)S(1)} collective-permute-done((f32[16,128]{1,0:T(8,128)S(1)}, f32[16,128]{1,0:T(8,128)S(1)}, u32[]{:S(2)}, u32[]{:S(2)}) %collective-permute-start.7) | collective-permute-done | bytes 8224 | tf_op jit(solution)/shard_map/ppermute | solution.py:458
  44.7 1.3 %finish.1 = (f32[128,1536]{1,0:T(8,128)}, f32[1,128]{1,0:T(1,128)}) custom-call(f32[8,128]{1,0:T(8,128)S(1)} %get-tuple-element.42.refs_0_, f32[8,128]{1,0:T(8,128)S(1)} %collective-permute-done.5.refs_1_, f32[16,128]{1,0:T(8,128)S(1)} %collective-permute-done.6.refs_2_, f32[16,128]{1,0:T(8,128)S(1)} %collective-permute-done.7.refs_3_, ...), custom_call_target="tpu_custom_call" | custom-call | flops 3932160 | bytes 2359296 | tf_op jit(solution)/shard_map/finish/pallas_call | solution.py:438
  (25 shorter events, 0.8 us)
Async XLA Ops:
  5.0 9.5 %copy-start.2 = (bf16[2048,1536]{1,0:T(8,128)(2,1)}, bf16[2048,1536]{1,0:T(8,128)(2,1)S(1)}, u32[]{:S(2)}) copy-start(bf16[2048,1536]{1,0:T(8,128)(2,1)S(1)} %get-tuple-element.28) | copy-start | bytes 18874372
  7.6 19.8 %collective-permute-start.2 = (s16[1552,128]{1,0:T(8,128)(2,1)S(1)}, s16[1552,128]{1,0:T(8,128)(2,1)S(1)}, u32[]{:S(2)}, u32[]{:S(2)}) collective-permute-start(s16[1552,128]{1,0:T(8,128)(2,1)S(1)} %encode_parts.3), channel_id=1, source_target_pairs={{0,17},{1,16},{16,1},{17,0},{2,19},{3,18},{18,3},{19,2},{4,21},{5,... | collective-permute-start | bytes 1191944 | tf_op jit(solution)/shard_map/ppermute | solution.py:485
  14.0 15.2 %collective-permute-start = (s16[1552,128]{1,0:T(8,128)(2,1)S(1)}, s16[1552,128]{1,0:T(8,128)(2,1)S(1)}, u32[]{:S(2)}, u32[]{:S(2)}) collective-permute-start(s16[1552,128]{1,0:T(8,128)(2,1)S(1)} %encode_parts.4), channel_id=1, source_target_pairs={{0,1},{1,0},{2,3},{3,2},{4,5},{5,4},{6,7},{7,6},{8,9},{9,8},{10,11... | collective-permute-start | bytes 1191944 | tf_op jit(solution)/shard_map/ppermute | solution.py:488
  14.5 3.3 %copy-start.3 = (s32[4]{0:T(128)S(1)}, s32[4]{0:T(128)}, u32[]{:S(2)}) copy-start(s32[4]{0:T(128)} %param.11) | copy-start | bytes 52
  14.5 3.3 %copy-start.4 = (s32[4]{0:T(128)S(1)}, s32[4]{0:T(128)}, u32[]{:S(2)}) copy-start(s32[4]{0:T(128)} %param.12) | copy-start | bytes 52
  14.5 3.4 %copy-start.1 = (s32[128]{0:T(128)S(1)}, s32[128]{0:T(128)}, u32[]{:S(2)}) copy-start(s32[128]{0:T(128)} %param.15) | copy-start | bytes 1540
  17.0 12.5 %collective-permute-start.1 = (s16[1552,128]{1,0:T(8,128)(2,1)S(1)}, s16[1552,128]{1,0:T(8,128)(2,1)S(1)}, u32[]{:S(2)}, u32[]{:S(2)}) collective-permute-start(s16[1552,128]{1,0:T(8,128)(2,1)S(1)} %encode_parts.5), channel_id=1, source_target_pairs={{0,16},{16,0},{1,17},{17,1},{2,18},{18,2},{3,19},{19,3},{4,20},{20... | collective-permute-start | bytes 1191944 | tf_op jit(solution)/shard_map/ppermute | solution.py:491
  22.0 12.6 %collective-permute-start.3 = (bf16[144,1536]{1,0:T(8,128)(2,1)S(1)}, bf16[144,1536]{1,0:T(8,128)(2,1)S(1)}, u32[]{:S(2)}, u32[]{:S(2)}) collective-permute-start(bf16[144,1536]{1,0:T(8,128)(2,1)S(1)} %get-tuple-element.38), channel_id=1, source_target_pairs={{0,2},{2,0},{4,6},{6,4},{8,10},{10,8},{12,14},{14,12},{1,3},{3,1},... | collective-permute-start | bytes 1327112 | tf_op jit(solution)/shard_map/ppermute | solution.py:497
  22.0 12.5 %collective-permute-start.4 = (bf16[144,1536]{1,0:T(8,128)(2,1)S(1)}, bf16[144,1536]{1,0:T(8,128)(2,1)S(1)}, u32[]{:S(2)}, u32[]{:S(2)}) collective-permute-start(bf16[144,1536]{1,0:T(8,128)(2,1)S(1)} %get-tuple-element.40), channel_id=1, source_target_pairs={{2,4},{4,2},{6,8},{8,6},{10,12},{12,10},{3,5},{5,3},{7,9},{9,7},{1... | collective-permute-start | bytes 1327112 | tf_op jit(solution)/shard_map/ppermute | solution.py:496
  27.3 14.6 %copy-start = (bf16[4,512,512]{2,1,0:T(8,128)(2,1)S(1)}, bf16[4,512,512]{2,1,0:T(8,128)(2,1)}, u32[]{:S(2)}) copy-start(bf16[4,512,512]{2,1,0:T(8,128)(2,1)} %w_ref.3) | copy-start | bytes 6291460
  30.9 11.0 %collective-permute-start.10 = (bf16[128,1664]{1,0:T(8,128)(2,1)S(1)}, bf16[128,1664]{1,0:T(8,128)(2,1)S(1)}, u32[]{:S(2)}, u32[]{:S(2)}) collective-permute-start(bf16[128,1664]{1,0:T(8,128)(2,1)S(1)} %get-tuple-element.37.u_ref), channel_id=1, source_target_pairs={{2,4},{4,2},{6,8},{8,6},{10,12},{12,10},{3,5},{5,3},{7,9},{9,7},{1... | collective-permute-start | bytes 1277960 | tf_op jit(solution)/shard_map/ppermute | solution.py:502
  31.6 10.3 %collective-permute-start.9 = (bf16[128,1664]{1,0:T(8,128)(2,1)S(1)}, bf16[128,1664]{1,0:T(8,128)(2,1)S(1)}, u32[]{:S(2)}, u32[]{:S(2)}) collective-permute-start(bf16[128,1664]{1,0:T(8,128)(2,1)S(1)} %get-tuple-element.37.u_ref), channel_id=1, source_target_pairs={{0,2},{2,0},{4,6},{6,4},{8,10},{10,8},{12,14},{14,12},{1,3},{3,1},... | collective-permute-start | bytes 1277960 | tf_op jit(solution)/shard_map/ppermute | solution.py:503
  36.3 1.2 %collective-permute-start.5 = (f32[8,128]{1,0:T(8,128)S(1)}, f32[8,128]{1,0:T(8,128)S(1)}, u32[]{:S(2)}, u32[]{:S(2)}) collective-permute-start(f32[8,128]{1,0:T(8,128)S(1)} %get-tuple-element.42.refs_0_), channel_id=1, source_target_pairs={{0,2},{2,0},{4,6},{6,4},{8,10},{10,8},{12,14},{14,12},{1,3},{3,1},... | collective-permute-start | bytes 12296 | tf_op jit(solution)/shard_map/ppermute | solution.py:458
  37.5 6.2 %collective-permute-start.8 = (f32[16,128]{1,0:T(8,128)S(1)}, f32[16,128]{1,0:T(8,128)S(1)}, u32[]{:S(2)}, u32[]{:S(2)}) collective-permute-start(f32[16,128]{1,0:T(8,128)S(1)} %constant_dynamic-update-slice_fusion), channel_id=1, source_target_pairs={{0,12},{2,14},{4,8},{6,10},{8,4},{10,6},{12,0},{14,2},{1,13},{3,15... | collective-permute-start | bytes 24584 | tf_op jit(solution)/shard_map/ppermute | solution.py:458
  40.2 4.5 %collective-permute-start.7 = (f32[16,128]{1,0:T(8,128)S(1)}, f32[16,128]{1,0:T(8,128)S(1)}, u32[]{:S(2)}, u32[]{:S(2)}) collective-permute-start(f32[16,128]{1,0:T(8,128)S(1)} %constant_dynamic-update-slice_fusion), channel_id=1, source_target_pairs={{0,8},{2,10},{4,12},{6,14},{8,0},{10,2},{12,4},{14,6},{1,9},{3,11}... | collective-permute-start | bytes 24584 | tf_op jit(solution)/shard_map/ppermute | solution.py:458
  40.6 4.2 %collective-permute-start.6 = (f32[16,128]{1,0:T(8,128)S(1)}, f32[16,128]{1,0:T(8,128)S(1)}, u32[]{:S(2)}, u32[]{:S(2)}) collective-permute-start(f32[16,128]{1,0:T(8,128)S(1)} %constant_dynamic-update-slice_fusion), channel_id=1, source_target_pairs={{0,4},{2,6},{4,0},{6,2},{8,12},{10,14},{12,8},{14,10},{1,5},{3,7},... | collective-permute-start | bytes 24584 | tf_op jit(solution)/shard_map/ppermute | solution.py:458

commit v2 on v1

--- a/solution.py
+++ b/solution.py
@@ -10,7 +10,7 @@
 LANES = 128
 EXTRA = 16
 CODE = 512
-HEAD_COPIES = 4
+HEAD_COPIES = 1
 TOP = 32767.0
 LEAST = 1e-30
 FLOOR = 1.9287498479639178e-22
@@ -313,7 +313,7 @@
         ],
         scratch_shapes=[pltpu.VMEM((rows, cols), f32)],
         compiler_params=params(),
-        cost_estimate=pl.CostEstimate(flops=1, bytes_accessed=8 * 1024 * 1024, transcendentals=0),
+        cost_estimate=pl.CostEstimate(flops=20000000000, bytes_accessed=8 * 1024 * 1024, transcendentals=0),
         name="join_qwen",
     )(meta, own, squares, *codes)
 
@@ -354,7 +354,7 @@
         in_specs=[pl.BlockSpec(memory_space=pltpu.SMEM)] + [whole] * 11,
         out_shape=[jax.ShapeDtypeStruct((rows, cols), f32), jax.ShapeDtypeStruct((8, rows), f32)],
         compiler_params=params(),
-        cost_estimate=pl.CostEstimate(flops=1, bytes_accessed=8 * 1024 * 1024, transcendentals=0),
+        cost_estimate=pl.CostEstimate(flops=20000000000, bytes_accessed=8 * 1024 * 1024, transcendentals=0),
         name="join_llama",
     )(meta, own, squares, *codes, token, u, *columns, stats)
 
@@ -457,7 +457,7 @@
         for turn in range(1, radix):
             pieces.append(lax.ppermute(sent, "vocab", [(i, i ^ (turn * step)) for i in range(shards)]))
         step *= radix
-    return pieces
+    return pieces, sent
 
 
 def on_device(
@@ -500,12 +500,14 @@
     codes = (from_y, from_x, from_d)
     u, stats = join_qwen(meta, own, squares_own, codes, width, features)
     far = lax.ppermute(u, "vocab", across)
-    near = lax.ppermute(u, "vocab", inside)
     e, stats = join_llama(
         meta, own, squares_own, codes, token, u, (near_columns, columns, far_columns), stats, width, features
     )
+    pieces, last = gather_pieces(stats, shards)
+    late_u, _ = lax.optimization_barrier((u, last))
+    near = lax.ppermute(late_u, "vocab", inside)
     m, m_top = map_parts(meta, u, near, far, pair_weight, width, shards)
-    out, nll = finish(gather_pieces(stats, shards), e, m, m_top)
+    out, nll = finish(pieces, e, m, m_top)
     return out, nll[0]
 
 

time: 46.6 us -> 46.3 us (level)
  Pallas kernels: 16.7 us -> 15.2 us
  waiting for transfers between devices: 4.33 us -> 5.45 us
    ppermute x4, starting transfers between devices: 4.46 us -> 7.34 us  [gather_pieces(): lax.ppermute(sent, 'vocab', [(i, i ^ turn * step) for i in range(shards)])]
    ppermute x1, starting transfers between devices: 2.98 us -> 0.34 us  [on_device(): near = lax.ppermute(late_u, 'vocab', inside)]
    ppermute x1, waiting for transfers between devices: 1.89 us -> 2.54 us  [on_device(): from_y = lax.ppermute(to_y, 'rows', [(0, 1), (1, 0)])]
    pallas_call x1, Pallas kernels: 4.03 us -> 3.39 us  [side_parts(): pl.pallas_call(functools.partial(side_kernel, width, cols // width, 0), i...]
    ppermute x4, waiting for transfers between devices: 2.13 us -> 2.6 us  [gather_pieces(): lax.ppermute(sent, 'vocab', [(i, i ^ turn * step) for i in range(shards)])]
  transfers between devices with their start and end apart: 11 -> 11, of which waited for: 4 -> 5; matrix products, arithmetic and copies ran while one was open for 18% -> 18% of each run, Pallas kernels for 23% -> 20%
where the time goes in v2:
time: 46.3 us; the launch traced here: 45.9 us
  Pallas kernels  15.2 us (33%)
  starting transfers between devices  13.7 us (30%)
  matrix products  9.9 us (21%)
  waiting for transfers between devices  5.45 us (12%)
  between operations  1.44 us (3%)
    dot_general x4, matrix products, product(): return jnp.dot(left, head, preferred_element_type=f32)  9.9 us
    ppermute x4, starting transfers between devices, gather_pieces(): lax.ppermute(sent, 'vocab', [(i, i ^ turn * step) for i in range(shards)])  7.34 us
    ppermute x1, starting transfers between devices, on_device(): lax.ppermute(to_d, ('mp', 'rows'), [(0, 3), (1, 2), (2, 1), (3, 0)])  3.93 us
    pallas_call x1, Pallas kernels, first_prep(): pl.pallas_call(functools.partial(first_kernel, kinds, rows), in_specs=[pl...  3.89 us
    pallas_call x1, Pallas kernels, side_parts(): pl.pallas_call(functools.partial(side_kernel, width, cols // width, 0), i...  3.39 us
    ppermute x4, waiting for transfers between devices, gather_pieces(): lax.ppermute(sent, 'vocab', [(i, i ^ turn * step) for i in range(shards)])  2.6 us
    ppermute x1, waiting for transfers between devices, on_device(): from_y = lax.ppermute(to_y, 'rows', [(0, 1), (1, 0)])  2.54 us
    pallas_call x3, Pallas kernels, encode_parts(): pl.pallas_call(functools.partial(encode_kernel, count), out_shape=[jax.Sh...  2.13 us
  transfers between devices with their start and end apart: 11, of which 5 were waited for; matrix products, arithmetic and copies ran while one was open for 18% of the time, Pallas kernels for 20%

profile of v2, /device:TPU:0, one launch (start us, length us, event | category | flops | bytes accessed | tf_op | source)
XLA Modules:
  0.0 45.9 jit_solution(2751969295815328000)
XLA Ops:
  0.7 3.9 %first_prep.1 = (bf16[256,2048]{1,0:T(8,128)(2,1)S(1)}, bf16[256,2048]{1,0:T(8,128)(2,1)S(1)}, bf16[256,2048]{1,0:T(8,128)(2,1)S(1)}, f32[128,128]{1,0:T(8,128)S...) custom-call(s32[4]{0:T(128)S(1)} %pad_add_fusion.quarter_ref, ...), custom_call_target="tpu_custom_call" | custom-call | flops 6291456 | bytes 6291456 | tf_op jit(solution)/shard_map/first_prep/pallas_call | solution.py:122
  4.6 1.8 %fusion.both_ref = f32[256,1536]{1,0:T(8,128)S(1)} fusion(bf16[256,2048]{1,0:T(8,128)(2,1)S(1)} %get-tuple-element.28, bf16[2048,1536]{1,0:T(8,128)(2,1)S(1)} %get-tuple-element.29), kind=kOutput, calls=%fused_computation.3 | convolution fusion | flops 1610612736 | bytes 8912896 | tf_op jit(solution)/shard_map/dot_general | solution.py:170
  6.4 0.7 %encode_parts.3 = s16[1552,128]{1,0:T(8,128)(2,1)S(1)} custom-call(f32[256,1536]{1,0:T(8,128)S(1)} %fusion.both_ref, f32[128,128]{1,0:T(8,128)S(1)} %get-tuple-element.30.refs_0_), custom_call_target="tpu_custom_call" | custom-call | flops 3932160 | bytes 1966080 | tf_op jit(solution)/shard_map/encode_parts/pallas_call | solution.py:158
  7.1 3.9 %collective-permute-start.2 = (s16[1552,128]{1,0:T(8,128)(2,1)S(1)}, s16[1552,128]{1,0:T(8,128)(2,1)S(1)}, u32[]{:S(2)}, u32[]{:S(2)}) collective-permute-start(s16[1552,128]{1,0:T(8,128)(2,1)S(1)} %encode_parts.3), channel_id=1, source_target_pairs={{0,17},{1,16},{16,1},{17,0},{2,19},{3,18},{18,3},{19,2},{4,21},{5,... | collective-permute-start | bytes 1191944 | tf_op jit(solution)/shard_map/ppermute | solution.py:485
  11.0 1.8 %fusion.1.both_ref = f32[256,1536]{1,0:T(8,128)S(1)} fusion(bf16[256,2048]{1,0:T(8,128)(2,1)S(1)} %get-tuple-element.31, bf16[2048,1536]{1,0:T(8,128)(2,1)S(1)} %get-tuple-element.29), kind=kOutput, calls=%fused_computation.4 | convolution fusion | flops 1610612736 | bytes 8912896 | tf_op jit(solution)/shard_map/dot_general | solution.py:170
  12.8 0.7 %encode_parts.4 = s16[1552,128]{1,0:T(8,128)(2,1)S(1)} custom-call(f32[256,1536]{1,0:T(8,128)S(1)} %fusion.1.both_ref, f32[128,128]{1,0:T(8,128)S(1)} %get-tuple-element.32.refs_0_), custom_call_target="tpu_custom_call" | custom-call | flops 3932160 | bytes 1966080 | tf_op jit(solution)/shard_map/encode_parts/pallas_call | solution.py:158
  13.5 0.5 %collective-permute-start = (s16[1552,128]{1,0:T(8,128)(2,1)S(1)}, s16[1552,128]{1,0:T(8,128)(2,1)S(1)}, u32[]{:S(2)}, u32[]{:S(2)}) collective-permute-start(s16[1552,128]{1,0:T(8,128)(2,1)S(1)} %encode_parts.4), channel_id=1, source_target_pairs={{0,1},{1,0},{2,3},{3,2},{4,5},{5,4},{6,7},{7,6},{8,9},{9,8},{10,11... | collective-permute-start | bytes 1191944 | tf_op jit(solution)/shard_map/ppermute | solution.py:488
  14.1 1.8 %fusion.2.both_ref = f32[256,1536]{1,0:T(8,128)S(1)} fusion(bf16[256,2048]{1,0:T(8,128)(2,1)S(1)} %get-tuple-element.33, bf16[2048,1536]{1,0:T(8,128)(2,1)S(1)} %get-tuple-element.29), kind=kOutput, calls=%fused_computation.5 | convolution fusion | flops 1610612736 | bytes 8912896 | tf_op jit(solution)/shard_map/dot_general | solution.py:170
  15.9 0.7 %encode_parts.5 = s16[1552,128]{1,0:T(8,128)(2,1)S(1)} custom-call(f32[256,1536]{1,0:T(8,128)S(1)} %fusion.2.both_ref, f32[128,128]{1,0:T(8,128)S(1)} %get-tuple-element.34.refs_0_), custom_call_target="tpu_custom_call" | custom-call | flops 3932160 | bytes 1966080 | tf_op jit(solution)/shard_map/encode_parts/pallas_call | solution.py:158
  17.5 3.4 %side_parts.1 = (bf16[144,1536]{1,0:T(8,128)(2,1)S(1)}, bf16[144,1536]{1,0:T(8,128)(2,1)S(1)}, bf16[144,1536]{1,0:T(8,128)(2,1)S(1)}, bf16[256,2048]{1,0:T(8,128)(2,1)S(1)}, f32[128,128]{1,0:T(8,128)S(1)}) custom-call(s32[11]{0:T(128)S(1)} %concatenate.6.meta_ref, s32[4]{0:T(128)S(1)} %pad_add_fusion.quarter_ref, s32[1,128]{1,0:T(1,128)S(1)} %bitcast.18, ...), custom_call_target="tpu_custom_call" | custom-call | flops 1 | bytes 1 | tf_op jit(solution)/shard_map/side_parts/pallas_call | solution.py:222
  20.9 0.7 %collective-permute-start.4 = (bf16[144,1536]{1,0:T(8,128)(2,1)S(1)}, bf16[144,1536]{1,0:T(8,128)(2,1)S(1)}, u32[]{:S(2)}, u32[]{:S(2)}) collective-permute-start(bf16[144,1536]{1,0:T(8,128)(2,1)S(1)} %get-tuple-element.41), channel_id=1, source_target_pairs={{2,4},{4,2},{6,8},{8,6},{10,12},{12,10},{3,5},{5,3},{7,9},{9,7},{1... | collective-permute-start | bytes 1327112 | tf_op jit(solution)/shard_map/ppermute | solution.py:496
  21.6 4.6 %fusion.3.own_ref = f32[256,1536]{1,0:T(8,128)S(1)} fusion(bf16[256,2048]{1,0:T(8,128)(2,1)S(1)} %get-tuple-element.36, bf16[2048,1536]{1,0:T(8,128)(2,1)} %copy-done.2), kind=kOutput, calls=%fused_computation.6 | convolution fusion | flops 1610612736 | bytes 8912896 | tf_op jit(solution)/shard_map/dot_general | solution.py:170
  26.2 2.5 %collective-permute-done.cy_ref = s16[1552,128]{1,0:T(8,128)(2,1)S(1)} collective-permute-done((s16[1552,128]{1,0:T(8,128)(2,1)S(1)}, s16[1552,128]{1,0:T(8,128)(2,1)S(1)}, u32[]{:S(2)}, u32[]{:S(2)}) %collective-permute-start) | collective-permute-done | bytes 397344 | tf_op jit(solution)/shard_map/ppermute | solution.py:488
  29.1 1.4 %join_qwen.1 = (bf16[128,1664]{1,0:T(8,128)(2,1)S(1)}, f32[128,128]{1,0:T(8,128)S(1)}) custom-call(s32[11]{0:T(128)S(1)} %concatenate.6.meta_ref, f32[256,1536]{1,0:T(8,128)S(1)} %fusion.3.own_ref, f32[128,128]{1,0:T(8,128)S(1)} %get-tuple-element.37.squares_ref, s16[1552,128]{1,0:T(8,128)(2,1)S(1)} %collective-permute-done.cy_ref, ...), custom_call_target="tpu_custom_call" | custom-call | flops 20000000000 | bytes 8388608 | tf_op jit(solution)/shard_map/join_qwen/pallas_call | solution.py:307
  30.4 0.7 %collective-permute-start.10 = (bf16[128,1664]{1,0:T(8,128)(2,1)S(1)}, bf16[128,1664]{1,0:T(8,128)(2,1)S(1)}, u32[]{:S(2)}, u32[]{:S(2)}) collective-permute-start(bf16[128,1664]{1,0:T(8,128)(2,1)S(1)} %get-tuple-element.45.u_ref), channel_id=1, source_target_pairs={{2,4},{4,2},{6,8},{8,6},{10,12},{12,10},{3,5},{5,3},{7,9},{9,7},{1... | collective-permute-start | bytes 1277960 | tf_op jit(solution)/shard_map/ppermute | solution.py:502
  31.2 1.7 %join_llama.1 = (f32[128,1536]{1,0:T(8,128)S(1)}, f32[8,128]{1,0:T(8,128)S(1)}) custom-call(s32[11]{0:T(128)S(1)} %concatenate.6.meta_ref, f32[256,1536]{1,0:T(8,128)S(1)} %fusion.3.own_ref, f32[128,128]{1,0:T(8,128)S(1)} %get-tuple-element.37.squares_ref, s16[1552,128]{1,0:T(8,128)(2,1)S(1)} %collective-permute-done.cy_ref, ...), custom_call_target="tpu_custom_call" | custom-call | flops 20000000000 | bytes 8388608 | tf_op jit(solution)/shard_map/join_llama/pallas_call | solution.py:352
  32.9 3.0 %collective-permute-start.5 = (f32[8,128]{1,0:T(8,128)S(1)}, f32[8,128]{1,0:T(8,128)S(1)}, u32[]{:S(2)}, u32[]{:S(2)}) collective-permute-start(f32[8,128]{1,0:T(8,128)S(1)} %get-tuple-element.43.refs_0_), channel_id=1, source_target_pairs={{0,2},{2,0},{4,6},{6,4},{8,10},{10,8},{12,14},{14,12},{1,3},{3,1},... | collective-permute-start | bytes 12296 | tf_op jit(solution)/shard_map/ppermute | solution.py:458
  35.8 0.8 %collective-permute-done.5.refs_1_ = f32[8,128]{1,0:T(8,128)S(1)} collective-permute-done((f32[8,128]{1,0:T(8,128)S(1)}, f32[8,128]{1,0:T(8,128)S(1)}, u32[]{:S(2)}, u32[]{:S(2)}) %collective-permute-start.5) | collective-permute-done | bytes 4128 | tf_op jit(solution)/shard_map/ppermute | solution.py:458
  37.0 3.0 %collective-permute-start.8 = (f32[16,128]{1,0:T(8,128)S(1)}, f32[16,128]{1,0:T(8,128)S(1)}, u32[]{:S(2)}, u32[]{:S(2)}) collective-permute-start(f32[16,128]{1,0:T(8,128)S(1)} %constant_dynamic-update-slice_fusion), channel_id=1, source_target_pairs={{0,12},{2,14},{4,8},{6,10},{8,4},{10,6},{12,0},{14,2},{1,13},{3,15... | collective-permute-start | bytes 24584 | tf_op jit(solution)/shard_map/ppermute | solution.py:458
  40.0 1.3 %collective-permute-start.6 = (f32[16,128]{1,0:T(8,128)S(1)}, f32[16,128]{1,0:T(8,128)S(1)}, u32[]{:S(2)}, u32[]{:S(2)}) collective-permute-start(f32[16,128]{1,0:T(8,128)S(1)} %constant_dynamic-update-slice_fusion), channel_id=1, source_target_pairs={{0,4},{2,6},{4,0},{6,2},{8,12},{10,14},{12,8},{14,10},{1,5},{3,7},... | collective-permute-start | bytes 24584 | tf_op jit(solution)/shard_map/ppermute | solution.py:458
  41.4 1.4 %map_parts.1 = (f32[128,1536]{1,0:T(8,128)S(1)}, f32[128,128]{1,0:T(8,128)S(1)}) custom-call(s32[11]{0:T(128)S(1)} %concatenate.6.meta_ref, bf16[128,1664]{1,0:T(8,128)(2,1)S(1)} %get-tuple-element.45.u_ref, bf16[128,1664]{1,0:T(8,128)(2,1)S(1)} %collective-permute-done.9.near_ref, bf16[128,1664]{1,0:T(8,128)(2,1)S(1)} %collective-permute-done.10.far_ref, ...), custom_call_target="tpu_custom_call" | custom-call | flops 268435456 | bytes 2097152 | tf_op jit(solution)/shard_map/map_parts/pallas_call | solution.py:400
  42.8 0.5 collective-permute-done.8.refs_4_
  43.2 1.3 %collective-permute-done.7.refs_3_ = f32[16,128]{1,0:T(8,128)S(1)} collective-permute-done((f32[16,128]{1,0:T(8,128)S(1)}, f32[16,128]{1,0:T(8,128)S(1)}, u32[]{:S(2)}, u32[]{:S(2)}) %collective-permute-start.7) | collective-permute-done | bytes 8224 | tf_op jit(solution)/shard_map/ppermute | solution.py:458
  44.6 1.3 %finish.1 = (f32[128,1536]{1,0:T(8,128)}, f32[1,128]{1,0:T(1,128)}) custom-call(f32[8,128]{1,0:T(8,128)S(1)} %get-tuple-element.43.refs_0_, f32[8,128]{1,0:T(8,128)S(1)} %collective-permute-done.5.refs_1_, f32[16,128]{1,0:T(8,128)S(1)} %collective-permute-done.6.refs_2_, f32[16,128]{1,0:T(8,128)S(1)} %collective-permute-done.7.refs_3_, ...), custom_call_target="tpu_custom_call" | custom-call | flops 3932160 | bytes 2359296 | tf_op jit(solution)/shard_map/finish/pallas_call | solution.py:438
  (25 shorter events, 1.0 us)
Async XLA Ops:
  4.6 9.5 %copy-start.2 = (bf16[2048,1536]{1,0:T(8,128)(2,1)}, bf16[2048,1536]{1,0:T(8,128)(2,1)S(1)}, u32[]{:S(2)}) copy-start(bf16[2048,1536]{1,0:T(8,128)(2,1)S(1)} %get-tuple-element.29) | copy-start | bytes 18874372
  7.1 19.1 %collective-permute-start.2 = (s16[1552,128]{1,0:T(8,128)(2,1)S(1)}, s16[1552,128]{1,0:T(8,128)(2,1)S(1)}, u32[]{:S(2)}, u32[]{:S(2)}) collective-permute-start(s16[1552,128]{1,0:T(8,128)(2,1)S(1)} %encode_parts.3), channel_id=1, source_target_pairs={{0,17},{1,16},{16,1},{17,0},{2,19},{3,18},{18,3},{19,2},{4,21},{5,... | collective-permute-start | bytes 1191944 | tf_op jit(solution)/shard_map/ppermute | solution.py:485
  13.5 15.2 %collective-permute-start = (s16[1552,128]{1,0:T(8,128)(2,1)S(1)}, s16[1552,128]{1,0:T(8,128)(2,1)S(1)}, u32[]{:S(2)}, u32[]{:S(2)}) collective-permute-start(s16[1552,128]{1,0:T(8,128)(2,1)S(1)} %encode_parts.4), channel_id=1, source_target_pairs={{0,1},{1,0},{2,3},{3,2},{4,5},{5,4},{6,7},{7,6},{8,9},{9,8},{10,11... | collective-permute-start | bytes 1191944 | tf_op jit(solution)/shard_map/ppermute | solution.py:488
  14.1 3.3 %copy-start.3 = (s32[4]{0:T(128)S(1)}, s32[4]{0:T(128)}, u32[]{:S(2)}) copy-start(s32[4]{0:T(128)} %param.11) | copy-start | bytes 52
  14.1 3.3 %copy-start.4 = (s32[4]{0:T(128)S(1)}, s32[4]{0:T(128)}, u32[]{:S(2)}) copy-start(s32[4]{0:T(128)} %param.12) | copy-start | bytes 52
  14.1 3.4 %copy-start.1 = (s32[128]{0:T(128)S(1)}, s32[128]{0:T(128)}, u32[]{:S(2)}) copy-start(s32[128]{0:T(128)} %param.15) | copy-start | bytes 1540
  16.6 12.5 %collective-permute-start.1 = (s16[1552,128]{1,0:T(8,128)(2,1)S(1)}, s16[1552,128]{1,0:T(8,128)(2,1)S(1)}, u32[]{:S(2)}, u32[]{:S(2)}) collective-permute-start(s16[1552,128]{1,0:T(8,128)(2,1)S(1)} %encode_parts.5), channel_id=1, source_target_pairs={{0,16},{16,0},{1,17},{17,1},{2,18},{18,2},{3,19},{19,3},{4,20},{20... | collective-permute-start | bytes 1191944 | tf_op jit(solution)/shard_map/ppermute | solution.py:491
  20.9 10.3 %collective-permute-start.3 = (bf16[144,1536]{1,0:T(8,128)(2,1)S(1)}, bf16[144,1536]{1,0:T(8,128)(2,1)S(1)}, u32[]{:S(2)}, u32[]{:S(2)}) collective-permute-start(bf16[144,1536]{1,0:T(8,128)(2,1)S(1)} %get-tuple-element.39), channel_id=1, source_target_pairs={{0,2},{2,0},{4,6},{6,4},{8,10},{10,8},{12,14},{14,12},{1,3},{3,1},... | collective-permute-start | bytes 1327112 | tf_op jit(solution)/shard_map/ppermute | solution.py:497
  20.9 10.2 %collective-permute-start.4 = (bf16[144,1536]{1,0:T(8,128)(2,1)S(1)}, bf16[144,1536]{1,0:T(8,128)(2,1)S(1)}, u32[]{:S(2)}, u32[]{:S(2)}) collective-permute-start(bf16[144,1536]{1,0:T(8,128)(2,1)S(1)} %get-tuple-element.41), channel_id=1, source_target_pairs={{2,4},{4,2},{6,8},{8,6},{10,12},{12,10},{3,5},{5,3},{7,9},{9,7},{1... | collective-permute-start | bytes 1327112 | tf_op jit(solution)/shard_map/ppermute | solution.py:496
  30.4 11.0 %collective-permute-start.10 = (bf16[128,1664]{1,0:T(8,128)(2,1)S(1)}, bf16[128,1664]{1,0:T(8,128)(2,1)S(1)}, u32[]{:S(2)}, u32[]{:S(2)}) collective-permute-start(bf16[128,1664]{1,0:T(8,128)(2,1)S(1)} %get-tuple-element.45.u_ref), channel_id=1, source_target_pairs={{2,4},{4,2},{6,8},{8,6},{10,12},{12,10},{3,5},{5,3},{7,9},{9,7},{1... | collective-permute-start | bytes 1277960 | tf_op jit(solution)/shard_map/ppermute | solution.py:502
  31.2 10.2 %copy-start = (bf16[4,512,512]{2,1,0:T(8,128)(2,1)S(1)}, bf16[4,512,512]{2,1,0:T(8,128)(2,1)}, u32[]{:S(2)}) copy-start(bf16[4,512,512]{2,1,0:T(8,128)(2,1)} %w_ref.3) | copy-start | bytes 6291460
  32.9 3.8 %collective-permute-start.5 = (f32[8,128]{1,0:T(8,128)S(1)}, f32[8,128]{1,0:T(8,128)S(1)}, u32[]{:S(2)}, u32[]{:S(2)}) collective-permute-start(f32[8,128]{1,0:T(8,128)S(1)} %get-tuple-element.43.refs_0_), channel_id=1, source_target_pairs={{0,2},{2,0},{4,6},{6,4},{8,10},{10,8},{12,14},{14,12},{1,3},{3,1},... | collective-permute-start | bytes 12296 | tf_op jit(solution)/shard_map/ppermute | solution.py:458
  36.7 4.7 %collective-permute-start.9 = (bf16[128,1664]{1,0:T(8,128)(2,1)S(1)}, bf16[128,1664]{1,0:T(8,128)(2,1)S(1)}, u32[]{:S(2)}, u32[]{:S(2)}) collective-permute-start(bf16[128,1664]{1,0:T(8,128)(2,1)S(1)} %get-tuple-element.45.u_ref), channel_id=1, source_target_pairs={{0,2},{2,0},{4,6},{6,4},{8,10},{10,8},{12,14},{14,12},{1,3},{3,1},... | collective-permute-start | bytes 1277960 | tf_op jit(solution)/shard_map/ppermute | solution.py:508
  37.0 6.2 %collective-permute-start.8 = (f32[16,128]{1,0:T(8,128)S(1)}, f32[16,128]{1,0:T(8,128)S(1)}, u32[]{:S(2)}, u32[]{:S(2)}) collective-permute-start(f32[16,128]{1,0:T(8,128)S(1)} %constant_dynamic-update-slice_fusion), channel_id=1, source_target_pairs={{0,12},{2,14},{4,8},{6,10},{8,4},{10,6},{12,0},{14,2},{1,13},{3,15... | collective-permute-start | bytes 24584 | tf_op jit(solution)/shard_map/ppermute | solution.py:458
  40.0 4.5 %collective-permute-start.7 = (f32[16,128]{1,0:T(8,128)S(1)}, f32[16,128]{1,0:T(8,128)S(1)}, u32[]{:S(2)}, u32[]{:S(2)}) collective-permute-start(f32[16,128]{1,0:T(8,128)S(1)} %constant_dynamic-update-slice_fusion), channel_id=1, source_target_pairs={{0,8},{2,10},{4,12},{6,14},{8,0},{10,2},{12,4},{14,6},{1,9},{3,11}... | collective-permute-start | bytes 24584 | tf_op jit(solution)/shard_map/ppermute | solution.py:458
  40.0 4.5 %collective-permute-start.6 = (f32[16,128]{1,0:T(8,128)S(1)}, f32[16,128]{1,0:T(8,128)S(1)}, u32[]{:S(2)}, u32[]{:S(2)}) collective-permute-start(f32[16,128]{1,0:T(8,128)S(1)} %constant_dynamic-update-slice_fusion), channel_id=1, source_target_pairs={{0,4},{2,6},{4,0},{6,2},{8,12},{10,14},{12,8},{14,10},{1,5},{3,7},... | collective-permute-start | bytes 24584 | tf_op jit(solution)/shard_map/ppermute | solution.py:458

commit v3 on v2

--- a/solution.py
+++ b/solution.py
@@ -170,7 +170,7 @@
     return jnp.dot(left, head, preferred_element_type=f32)
 
 
-def side_kernel(width, blocks, own_which, meta_ref, quarter_ref, token_ref, hidden_ref, gain_ref, w_ref, near_ref, own_ref, far_ref, left_ref, squares_ref, held, gain_held, w_held, sum_ref, sem, gain_sem, w_sems):
+def side_kernel(width, blocks, own_which, meta_ref, quarter_ref, token_ref, hidden_ref, gain_ref, w_ref, head_ref, near_ref, own_ref, far_ref, left_ref, squares_ref, head_out, held, gain_held, w_held, sum_ref, sem, gain_sem, w_sems, head_sem):
     rows = token_ref.shape[1]
     slots = w_ref.shape[0]
     at = pl.ds(pl.multiple_of(quarter_ref[own_which] * rows, rows), rows)
@@ -181,6 +181,8 @@
     hidden_copy.start()
     for copy in w_copies:
         copy.start()
+    head_copy = pltpu.make_async_copy(head_ref, head_out, head_sem)
+    head_copy.start()
     shard = meta_ref[1]
     near_at = jnp.where(shard % 2 == 0, 2, 0)
     token = jnp.transpose(jnp.broadcast_to(token_ref[...].astype(f32), (8, rows)))[:, :1].astype(i32)
@@ -213,17 +215,20 @@
         third = sums - first - second
         parts = jnp.where(order == 0, first, jnp.where(order == 1, second, jnp.where(order == 2, third, 0.0)))
         out_ref[pl.ds(rows, EXTRA), :] = parts.astype(bf16)
-
-
-def side_parts(meta, quarters, token, hidden, gain, weights, width, cols):
-    rows, feats = token.shape[1], hidden.shape[1]
+    near_ref[pl.ds(rows + EXTRA, EXTRA), :] = jnp.zeros((EXTRA, near_ref.shape[1]), bf16)
+    head_copy.wait()
+
+
+def side_parts(meta, quarters, token, hidden, gain, weights, head, width):
+    rows, feats, cols = token.shape[1], hidden.shape[1], head.shape[1]
     smem = pl.BlockSpec(memory_space=pltpu.SMEM)
     hbm = pl.BlockSpec(memory_space=pltpu.HBM)
     outs = pl.pallas_call(
         functools.partial(side_kernel, width, cols // width, 0),
-        in_specs=[smem, smem, pl.BlockSpec(memory_space=pltpu.VMEM), hbm, hbm, hbm],
-        out_shape=[jax.ShapeDtypeStruct((rows + EXTRA, cols), bf16)] * 3
-        + [jax.ShapeDtypeStruct((2 * rows, feats), bf16), jax.ShapeDtypeStruct((rows, LANES), f32)],
+        in_specs=[smem, smem, pl.BlockSpec(memory_space=pltpu.VMEM), hbm, hbm, hbm, hbm],
+        out_shape=[jax.ShapeDtypeStruct((rows + many * EXTRA, cols), bf16) for many in (2, 1, 1)]
+        + [jax.ShapeDtypeStruct((2 * rows, feats), bf16), jax.ShapeDtypeStruct((rows, LANES), f32)]
+        + [jax.ShapeDtypeStruct(head.shape, head.dtype)],
         scratch_shapes=[
             pltpu.VMEM((rows, feats), bf16),
             pltpu.VMEM(gain.shape, bf16),
@@ -232,12 +237,13 @@
             pltpu.SemaphoreType.DMA,
             pltpu.SemaphoreType.DMA,
             pltpu.SemaphoreType.DMA((weights.shape[0],)),
+            pltpu.SemaphoreType.DMA,
         ],
         compiler_params=params(),
         cost_estimate=pl.CostEstimate(flops=1, bytes_accessed=1, transcendentals=0),
         name="side_parts",
-    )(meta, quarters, token, hidden, gain, weights)
-    return outs[:3], outs[3], outs[4]
+    )(meta, quarters, token, hidden, gain, weights, head)
+    return outs[:3], outs[3], outs[4], outs[5]
 
 
 def extras(ref, rows):
@@ -470,7 +476,7 @@
     held_hidden = pltpu.with_memory_space_constraint(hidden, pltpu.HBM)
     held_weight = pltpu.with_memory_space_constraint(pair_weight, pltpu.HBM)
     held_gain = pltpu.with_memory_space_constraint(norm_gain, pltpu.HBM)
-    head = pltpu.with_memory_space_constraint(head, pltpu.HBM)
+    held_head = pltpu.with_memory_space_constraint(head, pltpu.HBM)
     width = pair_weight.shape[1]
     features = hidden.shape[1] * row_groups
     model, shard, side = (lax.axis_index(name).astype(i32) for name in ("mp", "vocab", "rows"))
@@ -480,7 +486,7 @@
 
     inside = [(i, i ^ 1) for i in range(shards)]
     across = [(i, i + 1 if i % 2 else i - 1) for i in range(1, shards - 1)]
-    lefts, squares, head = first_prep(quarters, held_hidden, held_gain, head, (3, 1, 2))
+    lefts, squares, head = first_prep(quarters, held_hidden, held_gain, held_head, (3, 1, 2))
     (to_d,) = encode_parts(product(lefts[0], head), squares[:1])
     from_d = lax.ppermute(to_d, ("mp", "rows"), [(0, 3), (1, 2), (2, 1), (3, 0)])
     left_y, _ = lax.optimization_barrier((lefts[1], to_d))
@@ -490,12 +496,13 @@
     (to_x,) = encode_parts(product(left_x, head), squares[2:])
     from_x = lax.ppermute(to_x, "mp", [(0, 1), (1, 0)])
     early, _ = lax.optimization_barrier((meta, to_x))
-    (to_near, columns, to_far), left_own, squares_own = side_parts(
-        early, quarters, token, held_hidden, held_gain, held_weight, width, head.shape[1]
+    (to_near, columns, to_far), left_own, squares_own, head = side_parts(
+        early, quarters, token, held_hidden, held_gain, held_weight, held_head, width
     )
+    own = product(left_own, head)
+    to_near, _ = lax.optimization_barrier((to_near, own))
+    near_columns = lax.ppermute(to_near, "vocab", inside)
     far_columns = lax.ppermute(to_far, "vocab", across)
-    near_columns = lax.ppermute(to_near, "vocab", inside)
-    own = product(left_own, head)
 
     codes = (from_y, from_x, from_d)
     u, stats = join_qwen(meta, own, squares_own, codes, width, features)

time: 46.3 us -> 45.3 us (0.978)
  starting transfers between devices: 13.7 us -> 17.1 us
  waiting for transfers between devices: 5.45 us -> 2.7 us
  matrix products: 9.9 us -> 7.21 us
  Pallas kernels: 15.2 us -> 16.5 us
    ppermute x1, starting transfers between devices: 0.07 us -> 3.44 us  [on_device(): near_columns = lax.ppermute(to_near, 'vocab', inside)]
    dot_general x4, matrix products: 9.9 us -> 7.21 us  [product(): return jnp.dot(left, head, preferred_element_type=f32)]
    ppermute x1, waiting for transfers between devices: 2.54 us -> 0.01 us  [on_device(): from_y = lax.ppermute(to_y, 'rows', [(0, 1), (1, 0)])]
    ppermute x4, waiting for transfers between devices: 2.6 us -> 1.31 us  [gather_pieces(): lax.ppermute(sent, 'vocab', [(i, i ^ turn * step) for i in range(shards)])]
    ppermute x1, waiting for transfers between devices: 0.29 us -> 1.37 us  [on_device(): from_x = lax.ppermute(to_x, 'mp', [(0, 1), (1, 0)])]
    pallas_call x1, Pallas kernels: 3.39 us -> 4.23 us  [side_parts(): pl.pallas_call(functools.partial(side_kernel, width, cols // width, 0), i...]
  transfers between devices with their start and end apart: 11 -> 11, of which waited for: 5 -> 4; matrix products, arithmetic and copies ran while one was open for 18% -> 12% of each run, Pallas kernels for 20% -> 23%
where the time goes in v3:
time: 45.3 us; the launch traced here: 45.1 us
  starting transfers between devices  17.1 us (38%)
  Pallas kernels  16.5 us (36%)
  matrix products  7.21 us (16%)
  waiting for transfers between devices  2.7 us (6%)
  between operations  1.43 us (3%)
    ppermute x4, starting transfers between devices, gather_pieces(): lax.ppermute(sent, 'vocab', [(i, i ^ turn * step) for i in range(shards)])  7.34 us
    dot_general x4, matrix products, product(): return jnp.dot(left, head, preferred_element_type=f32)  7.21 us
    pallas_call x1, Pallas kernels, side_parts(): pl.pallas_call(functools.partial(side_kernel, width, cols // width, 0), i...  4.23 us
    ppermute x1, starting transfers between devices, on_device(): lax.ppermute(to_d, ('mp', 'rows'), [(0, 3), (1, 2), (2, 1), (3, 0)])  3.93 us
    pallas_call x1, Pallas kernels, first_prep(): pl.pallas_call(functools.partial(first_kernel, kinds, rows), in_specs=[pl...  3.89 us
    ppermute x1, starting transfers between devices, on_device(): near_columns = lax.ppermute(to_near, 'vocab', inside)  3.44 us
    pallas_call x3, Pallas kernels, encode_parts(): pl.pallas_call(functools.partial(encode_kernel, count), out_shape=[jax.Sh...  2.14 us
    pallas_call x1, Pallas kernels, map_parts(): pl.pallas_call(functools.partial(map_kernel, width, blocks, shards), in_s...  1.83 us
  transfers between devices with their start and end apart: 11, of which 4 were waited for; matrix products, arithmetic and copies ran while one was open for 12% of the time, Pallas kernels for 23%

profile of v3, /device:TPU:0, one launch (start us, length us, event | category | flops | bytes accessed | tf_op | source)
XLA Modules:
  0.0 45.1 jit_solution(8447647682180779690)
XLA Ops:
  0.7 3.9 %first_prep.1 = (bf16[256,2048]{1,0:T(8,128)(2,1)S(1)}, bf16[256,2048]{1,0:T(8,128)(2,1)S(1)}, bf16[256,2048]{1,0:T(8,128)(2,1)S(1)}, f32[128,128]{1,0:T(8,128)S...) custom-call(s32[4]{0:T(128)S(1)} %pad_add_fusion.quarter_ref, ...), custom_call_target="tpu_custom_call" | custom-call | flops 6291456 | bytes 6291456 | tf_op jit(solution)/shard_map/first_prep/pallas_call | solution.py:122
  4.6 1.8 %fusion.both_ref = f32[256,1536]{1,0:T(8,128)S(1)} fusion(bf16[256,2048]{1,0:T(8,128)(2,1)S(1)} %get-tuple-element.30, bf16[2048,1536]{1,0:T(8,128)(2,1)S(1)} %get-tuple-element.31), kind=kOutput, calls=%fused_computation.3 | convolution fusion | flops 1610612736 | bytes 8912896 | tf_op jit(solution)/shard_map/dot_general | solution.py:170
  6.4 0.7 %encode_parts.3 = s16[1552,128]{1,0:T(8,128)(2,1)S(1)} custom-call(f32[256,1536]{1,0:T(8,128)S(1)} %fusion.both_ref, f32[128,128]{1,0:T(8,128)S(1)} %get-tuple-element.32.refs_0_), custom_call_target="tpu_custom_call" | custom-call | flops 3932160 | bytes 1966080 | tf_op jit(solution)/shard_map/encode_parts/pallas_call | solution.py:158
  7.1 3.9 %collective-permute-start.2 = (s16[1552,128]{1,0:T(8,128)(2,1)S(1)}, s16[1552,128]{1,0:T(8,128)(2,1)S(1)}, u32[]{:S(2)}, u32[]{:S(2)}) collective-permute-start(s16[1552,128]{1,0:T(8,128)(2,1)S(1)} %encode_parts.3), channel_id=1, source_target_pairs={{0,17},{1,16},{16,1},{17,0},{2,19},{3,18},{18,3},{19,2},{4,21},{5,... | collective-permute-start | bytes 1191944 | tf_op jit(solution)/shard_map/ppermute | solution.py:491
  11.1 1.8 %fusion.1.both_ref = f32[256,1536]{1,0:T(8,128)S(1)} fusion(bf16[256,2048]{1,0:T(8,128)(2,1)S(1)} %get-tuple-element.33, bf16[2048,1536]{1,0:T(8,128)(2,1)S(1)} %get-tuple-element.31), kind=kOutput, calls=%fused_computation.4 | convolution fusion | flops 1610612736 | bytes 8912896 | tf_op jit(solution)/shard_map/dot_general | solution.py:170
  12.9 0.7 %encode_parts.4 = s16[1552,128]{1,0:T(8,128)(2,1)S(1)} custom-call(f32[256,1536]{1,0:T(8,128)S(1)} %fusion.1.both_ref, f32[128,128]{1,0:T(8,128)S(1)} %get-tuple-element.34.refs_0_), custom_call_target="tpu_custom_call" | custom-call | flops 3932160 | bytes 1966080 | tf_op jit(solution)/shard_map/encode_parts/pallas_call | solution.py:158
  13.6 0.5 %collective-permute-start = (s16[1552,128]{1,0:T(8,128)(2,1)S(1)}, s16[1552,128]{1,0:T(8,128)(2,1)S(1)}, u32[]{:S(2)}, u32[]{:S(2)}) collective-permute-start(s16[1552,128]{1,0:T(8,128)(2,1)S(1)} %encode_parts.4), channel_id=1, source_target_pairs={{0,1},{1,0},{2,3},{3,2},{4,5},{5,4},{6,7},{7,6},{8,9},{9,8},{10,11... | collective-permute-start | bytes 1191944 | tf_op jit(solution)/shard_map/ppermute | solution.py:494
  14.2 1.8 %fusion.2.both_ref = f32[256,1536]{1,0:T(8,128)S(1)} fusion(bf16[256,2048]{1,0:T(8,128)(2,1)S(1)} %get-tuple-element.35, bf16[2048,1536]{1,0:T(8,128)(2,1)S(1)} %get-tuple-element.31), kind=kOutput, calls=%fused_computation.5 | convolution fusion | flops 1610612736 | bytes 8912896 | tf_op jit(solution)/shard_map/dot_general | solution.py:170
  16.0 0.7 %encode_parts.5 = s16[1552,128]{1,0:T(8,128)(2,1)S(1)} custom-call(f32[256,1536]{1,0:T(8,128)S(1)} %fusion.2.both_ref, f32[128,128]{1,0:T(8,128)S(1)} %get-tuple-element.36.refs_0_), custom_call_target="tpu_custom_call" | custom-call | flops 3932160 | bytes 1966080 | tf_op jit(solution)/shard_map/encode_parts/pallas_call | solution.py:158
  17.5 4.2 %side_parts.1 = (bf16[160,1536]{1,0:T(8,128)(2,1)S(1)}, bf16[144,1536]{1,0:T(8,128)(2,1)S(1)}, bf16[144,1536]{1,0:T(8,128)(2,1)S(1)}, bf16[256,2048]{1,0:T(8,128...) custom-call(s32[11]{0:T(128)S(1)} %concatenate.6.meta_ref, s32[4]{0:T(128)S(1)} %pad_add_fusion.quarter_ref, ...), custom_call_target="tpu_custom_call" | custom-call | flops 1 | bytes 1 | tf_op jit(solution)/shard_map/side_parts/pallas_call | solution.py:226
  21.8 0.7 %collective-permute-start.4 = (bf16[144,1536]{1,0:T(8,128)(2,1)S(1)}, bf16[144,1536]{1,0:T(8,128)(2,1)S(1)}, u32[]{:S(2)}, u32[]{:S(2)}) collective-permute-start(bf16[144,1536]{1,0:T(8,128)(2,1)S(1)} %get-tuple-element.45), channel_id=1, source_target_pairs={{2,4},{4,2},{6,8},{8,6},{10,12},{12,10},{3,5},{5,3},{7,9},{9,7},{1... | collective-permute-start | bytes 1327112 | tf_op jit(solution)/shard_map/ppermute | solution.py:505
  22.5 1.8 %fusion.3.own_ref = f32[256,1536]{1,0:T(8,128)S(1)} fusion(bf16[256,2048]{1,0:T(8,128)(2,1)S(1)} %get-tuple-element.38, bf16[2048,1536]{1,0:T(8,128)(2,1)S(1)} %get-tuple-element.39), kind=kOutput, calls=%fused_computation.6 | convolution fusion | flops 1610612736 | bytes 8912896 | tf_op jit(solution)/shard_map/dot_general | solution.py:170
  24.3 3.4 %collective-permute-start.3 = (bf16[160,1536]{1,0:T(8,128)(2,1)S(1)}, bf16[160,1536]{1,0:T(8,128)(2,1)S(1)}, u32[]{:S(2)}, u32[]{:S(2)}) collective-permute-start(bf16[160,1536]{1,0:T(8,128)(2,1)S(1)} %get-tuple-element.43), channel_id=1, source_target_pairs={{0,2},{2,0},{4,6},{6,4},{8,10},{10,8},{12,14},{14,12},{1,3},{3,1},... | collective-permute-start | bytes 1474568 | tf_op jit(solution)/shard_map/ppermute | solution.py:504
  27.7 1.4 %collective-permute-done.1.cx_ref = s16[1552,128]{1,0:T(8,128)(2,1)S(1)} collective-permute-done((s16[1552,128]{1,0:T(8,128)(2,1)S(1)}, s16[1552,128]{1,0:T(8,128)(2,1)S(1)}, u32[]{:S(2)}, u32[]{:S(2)}) %collective-permute-start.1) | collective-permute-done | bytes 397344 | tf_op jit(solution)/shard_map/ppermute | solution.py:497
  29.1 1.4 %join_qwen.1 = (bf16[128,1664]{1,0:T(8,128)(2,1)S(1)}, f32[128,128]{1,0:T(8,128)S(1)}) custom-call(s32[11]{0:T(128)S(1)} %concatenate.6.meta_ref, f32[256,1536]{1,0:T(8,128)S(1)} %fusion.3.own_ref, f32[128,128]{1,0:T(8,128)S(1)} %get-tuple-element.40.squares_ref, s16[1552,128]{1,0:T(8,128)(2,1)S(1)} %collective-permute-done.cy_ref, ...), custom_call_target="tpu_custom_call" | custom-call | flops 20000000000 | bytes 8388608 | tf_op jit(solution)/shard_map/join_qwen/pallas_call | solution.py:313
  30.5 0.7 %collective-permute-start.10 = (bf16[128,1664]{1,0:T(8,128)(2,1)S(1)}, bf16[128,1664]{1,0:T(8,128)(2,1)S(1)}, u32[]{:S(2)}, u32[]{:S(2)}) collective-permute-start(bf16[128,1664]{1,0:T(8,128)(2,1)S(1)} %get-tuple-element.49.u_ref), channel_id=1, source_target_pairs={{2,4},{4,2},{6,8},{8,6},{10,12},{12,10},{3,5},{5,3},{7,9},{9,7},{1... | collective-permute-start | bytes 1277960 | tf_op jit(solution)/shard_map/ppermute | solution.py:509
  31.2 1.7 %join_llama.1 = (f32[128,1536]{1,0:T(8,128)S(1)}, f32[8,128]{1,0:T(8,128)S(1)}) custom-call(s32[11]{0:T(128)S(1)} %concatenate.6.meta_ref, f32[256,1536]{1,0:T(8,128)S(1)} %fusion.3.own_ref, f32[128,128]{1,0:T(8,128)S(1)} %get-tuple-element.40.squares_ref, s16[1552,128]{1,0:T(8,128)(2,1)S(1)} %collective-permute-done.cy_ref, ...), custom_call_target="tpu_custom_call" | custom-call | flops 20000000000 | bytes 8388608 | tf_op jit(solution)/shard_map/join_llama/pallas_call | solution.py:358
  32.9 3.0 %collective-permute-start.5 = (f32[8,128]{1,0:T(8,128)S(1)}, f32[8,128]{1,0:T(8,128)S(1)}, u32[]{:S(2)}, u32[]{:S(2)}) collective-permute-start(f32[8,128]{1,0:T(8,128)S(1)} %get-tuple-element.47.refs_0_), channel_id=1, source_target_pairs={{0,2},{2,0},{4,6},{6,4},{8,10},{10,8},{12,14},{14,12},{1,3},{3,1},... | collective-permute-start | bytes 12296 | tf_op jit(solution)/shard_map/ppermute | solution.py:464
  35.9 0.8 %collective-permute-done.5.refs_1_ = f32[8,128]{1,0:T(8,128)S(1)} collective-permute-done((f32[8,128]{1,0:T(8,128)S(1)}, f32[8,128]{1,0:T(8,128)S(1)}, u32[]{:S(2)}, u32[]{:S(2)}) %collective-permute-start.5) | collective-permute-done | bytes 4128 | tf_op jit(solution)/shard_map/ppermute | solution.py:464
  37.0 2.1 %collective-permute-start.8 = (f32[16,128]{1,0:T(8,128)S(1)}, f32[16,128]{1,0:T(8,128)S(1)}, u32[]{:S(2)}, u32[]{:S(2)}) collective-permute-start(f32[16,128]{1,0:T(8,128)S(1)} %constant_dynamic-update-slice_fusion), channel_id=1, source_target_pairs={{0,12},{2,14},{4,8},{6,10},{8,4},{10,6},{12,0},{14,2},{1,13},{3,15... | collective-permute-start | bytes 24584 | tf_op jit(solution)/shard_map/ppermute | solution.py:464
  39.1 0.9 %collective-permute-start.7 = (f32[16,128]{1,0:T(8,128)S(1)}, f32[16,128]{1,0:T(8,128)S(1)}, u32[]{:S(2)}, u32[]{:S(2)}) collective-permute-start(f32[16,128]{1,0:T(8,128)S(1)} %constant_dynamic-update-slice_fusion), channel_id=1, source_target_pairs={{0,8},{2,10},{4,12},{6,14},{8,0},{10,2},{12,4},{14,6},{1,9},{3,11}... | collective-permute-start | bytes 24584 | tf_op jit(solution)/shard_map/ppermute | solution.py:464
  40.1 1.3 %collective-permute-start.6 = (f32[16,128]{1,0:T(8,128)S(1)}, f32[16,128]{1,0:T(8,128)S(1)}, u32[]{:S(2)}, u32[]{:S(2)}) collective-permute-start(f32[16,128]{1,0:T(8,128)S(1)} %constant_dynamic-update-slice_fusion), channel_id=1, source_target_pairs={{0,4},{2,6},{4,0},{6,2},{8,12},{10,14},{12,8},{14,10},{1,5},{3,7},... | collective-permute-start | bytes 24584 | tf_op jit(solution)/shard_map/ppermute | solution.py:464
  41.4 1.8 %map_parts.1 = (f32[128,1536]{1,0:T(8,128)S(1)}, f32[128,128]{1,0:T(8,128)S(1)}) custom-call(s32[11]{0:T(128)S(1)} %concatenate.6.meta_ref, bf16[128,1664]{1,0:T(8,128)(2,1)S(1)} %get-tuple-element.49.u_ref, bf16[128,1664]{1,0:T(8,128)(2,1)S(1)} %collective-permute-done.9.near_ref, bf16[128,1664]{1,0:T(8,128)(2,1)S(1)} %collective-permute-done.10.far_ref, ...), custom_call_target="tpu_custom_call" | custom-call | flops 268435456 | bytes 2097152 | tf_op jit(solution)/shard_map/map_parts/pallas_call | solution.py:406
  43.8 1.3 %finish.1 = (f32[128,1536]{1,0:T(8,128)}, f32[1,128]{1,0:T(1,128)}) custom-call(f32[8,128]{1,0:T(8,128)S(1)} %get-tuple-element.47.refs_0_, f32[8,128]{1,0:T(8,128)S(1)} %collective-permute-done.5.refs_1_, f32[16,128]{1,0:T(8,128)S(1)} %collective-permute-done.6.refs_2_, f32[16,128]{1,0:T(8,128)S(1)} %collective-permute-done.7.refs_3_, ...), custom_call_target="tpu_custom_call" | custom-call | flops 3932160 | bytes 2359296 | tf_op jit(solution)/shard_map/finish/pallas_call | solution.py:444
  (23 shorter events, 1.1 us)
Async XLA Ops:
  7.1 20.6 %collective-permute-start.2 = (s16[1552,128]{1,0:T(8,128)(2,1)S(1)}, s16[1552,128]{1,0:T(8,128)(2,1)S(1)}, u32[]{:S(2)}, u32[]{:S(2)}) collective-permute-start(s16[1552,128]{1,0:T(8,128)(2,1)S(1)} %encode_parts.3), channel_id=1, source_target_pairs={{0,17},{1,16},{16,1},{17,0},{2,19},{3,18},{18,3},{19,2},{4,21},{5,... | collective-permute-start | bytes 1191944 | tf_op jit(solution)/shard_map/ppermute | solution.py:491
  13.6 15.5 %collective-permute-start = (s16[1552,128]{1,0:T(8,128)(2,1)S(1)}, s16[1552,128]{1,0:T(8,128)(2,1)S(1)}, u32[]{:S(2)}, u32[]{:S(2)}) collective-permute-start(s16[1552,128]{1,0:T(8,128)(2,1)S(1)} %encode_parts.4), channel_id=1, source_target_pairs={{0,1},{1,0},{2,3},{3,2},{4,5},{5,4},{6,7},{7,6},{8,9},{9,8},{10,11... | collective-permute-start | bytes 1191944 | tf_op jit(solution)/shard_map/ppermute | solution.py:494
  14.1 3.3 %copy-start.2 = (s32[4]{0:T(128)S(1)}, s32[4]{0:T(128)}, u32[]{:S(2)}) copy-start(s32[4]{0:T(128)} %param.11) | copy-start | bytes 52
  14.1 3.3 %copy-start.3 = (s32[4]{0:T(128)S(1)}, s32[4]{0:T(128)}, u32[]{:S(2)}) copy-start(s32[4]{0:T(128)} %param.12) | copy-start | bytes 52
  14.1 3.4 %copy-start.1 = (s32[128]{0:T(128)S(1)}, s32[128]{0:T(128)}, u32[]{:S(2)}) copy-start(s32[128]{0:T(128)} %param.15) | copy-start | bytes 1540
  16.7 12.4 %collective-permute-start.1 = (s16[1552,128]{1,0:T(8,128)(2,1)S(1)}, s16[1552,128]{1,0:T(8,128)(2,1)S(1)}, u32[]{:S(2)}, u32[]{:S(2)}) collective-permute-start(s16[1552,128]{1,0:T(8,128)(2,1)S(1)} %encode_parts.5), channel_id=1, source_target_pairs={{0,16},{16,0},{1,17},{17,1},{2,18},{18,2},{3,19},{19,3},{4,20},{20... | collective-permute-start | bytes 1191944 | tf_op jit(solution)/shard_map/ppermute | solution.py:497
  21.8 9.4 %collective-permute-start.4 = (bf16[144,1536]{1,0:T(8,128)(2,1)S(1)}, bf16[144,1536]{1,0:T(8,128)(2,1)S(1)}, u32[]{:S(2)}, u32[]{:S(2)}) collective-permute-start(bf16[144,1536]{1,0:T(8,128)(2,1)S(1)} %get-tuple-element.45), channel_id=1, source_target_pairs={{2,4},{4,2},{6,8},{8,6},{10,12},{12,10},{3,5},{5,3},{7,9},{9,7},{1... | collective-permute-start | bytes 1327112 | tf_op jit(solution)/shard_map/ppermute | solution.py:505
  24.3 6.9 %collective-permute-start.3 = (bf16[160,1536]{1,0:T(8,128)(2,1)S(1)}, bf16[160,1536]{1,0:T(8,128)(2,1)S(1)}, u32[]{:S(2)}, u32[]{:S(2)}) collective-permute-start(bf16[160,1536]{1,0:T(8,128)(2,1)S(1)} %get-tuple-element.43), channel_id=1, source_target_pairs={{0,2},{2,0},{4,6},{6,4},{8,10},{10,8},{12,14},{14,12},{1,3},{3,1},... | collective-permute-start | bytes 1474568 | tf_op jit(solution)/shard_map/ppermute | solution.py:504
  30.5 10.9 %collective-permute-start.10 = (bf16[128,1664]{1,0:T(8,128)(2,1)S(1)}, bf16[128,1664]{1,0:T(8,128)(2,1)S(1)}, u32[]{:S(2)}, u32[]{:S(2)}) collective-permute-start(bf16[128,1664]{1,0:T(8,128)(2,1)S(1)} %get-tuple-element.49.u_ref), channel_id=1, source_target_pairs={{2,4},{4,2},{6,8},{8,6},{10,12},{12,10},{3,5},{5,3},{7,9},{9,7},{1... | collective-permute-start | bytes 1277960 | tf_op jit(solution)/shard_map/ppermute | solution.py:509
  31.2 10.2 %copy-start = (bf16[4,512,512]{2,1,0:T(8,128)(2,1)S(1)}, bf16[4,512,512]{2,1,0:T(8,128)(2,1)}, u32[]{:S(2)}) copy-start(bf16[4,512,512]{2,1,0:T(8,128)(2,1)} %w_ref.3) | copy-start | bytes 6291460
  32.9 3.8 %collective-permute-start.5 = (f32[8,128]{1,0:T(8,128)S(1)}, f32[8,128]{1,0:T(8,128)S(1)}, u32[]{:S(2)}, u32[]{:S(2)}) collective-permute-start(f32[8,128]{1,0:T(8,128)S(1)} %get-tuple-element.47.refs_0_), channel_id=1, source_target_pairs={{0,2},{2,0},{4,6},{6,4},{8,10},{10,8},{12,14},{14,12},{1,3},{3,1},... | collective-permute-start | bytes 12296 | tf_op jit(solution)/shard_map/ppermute | solution.py:464
  36.7 4.7 %collective-permute-start.9 = (bf16[128,1664]{1,0:T(8,128)(2,1)S(1)}, bf16[128,1664]{1,0:T(8,128)(2,1)S(1)}, u32[]{:S(2)}, u32[]{:S(2)}) collective-permute-start(bf16[128,1664]{1,0:T(8,128)(2,1)S(1)} %get-tuple-element.49.u_ref), channel_id=1, source_target_pairs={{0,2},{2,0},{4,6},{6,4},{8,10},{10,8},{12,14},{14,12},{1,3},{3,1},... | collective-permute-start | bytes 1277960 | tf_op jit(solution)/shard_map/ppermute | solution.py:515
  37.0 6.2 %collective-permute-start.8 = (f32[16,128]{1,0:T(8,128)S(1)}, f32[16,128]{1,0:T(8,128)S(1)}, u32[]{:S(2)}, u32[]{:S(2)}) collective-permute-start(f32[16,128]{1,0:T(8,128)S(1)} %constant_dynamic-update-slice_fusion), channel_id=1, source_target_pairs={{0,12},{2,14},{4,8},{6,10},{8,4},{10,6},{12,0},{14,2},{1,13},{3,15... | collective-permute-start | bytes 24584 | tf_op jit(solution)/shard_map/ppermute | solution.py:464
  39.1 4.5 %collective-permute-start.7 = (f32[16,128]{1,0:T(8,128)S(1)}, f32[16,128]{1,0:T(8,128)S(1)}, u32[]{:S(2)}, u32[]{:S(2)}) collective-permute-start(f32[16,128]{1,0:T(8,128)S(1)} %constant_dynamic-update-slice_fusion), channel_id=1, source_target_pairs={{0,8},{2,10},{4,12},{6,14},{8,0},{10,2},{12,4},{14,6},{1,9},{3,11}... | collective-permute-start | bytes 24584 | tf_op jit(solution)/shard_map/ppermute | solution.py:464
  40.1 3.7 %collective-permute-start.6 = (f32[16,128]{1,0:T(8,128)S(1)}, f32[16,128]{1,0:T(8,128)S(1)}, u32[]{:S(2)}, u32[]{:S(2)}) collective-permute-start(f32[16,128]{1,0:T(8,128)S(1)} %constant_dynamic-update-slice_fusion), channel_id=1, source_target_pairs={{0,4},{2,6},{4,0},{6,2},{8,12},{10,14},{12,8},{14,10},{1,5},{3,7},... | collective-permute-start | bytes 24584 | tf_op jit(solution)/shard_map/ppermute | solution.py:464

commit v4 on v3

--- a/solution.py
+++ b/solution.py
@@ -11,7 +11,8 @@
 EXTRA = 16
 CODE = 512
 HEAD_COPIES = 1
-TOP = 32767.0
+TOP = 32700.0
+ROUNDER = 12582912.0
 LEAST = 1e-30
 FLOOR = 1.9287498479639178e-22
 VMEM = 16 * 1024 * 1024
@@ -41,9 +42,9 @@
 
 
 def encode(values, power):
-    size = jnp.sqrt(jnp.abs(values) * jnp.exp2(-power)) * TOP
-    code = jnp.minimum(size + 0.5, TOP).astype(i32)
-    return jnp.where(values < 0, -code, code).astype(i16)
+    wide = values * (jnp.exp2(-power) * (TOP * TOP))
+    root = wide * lax.rsqrt(jnp.maximum(jnp.abs(wide), LEAST))
+    return ((root + ROUNDER) - ROUNDER).astype(i32).astype(i16)
 
 
 def decode(codes, power):

time: 45.3 us -> 45.1 us (level)
  Pallas kernels: 16.5 us -> 15.8 us
  waiting for transfers between devices: 2.7 us -> 3.17 us
    pallas_call x3, Pallas kernels: 2.14 us -> 1.43 us  [encode_parts(): pl.pallas_call(functools.partial(encode_kernel, count), out_shape=[jax.Sh...]
    ppermute x1, waiting for transfers between devices: 1.37 us -> 1.84 us  [on_device(): from_x = lax.ppermute(to_x, 'mp', [(0, 1), (1, 0)])]
  transfers between devices with their start and end apart: 11 -> 11, of which waited for: 4 -> 4; matrix products, arithmetic and copies ran while one was open for 12% -> 12% of each run, Pallas kernels for 23% -> 22%
where the time goes in v4:
time: 45.1 us; the launch traced here: 44.9 us
  starting transfers between devices  17.1 us (38%)
  Pallas kernels  15.8 us (35%)
  matrix products  7.21 us (16%)
  waiting for transfers between devices  3.17 us (7%)
  between operations  1.43 us (3%)
    ppermute x4, starting transfers between devices, gather_pieces(): lax.ppermute(sent, 'vocab', [(i, i ^ turn * step) for i in range(shards)])  7.34 us
    dot_general x4, matrix products, product(): return jnp.dot(left, head, preferred_element_type=f32)  7.21 us
    pallas_call x1, Pallas kernels, side_parts(): pl.pallas_call(functools.partial(side_kernel, width, cols // width, 0), i...  4.23 us
    ppermute x1, starting transfers between devices, on_device(): lax.ppermute(to_d, ('mp', 'rows'), [(0, 3), (1, 2), (2, 1), (3, 0)])  3.93 us
    pallas_call x1, Pallas kernels, first_prep(): pl.pallas_call(functools.partial(first_kernel, kinds, rows), in_specs=[pl...  3.89 us
    ppermute x1, starting transfers between devices, on_device(): near_columns = lax.ppermute(to_near, 'vocab', inside)  3.43 us
    ppermute x1, waiting for transfers between devices, on_device(): from_x = lax.ppermute(to_x, 'mp', [(0, 1), (1, 0)])  1.84 us
    pallas_call x1, Pallas kernels, map_parts(): pl.pallas_call(functools.partial(map_kernel, width, blocks, shards), in_s...  1.83 us
  transfers between devices with their start and end apart: 11, of which 4 were waited for; matrix products, arithmetic and copies ran while one was open for 12% of the time, Pallas kernels for 22%

profile of v4, /device:TPU:0, one launch (start us, length us, event | category | flops | bytes accessed | tf_op | source)
XLA Modules:
  0.0 44.9 jit_solution(17992351568136638619)
XLA Ops:
  0.7 3.9 %first_prep.1 = (bf16[256,2048]{1,0:T(8,128)(2,1)S(1)}, bf16[256,2048]{1,0:T(8,128)(2,1)S(1)}, bf16[256,2048]{1,0:T(8,128)(2,1)S(1)}, f32[128,128]{1,0:T(8,128)S...) custom-call(s32[4]{0:T(128)S(1)} %pad_add_fusion.quarter_ref, ...), custom_call_target="tpu_custom_call" | custom-call | flops 6291456 | bytes 6291456 | tf_op jit(solution)/shard_map/first_prep/pallas_call | solution.py:123
  4.6 1.8 %fusion.both_ref = f32[256,1536]{1,0:T(8,128)S(1)} fusion(bf16[256,2048]{1,0:T(8,128)(2,1)S(1)} %get-tuple-element.30, bf16[2048,1536]{1,0:T(8,128)(2,1)S(1)} %get-tuple-element.31), kind=kOutput, calls=%fused_computation.3 | convolution fusion | flops 1610612736 | bytes 8912896 | tf_op jit(solution)/shard_map/dot_general | solution.py:171
  6.4 0.5 %encode_parts.3 = s16[1552,128]{1,0:T(8,128)(2,1)S(1)} custom-call(f32[256,1536]{1,0:T(8,128)S(1)} %fusion.both_ref, f32[128,128]{1,0:T(8,128)S(1)} %get-tuple-element.32.refs_0_), custom_call_target="tpu_custom_call" | custom-call | flops 3932160 | bytes 1966080 | tf_op jit(solution)/shard_map/encode_parts/pallas_call | solution.py:159
  6.9 3.9 %collective-permute-start.2 = (s16[1552,128]{1,0:T(8,128)(2,1)S(1)}, s16[1552,128]{1,0:T(8,128)(2,1)S(1)}, u32[]{:S(2)}, u32[]{:S(2)}) collective-permute-start(s16[1552,128]{1,0:T(8,128)(2,1)S(1)} %encode_parts.3), channel_id=1, source_target_pairs={{0,17},{1,16},{16,1},{17,0},{2,19},{3,18},{18,3},{19,2},{4,21},{5,... | collective-permute-start | bytes 1191944 | tf_op jit(solution)/shard_map/ppermute | solution.py:492
  10.8 1.8 %fusion.1.both_ref = f32[256,1536]{1,0:T(8,128)S(1)} fusion(bf16[256,2048]{1,0:T(8,128)(2,1)S(1)} %get-tuple-element.33, bf16[2048,1536]{1,0:T(8,128)(2,1)S(1)} %get-tuple-element.31), kind=kOutput, calls=%fused_computation.4 | convolution fusion | flops 1610612736 | bytes 8912896 | tf_op jit(solution)/shard_map/dot_general | solution.py:171
  12.7 0.5 %encode_parts.4 = s16[1552,128]{1,0:T(8,128)(2,1)S(1)} custom-call(f32[256,1536]{1,0:T(8,128)S(1)} %fusion.1.both_ref, f32[128,128]{1,0:T(8,128)S(1)} %get-tuple-element.34.refs_0_), custom_call_target="tpu_custom_call" | custom-call | flops 3932160 | bytes 1966080 | tf_op jit(solution)/shard_map/encode_parts/pallas_call | solution.py:159
  13.1 0.5 %collective-permute-start = (s16[1552,128]{1,0:T(8,128)(2,1)S(1)}, s16[1552,128]{1,0:T(8,128)(2,1)S(1)}, u32[]{:S(2)}, u32[]{:S(2)}) collective-permute-start(s16[1552,128]{1,0:T(8,128)(2,1)S(1)} %encode_parts.4), channel_id=1, source_target_pairs={{0,1},{1,0},{2,3},{3,2},{4,5},{5,4},{6,7},{7,6},{8,9},{9,8},{10,11... | collective-permute-start | bytes 1191944 | tf_op jit(solution)/shard_map/ppermute | solution.py:495
  13.7 1.8 %fusion.2.both_ref = f32[256,1536]{1,0:T(8,128)S(1)} fusion(bf16[256,2048]{1,0:T(8,128)(2,1)S(1)} %get-tuple-element.35, bf16[2048,1536]{1,0:T(8,128)(2,1)S(1)} %get-tuple-element.31), kind=kOutput, calls=%fused_computation.5 | convolution fusion | flops 1610612736 | bytes 8912896 | tf_op jit(solution)/shard_map/dot_general | solution.py:171
  15.5 0.5 %encode_parts.5 = s16[1552,128]{1,0:T(8,128)(2,1)S(1)} custom-call(f32[256,1536]{1,0:T(8,128)S(1)} %fusion.2.both_ref, f32[128,128]{1,0:T(8,128)S(1)} %get-tuple-element.36.refs_0_), custom_call_target="tpu_custom_call" | custom-call | flops 3932160 | bytes 1966080 | tf_op jit(solution)/shard_map/encode_parts/pallas_call | solution.py:159
  16.8 4.2 %side_parts.1 = (bf16[160,1536]{1,0:T(8,128)(2,1)S(1)}, bf16[144,1536]{1,0:T(8,128)(2,1)S(1)}, bf16[144,1536]{1,0:T(8,128)(2,1)S(1)}, bf16[256,2048]{1,0:T(8,128...) custom-call(s32[11]{0:T(128)S(1)} %concatenate.6.meta_ref, s32[4]{0:T(128)S(1)} %pad_add_fusion.quarter_ref, ...), custom_call_target="tpu_custom_call" | custom-call | flops 1 | bytes 1 | tf_op jit(solution)/shard_map/side_parts/pallas_call | solution.py:227
  21.1 0.7 %collective-permute-start.4 = (bf16[144,1536]{1,0:T(8,128)(2,1)S(1)}, bf16[144,1536]{1,0:T(8,128)(2,1)S(1)}, u32[]{:S(2)}, u32[]{:S(2)}) collective-permute-start(bf16[144,1536]{1,0:T(8,128)(2,1)S(1)} %get-tuple-element.45), channel_id=1, source_target_pairs={{2,4},{4,2},{6,8},{8,6},{10,12},{12,10},{3,5},{5,3},{7,9},{9,7},{1... | collective-permute-start | bytes 1327112 | tf_op jit(solution)/shard_map/ppermute | solution.py:506
  21.8 1.8 %fusion.3.own_ref = f32[256,1536]{1,0:T(8,128)S(1)} fusion(bf16[256,2048]{1,0:T(8,128)(2,1)S(1)} %get-tuple-element.38, bf16[2048,1536]{1,0:T(8,128)(2,1)S(1)} %get-tuple-element.39), kind=kOutput, calls=%fused_computation.6 | convolution fusion | flops 1610612736 | bytes 8912896 | tf_op jit(solution)/shard_map/dot_general | solution.py:171
  23.6 3.4 %collective-permute-start.3 = (bf16[160,1536]{1,0:T(8,128)(2,1)S(1)}, bf16[160,1536]{1,0:T(8,128)(2,1)S(1)}, u32[]{:S(2)}, u32[]{:S(2)}) collective-permute-start(bf16[160,1536]{1,0:T(8,128)(2,1)S(1)} %get-tuple-element.43), channel_id=1, source_target_pairs={{0,2},{2,0},{4,6},{6,4},{8,10},{10,8},{12,14},{14,12},{1,3},{3,1},... | collective-permute-start | bytes 1474568 | tf_op jit(solution)/shard_map/ppermute | solution.py:505
  27.0 1.8 %collective-permute-done.1.cx_ref = s16[1552,128]{1,0:T(8,128)(2,1)S(1)} collective-permute-done((s16[1552,128]{1,0:T(8,128)(2,1)S(1)}, s16[1552,128]{1,0:T(8,128)(2,1)S(1)}, u32[]{:S(2)}, u32[]{:S(2)}) %collective-permute-start.1) | collective-permute-done | bytes 397344 | tf_op jit(solution)/shard_map/ppermute | solution.py:498
  28.8 1.4 %join_qwen.1 = (bf16[128,1664]{1,0:T(8,128)(2,1)S(1)}, f32[128,128]{1,0:T(8,128)S(1)}) custom-call(s32[11]{0:T(128)S(1)} %concatenate.6.meta_ref, f32[256,1536]{1,0:T(8,128)S(1)} %fusion.3.own_ref, f32[128,128]{1,0:T(8,128)S(1)} %get-tuple-element.40.squares_ref, s16[1552,128]{1,0:T(8,128)(2,1)S(1)} %collective-permute-done.cy_ref, ...), custom_call_target="tpu_custom_call" | custom-call | flops 20000000000 | bytes 8388608 | tf_op jit(solution)/shard_map/join_qwen/pallas_call | solution.py:314
  30.2 0.7 %collective-permute-start.10 = (bf16[128,1664]{1,0:T(8,128)(2,1)S(1)}, bf16[128,1664]{1,0:T(8,128)(2,1)S(1)}, u32[]{:S(2)}, u32[]{:S(2)}) collective-permute-start(bf16[128,1664]{1,0:T(8,128)(2,1)S(1)} %get-tuple-element.49.u_ref), channel_id=1, source_target_pairs={{2,4},{4,2},{6,8},{8,6},{10,12},{12,10},{3,5},{5,3},{7,9},{9,7},{1... | collective-permute-start | bytes 1277960 | tf_op jit(solution)/shard_map/ppermute | solution.py:510
  31.0 1.7 %join_llama.1 = (f32[128,1536]{1,0:T(8,128)S(1)}, f32[8,128]{1,0:T(8,128)S(1)}) custom-call(s32[11]{0:T(128)S(1)} %concatenate.6.meta_ref, f32[256,1536]{1,0:T(8,128)S(1)} %fusion.3.own_ref, f32[128,128]{1,0:T(8,128)S(1)} %get-tuple-element.40.squares_ref, s16[1552,128]{1,0:T(8,128)(2,1)S(1)} %collective-permute-done.cy_ref, ...), custom_call_target="tpu_custom_call" | custom-call | flops 20000000000 | bytes 8388608 | tf_op jit(solution)/shard_map/join_llama/pallas_call | solution.py:359
  32.7 3.0 %collective-permute-start.5 = (f32[8,128]{1,0:T(8,128)S(1)}, f32[8,128]{1,0:T(8,128)S(1)}, u32[]{:S(2)}, u32[]{:S(2)}) collective-permute-start(f32[8,128]{1,0:T(8,128)S(1)} %get-tuple-element.47.refs_0_), channel_id=1, source_target_pairs={{0,2},{2,0},{4,6},{6,4},{8,10},{10,8},{12,14},{14,12},{1,3},{3,1},... | collective-permute-start | bytes 12296 | tf_op jit(solution)/shard_map/ppermute | solution.py:465
  35.6 0.8 %collective-permute-done.5.refs_1_ = f32[8,128]{1,0:T(8,128)S(1)} collective-permute-done((f32[8,128]{1,0:T(8,128)S(1)}, f32[8,128]{1,0:T(8,128)S(1)}, u32[]{:S(2)}, u32[]{:S(2)}) %collective-permute-start.5) | collective-permute-done | bytes 4128 | tf_op jit(solution)/shard_map/ppermute | solution.py:465
  36.8 2.1 %collective-permute-start.8 = (f32[16,128]{1,0:T(8,128)S(1)}, f32[16,128]{1,0:T(8,128)S(1)}, u32[]{:S(2)}, u32[]{:S(2)}) collective-permute-start(f32[16,128]{1,0:T(8,128)S(1)} %constant_dynamic-update-slice_fusion), channel_id=1, source_target_pairs={{0,12},{2,14},{4,8},{6,10},{8,4},{10,6},{12,0},{14,2},{1,13},{3,15... | collective-permute-start | bytes 24584 | tf_op jit(solution)/shard_map/ppermute | solution.py:465
  38.9 0.9 %collective-permute-start.7 = (f32[16,128]{1,0:T(8,128)S(1)}, f32[16,128]{1,0:T(8,128)S(1)}, u32[]{:S(2)}, u32[]{:S(2)}) collective-permute-start(f32[16,128]{1,0:T(8,128)S(1)} %constant_dynamic-update-slice_fusion), channel_id=1, source_target_pairs={{0,8},{2,10},{4,12},{6,14},{8,0},{10,2},{12,4},{14,6},{1,9},{3,11}... | collective-permute-start | bytes 24584 | tf_op jit(solution)/shard_map/ppermute | solution.py:465
  39.8 1.3 %collective-permute-start.6 = (f32[16,128]{1,0:T(8,128)S(1)}, f32[16,128]{1,0:T(8,128)S(1)}, u32[]{:S(2)}, u32[]{:S(2)}) collective-permute-start(f32[16,128]{1,0:T(8,128)S(1)} %constant_dynamic-update-slice_fusion), channel_id=1, source_target_pairs={{0,4},{2,6},{4,0},{6,2},{8,12},{10,14},{12,8},{14,10},{1,5},{3,7},... | collective-permute-start | bytes 24584 | tf_op jit(solution)/shard_map/ppermute | solution.py:465
  41.2 1.8 %map_parts.1 = (f32[128,1536]{1,0:T(8,128)S(1)}, f32[128,128]{1,0:T(8,128)S(1)}) custom-call(s32[11]{0:T(128)S(1)} %concatenate.6.meta_ref, bf16[128,1664]{1,0:T(8,128)(2,1)S(1)} %get-tuple-element.49.u_ref, bf16[128,1664]{1,0:T(8,128)(2,1)S(1)} %collective-permute-done.9.near_ref, bf16[128,1664]{1,0:T(8,128)(2,1)S(1)} %collective-permute-done.10.far_ref, ...), custom_call_target="tpu_custom_call" | custom-call | flops 268435456 | bytes 2097152 | tf_op jit(solution)/shard_map/map_parts/pallas_call | solution.py:407
  43.5 1.3 %finish.1 = (f32[128,1536]{1,0:T(8,128)}, f32[1,128]{1,0:T(1,128)}) custom-call(f32[8,128]{1,0:T(8,128)S(1)} %get-tuple-element.47.refs_0_, f32[8,128]{1,0:T(8,128)S(1)} %collective-permute-done.5.refs_1_, f32[16,128]{1,0:T(8,128)S(1)} %collective-permute-done.6.refs_2_, f32[16,128]{1,0:T(8,128)S(1)} %collective-permute-done.7.refs_3_, ...), custom_call_target="tpu_custom_call" | custom-call | flops 3932160 | bytes 2359296 | tf_op jit(solution)/shard_map/finish/pallas_call | solution.py:445
  (23 shorter events, 1.1 us)
Async XLA Ops:
  6.9 20.1 %collective-permute-start.2 = (s16[1552,128]{1,0:T(8,128)(2,1)S(1)}, s16[1552,128]{1,0:T(8,128)(2,1)S(1)}, u32[]{:S(2)}, u32[]{:S(2)}) collective-permute-start(s16[1552,128]{1,0:T(8,128)(2,1)S(1)} %encode_parts.3), channel_id=1, source_target_pairs={{0,17},{1,16},{16,1},{17,0},{2,19},{3,18},{18,3},{19,2},{4,21},{5,... | collective-permute-start | bytes 1191944 | tf_op jit(solution)/shard_map/ppermute | solution.py:492
  13.1 15.7 %collective-permute-start = (s16[1552,128]{1,0:T(8,128)(2,1)S(1)}, s16[1552,128]{1,0:T(8,128)(2,1)S(1)}, u32[]{:S(2)}, u32[]{:S(2)}) collective-permute-start(s16[1552,128]{1,0:T(8,128)(2,1)S(1)} %encode_parts.4), channel_id=1, source_target_pairs={{0,1},{1,0},{2,3},{3,2},{4,5},{5,4},{6,7},{7,6},{8,9},{9,8},{10,11... | collective-permute-start | bytes 1191944 | tf_op jit(solution)/shard_map/ppermute | solution.py:495
  13.7 3.1 %copy-start.2 = (s32[4]{0:T(128)S(1)}, s32[4]{0:T(128)}, u32[]{:S(2)}) copy-start(s32[4]{0:T(128)} %param.11) | copy-start | bytes 52
  13.7 3.1 %copy-start.3 = (s32[4]{0:T(128)S(1)}, s32[4]{0:T(128)}, u32[]{:S(2)}) copy-start(s32[4]{0:T(128)} %param.12) | copy-start | bytes 52
  13.7 3.2 %copy-start.1 = (s32[128]{0:T(128)S(1)}, s32[128]{0:T(128)}, u32[]{:S(2)}) copy-start(s32[128]{0:T(128)} %param.15) | copy-start | bytes 1540
  16.0 12.9 %collective-permute-start.1 = (s16[1552,128]{1,0:T(8,128)(2,1)S(1)}, s16[1552,128]{1,0:T(8,128)(2,1)S(1)}, u32[]{:S(2)}, u32[]{:S(2)}) collective-permute-start(s16[1552,128]{1,0:T(8,128)(2,1)S(1)} %encode_parts.5), channel_id=1, source_target_pairs={{0,16},{16,0},{1,17},{17,1},{2,18},{18,2},{3,19},{19,3},{4,20},{20... | collective-permute-start | bytes 1191944 | tf_op jit(solution)/shard_map/ppermute | solution.py:498
  21.1 9.9 %collective-permute-start.4 = (bf16[144,1536]{1,0:T(8,128)(2,1)S(1)}, bf16[144,1536]{1,0:T(8,128)(2,1)S(1)}, u32[]{:S(2)}, u32[]{:S(2)}) collective-permute-start(bf16[144,1536]{1,0:T(8,128)(2,1)S(1)} %get-tuple-element.45), channel_id=1, source_target_pairs={{2,4},{4,2},{6,8},{8,6},{10,12},{12,10},{3,5},{5,3},{7,9},{9,7},{1... | collective-permute-start | bytes 1327112 | tf_op jit(solution)/shard_map/ppermute | solution.py:506
  23.6 7.4 %collective-permute-start.3 = (bf16[160,1536]{1,0:T(8,128)(2,1)S(1)}, bf16[160,1536]{1,0:T(8,128)(2,1)S(1)}, u32[]{:S(2)}, u32[]{:S(2)}) collective-permute-start(bf16[160,1536]{1,0:T(8,128)(2,1)S(1)} %get-tuple-element.43), channel_id=1, source_target_pairs={{0,2},{2,0},{4,6},{6,4},{8,10},{10,8},{12,14},{14,12},{1,3},{3,1},... | collective-permute-start | bytes 1474568 | tf_op jit(solution)/shard_map/ppermute | solution.py:505
  30.2 10.9 %collective-permute-start.10 = (bf16[128,1664]{1,0:T(8,128)(2,1)S(1)}, bf16[128,1664]{1,0:T(8,128)(2,1)S(1)}, u32[]{:S(2)}, u32[]{:S(2)}) collective-permute-start(bf16[128,1664]{1,0:T(8,128)(2,1)S(1)} %get-tuple-element.49.u_ref), channel_id=1, source_target_pairs={{2,4},{4,2},{6,8},{8,6},{10,12},{12,10},{3,5},{5,3},{7,9},{9,7},{1... | collective-permute-start | bytes 1277960 | tf_op jit(solution)/shard_map/ppermute | solution.py:510
  31.0 10.2 %copy-start = (bf16[4,512,512]{2,1,0:T(8,128)(2,1)S(1)}, bf16[4,512,512]{2,1,0:T(8,128)(2,1)}, u32[]{:S(2)}) copy-start(bf16[4,512,512]{2,1,0:T(8,128)(2,1)} %w_ref.3) | copy-start | bytes 6291460
  32.7 3.8 %collective-permute-start.5 = (f32[8,128]{1,0:T(8,128)S(1)}, f32[8,128]{1,0:T(8,128)S(1)}, u32[]{:S(2)}, u32[]{:S(2)}) collective-permute-start(f32[8,128]{1,0:T(8,128)S(1)} %get-tuple-element.47.refs_0_), channel_id=1, source_target_pairs={{0,2},{2,0},{4,6},{6,4},{8,10},{10,8},{12,14},{14,12},{1,3},{3,1},... | collective-permute-start | bytes 12296 | tf_op jit(solution)/shard_map/ppermute | solution.py:465
  36.4 4.7 %collective-permute-start.9 = (bf16[128,1664]{1,0:T(8,128)(2,1)S(1)}, bf16[128,1664]{1,0:T(8,128)(2,1)S(1)}, u32[]{:S(2)}, u32[]{:S(2)}) collective-permute-start(bf16[128,1664]{1,0:T(8,128)(2,1)S(1)} %get-tuple-element.49.u_ref), channel_id=1, source_target_pairs={{0,2},{2,0},{4,6},{6,4},{8,10},{10,8},{12,14},{14,12},{1,3},{3,1},... | collective-permute-start | bytes 1277960 | tf_op jit(solution)/shard_map/ppermute | solution.py:516
  36.8 6.2 %collective-permute-start.8 = (f32[16,128]{1,0:T(8,128)S(1)}, f32[16,128]{1,0:T(8,128)S(1)}, u32[]{:S(2)}, u32[]{:S(2)}) collective-permute-start(f32[16,128]{1,0:T(8,128)S(1)} %constant_dynamic-update-slice_fusion), channel_id=1, source_target_pairs={{0,12},{2,14},{4,8},{6,10},{8,4},{10,6},{12,0},{14,2},{1,13},{3,15... | collective-permute-start | bytes 24584 | tf_op jit(solution)/shard_map/ppermute | solution.py:465
  38.9 4.5 %collective-permute-start.7 = (f32[16,128]{1,0:T(8,128)S(1)}, f32[16,128]{1,0:T(8,128)S(1)}, u32[]{:S(2)}, u32[]{:S(2)}) collective-permute-start(f32[16,128]{1,0:T(8,128)S(1)} %constant_dynamic-update-slice_fusion), channel_id=1, source_target_pairs={{0,8},{2,10},{4,12},{6,14},{8,0},{10,2},{12,4},{14,6},{1,9},{3,11}... | collective-permute-start | bytes 24584 | tf_op jit(solution)/shard_map/ppermute | solution.py:465
  39.8 3.7 %collective-permute-start.6 = (f32[16,128]{1,0:T(8,128)S(1)}, f32[16,128]{1,0:T(8,128)S(1)}, u32[]{:S(2)}, u32[]{:S(2)}) collective-permute-start(f32[16,128]{1,0:T(8,128)S(1)} %constant_dynamic-update-slice_fusion), channel_id=1, source_target_pairs={{0,4},{2,6},{4,0},{6,2},{8,12},{10,14},{12,8},{14,10},{1,5},{3,7},... | collective-permute-start | bytes 24584 | tf_op jit(solution)/shard_map/ppermute | solution.py:465

commit v5 on v4

--- a/solution.py
+++ b/solution.py
@@ -89,13 +89,14 @@
     out_ref[pl.ds(body, EXTRA), :] = jnp.transpose(extra)[:EXTRA].astype(i32).astype(i16)
 
 
-def first_kernel(kinds, rows, quarter_ref, hidden_ref, gain_ref, head_ref, *refs):
+def first_kernel(kinds, rows, hidden_ref, gain_ref, head_ref, *refs):
     count = len(kinds)
     left_refs, square_refs, head_out = refs[:count], refs[count : 2 * count], refs[2 * count]
     held, gain_held, sems, gain_sem, head_sems = refs[2 * count + 1 :]
     copies = []
     for place, which in enumerate(kinds):
-        at = pl.ds(pl.multiple_of(quarter_ref[which] * rows, rows), rows)
+        quarter = jnp.bitwise_xor(2 * lax.axis_index("mp") + lax.axis_index("rows"), which)
+        at = pl.ds(pl.multiple_of(quarter * rows, rows), rows)
         copies.append(pltpu.make_async_copy(hidden_ref.at[at, :], held.at[place], sems.at[place]))
     gain_copy = pltpu.make_async_copy(gain_ref, gain_held, gain_sem)
     deep = head_ref.shape[0] // HEAD_COPIES
@@ -117,12 +118,12 @@
         copy.wait()
 
 
-def first_prep(quarters, hidden, gain, head, kinds):
+def first_prep(hidden, gain, head, kinds):
     rows, feats, count = hidden.shape[0] // 4, hidden.shape[1], len(kinds)
     hbm = pl.BlockSpec(memory_space=pltpu.HBM)
     outs = pl.pallas_call(
         functools.partial(first_kernel, kinds, rows),
-        in_specs=[pl.BlockSpec(memory_space=pltpu.SMEM), hbm, hbm, hbm],
+        in_specs=[hbm, hbm, hbm],
         out_shape=[jax.ShapeDtypeStruct((2 * rows, feats), bf16)] * count
         + [jax.ShapeDtypeStruct((rows, LANES), f32)] * count
         + [jax.ShapeDtypeStruct(head.shape, head.dtype)],
@@ -138,7 +139,7 @@
             flops=8 * count * rows * feats, bytes_accessed=2 * head.size, transcendentals=0
         ),
         name="first_prep",
-    )(quarters, hidden, gain, head)
+    )(hidden, gain, head)
     return outs[:count], outs[count : 2 * count], outs[2 * count]
 
 
@@ -291,10 +292,10 @@
     return jnp.max(peak, axis=1, keepdims=True)
 
 
-def qwen_kernel(width, blocks, features, meta_ref, own_ref, squares_ref, cy_ref, cx_ref, cd_ref, u_ref, stats_ref, q_ref):
+def qwen_kernel(width, blocks, features, own_ref, squares_ref, cy_ref, cx_ref, cd_ref, u_ref, stats_ref, q_ref):
     rows = squares_ref.shape[0]
     body = blocks * width
-    peak = model_logits(meta_ref[0] == 1, features, own_ref, squares_ref, cy_ref, cx_ref, cd_ref, q_ref)
+    peak = model_logits(lax.axis_index("mp") == 1, features, own_ref, squares_ref, cy_ref, cx_ref, cd_ref, q_ref)
     total = jnp.zeros((rows, 1), f32)
     for j in range(blocks):
         at = pl.ds(j * width, width)
@@ -308,12 +309,12 @@
     stats_ref[...] = columns_to_lanes([peak, total], rows)
 
 
-def join_qwen(meta, own, squares, codes, width, features):
+def join_qwen(own, squares, codes, width, features):
     rows, cols = own.shape[0] // 2, own.shape[1]
     whole = pl.BlockSpec(memory_space=pltpu.VMEM)
     return pl.pallas_call(
         functools.partial(qwen_kernel, width, cols // width, features),
-        in_specs=[pl.BlockSpec(memory_space=pltpu.SMEM)] + [whole] * 5,
+        in_specs=[whole] * 5,
         out_shape=[
             jax.ShapeDtypeStruct((rows, cols + LANES), bf16),
             jax.ShapeDtypeStruct((rows, LANES), f32),
@@ -322,20 +323,20 @@
         compiler_params=params(),
         cost_estimate=pl.CostEstimate(flops=20000000000, bytes_accessed=8 * 1024 * 1024, transcendentals=0),
         name="join_qwen",
-    )(meta, own, squares, *codes)
-
-
-def llama_kernel(width, blocks, features, meta_ref, own_ref, squares_ref, cy_ref, cx_ref, cd_ref, token_ref, u_ref, near_ref, mine_ref, far_ref, before_ref, e_ref, stats_ref):
+    )(own, squares, *codes)
+
+
+def llama_kernel(width, blocks, features, own_ref, squares_ref, cy_ref, cx_ref, cd_ref, token_ref, u_ref, near_ref, mine_ref, far_ref, before_ref, e_ref, stats_ref):
     rows = squares_ref.shape[0]
     body = blocks * width
     columns_refs = (near_ref, mine_ref, far_ref)
-    peak = model_logits(meta_ref[0] == 0, features, own_ref, squares_ref, cy_ref, cx_ref, cd_ref, e_ref)
+    peak = model_logits(lax.axis_index("mp") == 0, features, own_ref, squares_ref, cy_ref, cx_ref, cd_ref, e_ref)
     total = jnp.zeros((rows, 1), f32)
     mass = jnp.zeros((rows, 1), f32)
     pick_e = jnp.zeros((rows, 1), f32)
     pick_m = jnp.zeros((rows, 1), f32)
     token = jnp.transpose(jnp.broadcast_to(token_ref[...].astype(f32), (8, rows)))
-    token = token[:, :1].astype(i32) - meta_ref[1] * body
+    token = token[:, :1].astype(i32) - lax.axis_index("vocab") * body
     for j in range(blocks):
         at = pl.ds(j * width, width)
         llama = jnp.exp(e_ref[:, at] - peak)
@@ -353,17 +354,17 @@
     stats_ref[...] = jnp.transpose(stats)[:8]
 
 
-def join_llama(meta, own, squares, codes, token, u, columns, stats, width, features):
+def join_llama(own, squares, codes, token, u, columns, stats, width, features):
     rows, cols = own.shape[0] // 2, own.shape[1]
     whole = pl.BlockSpec(memory_space=pltpu.VMEM)
     return pl.pallas_call(
         functools.partial(llama_kernel, width, cols // width, features),
-        in_specs=[pl.BlockSpec(memory_space=pltpu.SMEM)] + [whole] * 11,
+        in_specs=[whole] * 11,
         out_shape=[jax.ShapeDtypeStruct((rows, cols), f32), jax.ShapeDtypeStruct((8, rows), f32)],
         compiler_params=params(),
         cost_estimate=pl.CostEstimate(flops=20000000000, bytes_accessed=8 * 1024 * 1024, transcendentals=0),
         name="join_llama",
-    )(meta, own, squares, *codes, token, u, *columns, stats)
+    )(own, squares, *codes, token, u, *columns, stats)
 
 
 def map_kernel(width, blocks, shards, meta_ref, u_ref, near_ref, far_ref, w_ref, m_ref, top_ref, all_ref, scale_ref):
@@ -487,7 +488,7 @@
 
     inside = [(i, i ^ 1) for i in range(shards)]
     across = [(i, i + 1 if i % 2 else i - 1) for i in range(1, shards - 1)]
-    lefts, squares, head = first_prep(quarters, held_hidden, held_gain, held_head, (3, 1, 2))
+    lefts, squares, head = first_prep(held_hidden, held_gain, held_head, (3, 1, 2))
     (to_d,) = encode_parts(product(lefts[0], head), squares[:1])
     from_d = lax.ppermute(to_d, ("mp", "rows"), [(0, 3), (1, 2), (2, 1), (3, 0)])
     left_y, _ = lax.optimization_barrier((lefts[1], to_d))
@@ -506,10 +507,10 @@
     far_columns = lax.ppermute(to_far, "vocab", across)
 
     codes = (from_y, from_x, from_d)
-    u, stats = join_qwen(meta, own, squares_own, codes, width, features)
+    u, stats = join_qwen(own, squares_own, codes, width, features)
     far = lax.ppermute(u, "vocab", across)
     e, stats = join_llama(
-        meta, own, squares_own, codes, token, u, (near_columns, columns, far_columns), stats, width, features
+        own, squares_own, codes, token, u, (near_columns, columns, far_columns), stats, width, features
     )
     pieces, last = gather_pieces(stats, shards)
     late_u, _ = lax.optimization_barrier((u, last))

time: 45.1 us -> 43.4 us (0.962)
  Pallas kernels: 15.8 us -> 13.7 us
    pallas_call x1, Pallas kernels: 1.38 us -> 0.84 us  [join_qwen(): pl.pallas_call(functools.partial(qwen_kernel, width, cols // width, featu...]
    pallas_call x1, Pallas kernels: 1.7 us -> 1.16 us  [join_llama(): pl.pallas_call(functools.partial(llama_kernel, width, cols // width, feat...]
    pallas_call x1, Pallas kernels: 3.89 us -> 3.35 us  [first_prep(): pl.pallas_call(functools.partial(first_kernel, kinds, rows), in_specs=[hb...]
    ppermute x4, waiting for transfers between devices: 1.31 us -> 1.78 us  [gather_pieces(): lax.ppermute(sent, 'vocab', [(i, i ^ turn * step) for i in range(shards)])]
    pallas_call x1, Pallas kernels: 1.83 us -> 1.37 us  [map_parts(): pl.pallas_call(functools.partial(map_kernel, width, blocks, shards), in_s...]
  transfers between devices with their start and end apart: 11 -> 11, of which waited for: 4 -> 5; matrix products, arithmetic and copies ran while one was open for 12% -> 13% of each run, Pallas kernels for 22% -> 20%
where the time goes in v5:
time: 43.4 us; the launch traced here: 43.1 us
  starting transfers between devices  17.1 us (39%)
  Pallas kernels  13.7 us (32%)
  matrix products  7.11 us (16%)
  waiting for transfers between devices  3.62 us (8%)
  between operations  1.41 us (3%)
    ppermute x4, starting transfers between devices, gather_pieces(): lax.ppermute(sent, 'vocab', [(i, i ^ turn * step) for i in range(shards)])  7.34 us
    dot_general x4, matrix products, product(): return jnp.dot(left, head, preferred_element_type=f32)  7.11 us
    pallas_call x1, Pallas kernels, side_parts(): pl.pallas_call(functools.partial(side_kernel, width, cols // width, 0), i...  4.23 us
    ppermute x1, starting transfers between devices, on_device(): lax.ppermute(to_d, ('mp', 'rows'), [(0, 3), (1, 2), (2, 1), (3, 0)])  3.93 us
    ppermute x1, starting transfers between devices, on_device(): near_columns = lax.ppermute(to_near, 'vocab', inside)  3.44 us
    pallas_call x1, Pallas kernels, first_prep(): pl.pallas_call(functools.partial(first_kernel, kinds, rows), in_specs=[hb...  3.35 us
    ppermute x1, waiting for transfers between devices, on_device(): from_x = lax.ppermute(to_x, 'mp', [(0, 1), (1, 0)])  1.82 us
    ppermute x4, waiting for transfers between devices, gather_pieces(): lax.ppermute(sent, 'vocab', [(i, i ^ turn * step) for i in range(shards)])  1.78 us
  transfers between devices with their start and end apart: 11, of which 5 were waited for; matrix products, arithmetic and copies ran while one was open for 13% of the time, Pallas kernels for 20%

profile of v5, /device:TPU:0, one launch (start us, length us, event | category | flops | bytes accessed | tf_op | source)
XLA Modules:
  0.0 43.1 jit_solution(9583293169184088561)
XLA Ops:
  0.6 3.4 %first_prep.1 = (bf16[256,2048]{1,0:T(8,128)(2,1)S(1)}, bf16[256,2048]{1,0:T(8,128)(2,1)S(1)}, bf16[256,2048]{1,0:T(8,128)(2,1)S(1)}, f32[128,128]{1,0:T(8,128)S...) custom-call(bf16[512,2048]{1,0:T(8,128)(2,1)} %bitcast.22, ...), custom_call_target="tpu_custom_call" | custom-call | flops 6291456 | bytes 6291456 | tf_op jit(solution)/shard_map/first_prep/pallas_call | solution.py:124
  4.0 1.8 %fusion.both_ref = f32[256,1536]{1,0:T(8,128)S(1)} fusion(bf16[256,2048]{1,0:T(8,128)(2,1)S(1)} %get-tuple-element.30, bf16[2048,1536]{1,0:T(8,128)(2,1)S(1)} %get-tuple-element.31), kind=kOutput, calls=%fused_computation.3 | convolution fusion | flops 1610612736 | bytes 8912896 | tf_op jit(solution)/shard_map/dot_general | solution.py:172
  5.8 0.5 %encode_parts.3 = s16[1552,128]{1,0:T(8,128)(2,1)S(1)} custom-call(f32[256,1536]{1,0:T(8,128)S(1)} %fusion.both_ref, f32[128,128]{1,0:T(8,128)S(1)} %get-tuple-element.32.refs_0_), custom_call_target="tpu_custom_call" | custom-call | flops 3932160 | bytes 1966080 | tf_op jit(solution)/shard_map/encode_parts/pallas_call | solution.py:160
  6.3 3.9 %collective-permute-start.2 = (s16[1552,128]{1,0:T(8,128)(2,1)S(1)}, s16[1552,128]{1,0:T(8,128)(2,1)S(1)}, u32[]{:S(2)}, u32[]{:S(2)}) collective-permute-start(s16[1552,128]{1,0:T(8,128)(2,1)S(1)} %encode_parts.3), channel_id=1, source_target_pairs={{0,17},{1,16},{16,1},{17,0},{2,19},{3,18},{18,3},{19,2},{4,21},{5,... | collective-permute-start | bytes 1191944 | tf_op jit(solution)/shard_map/ppermute | solution.py:493
  10.2 1.8 %fusion.1.both_ref = f32[256,1536]{1,0:T(8,128)S(1)} fusion(bf16[256,2048]{1,0:T(8,128)(2,1)S(1)} %get-tuple-element.33, bf16[2048,1536]{1,0:T(8,128)(2,1)S(1)} %get-tuple-element.31), kind=kOutput, calls=%fused_computation.4 | convolution fusion | flops 1610612736 | bytes 8912896 | tf_op jit(solution)/shard_map/dot_general | solution.py:172
  12.0 0.5 %encode_parts.4 = s16[1552,128]{1,0:T(8,128)(2,1)S(1)} custom-call(f32[256,1536]{1,0:T(8,128)S(1)} %fusion.1.both_ref, f32[128,128]{1,0:T(8,128)S(1)} %get-tuple-element.34.refs_0_), custom_call_target="tpu_custom_call" | custom-call | flops 3932160 | bytes 1966080 | tf_op jit(solution)/shard_map/encode_parts/pallas_call | solution.py:160
  12.4 0.5 %collective-permute-start = (s16[1552,128]{1,0:T(8,128)(2,1)S(1)}, s16[1552,128]{1,0:T(8,128)(2,1)S(1)}, u32[]{:S(2)}, u32[]{:S(2)}) collective-permute-start(s16[1552,128]{1,0:T(8,128)(2,1)S(1)} %encode_parts.4), channel_id=1, source_target_pairs={{0,1},{1,0},{2,3},{3,2},{4,5},{5,4},{6,7},{7,6},{8,9},{9,8},{10,11... | collective-permute-start | bytes 1191944 | tf_op jit(solution)/shard_map/ppermute | solution.py:496
  13.0 1.8 %fusion.2.both_ref = f32[256,1536]{1,0:T(8,128)S(1)} fusion(bf16[256,2048]{1,0:T(8,128)(2,1)S(1)} %get-tuple-element.35, bf16[2048,1536]{1,0:T(8,128)(2,1)S(1)} %get-tuple-element.31), kind=kOutput, calls=%fused_computation.5 | convolution fusion | flops 1610612736 | bytes 8912896 | tf_op jit(solution)/shard_map/dot_general | solution.py:172
  16.2 4.2 %side_parts.1 = (bf16[160,1536]{1,0:T(8,128)(2,1)S(1)}, bf16[144,1536]{1,0:T(8,128)(2,1)S(1)}, bf16[144,1536]{1,0:T(8,128)(2,1)S(1)}, bf16[256,2048]{1,0:T(8,128...) custom-call(s32[11]{0:T(128)S(1)} %concatenate.6.meta_ref, s32[4]{0:T(128)S(1)} %pad_add_fusion.quarter_ref, ...), custom_call_target="tpu_custom_call" | custom-call | flops 1 | bytes 1 | tf_op jit(solution)/shard_map/side_parts/pallas_call | solution.py:228
  20.4 0.7 %collective-permute-start.4 = (bf16[144,1536]{1,0:T(8,128)(2,1)S(1)}, bf16[144,1536]{1,0:T(8,128)(2,1)S(1)}, u32[]{:S(2)}, u32[]{:S(2)}) collective-permute-start(bf16[144,1536]{1,0:T(8,128)(2,1)S(1)} %get-tuple-element.45), channel_id=1, source_target_pairs={{2,4},{4,2},{6,8},{8,6},{10,12},{12,10},{3,5},{5,3},{7,9},{9,7},{1... | collective-permute-start | bytes 1327112 | tf_op jit(solution)/shard_map/ppermute | solution.py:507
  21.1 1.8 %fusion.3.own_ref = f32[256,1536]{1,0:T(8,128)S(1)} fusion(bf16[256,2048]{1,0:T(8,128)(2,1)S(1)} %get-tuple-element.38, bf16[2048,1536]{1,0:T(8,128)(2,1)S(1)} %get-tuple-element.39), kind=kOutput, calls=%fused_computation.6 | convolution fusion | flops 1610612736 | bytes 8912896 | tf_op jit(solution)/shard_map/dot_general | solution.py:172
  22.9 3.4 %collective-permute-start.3 = (bf16[160,1536]{1,0:T(8,128)(2,1)S(1)}, bf16[160,1536]{1,0:T(8,128)(2,1)S(1)}, u32[]{:S(2)}, u32[]{:S(2)}) collective-permute-start(bf16[160,1536]{1,0:T(8,128)(2,1)S(1)} %get-tuple-element.43), channel_id=1, source_target_pairs={{0,2},{2,0},{4,6},{6,4},{8,10},{10,8},{12,14},{14,12},{1,3},{3,1},... | collective-permute-start | bytes 1474568 | tf_op jit(solution)/shard_map/ppermute | solution.py:506
  26.4 1.8 %collective-permute-done.1.cx_ref = s16[1552,128]{1,0:T(8,128)(2,1)S(1)} collective-permute-done((s16[1552,128]{1,0:T(8,128)(2,1)S(1)}, s16[1552,128]{1,0:T(8,128)(2,1)S(1)}, u32[]{:S(2)}, u32[]{:S(2)}) %collective-permute-start.1) | collective-permute-done | bytes 397344 | tf_op jit(solution)/shard_map/ppermute | solution.py:499
  28.2 0.8 %join_qwen.1 = (bf16[128,1664]{1,0:T(8,128)(2,1)S(1)}, f32[128,128]{1,0:T(8,128)S(1)}) custom-call(f32[256,1536]{1,0:T(8,128)S(1)} %fusion.3.own_ref, f32[128,128]{1,0:T(8,128)S(1)} %get-tuple-element.40.squares_ref, s16[1552,128]{1,0:T(8,128)(2,1)S(1)} %collective-permute-done.cy_ref, s16[1552,128]{1,0:T(8,128)(2,1)S(1)} %collective-permute-done.1.cx_ref, ...), custom_call_target="tpu_custom_call" | custom-call | flops 20000000000 | bytes 8388608 | tf_op jit(solution)/shard_map/join_qwen/pallas_call | solution.py:315
  29.0 0.7 %collective-permute-start.10 = (bf16[128,1664]{1,0:T(8,128)(2,1)S(1)}, bf16[128,1664]{1,0:T(8,128)(2,1)S(1)}, u32[]{:S(2)}, u32[]{:S(2)}) collective-permute-start(bf16[128,1664]{1,0:T(8,128)(2,1)S(1)} %get-tuple-element.49.u_ref), channel_id=1, source_target_pairs={{2,4},{4,2},{6,8},{8,6},{10,12},{12,10},{3,5},{5,3},{7,9},{9,7},{1... | collective-permute-start | bytes 1277960 | tf_op jit(solution)/shard_map/ppermute | solution.py:511
  29.8 1.2 %join_llama.1 = (f32[128,1536]{1,0:T(8,128)S(1)}, f32[8,128]{1,0:T(8,128)S(1)}) custom-call(f32[256,1536]{1,0:T(8,128)S(1)} %fusion.3.own_ref, f32[128,128]{1,0:T(8,128)S(1)} %get-tuple-element.40.squares_ref, s16[1552,128]{1,0:T(8,128)(2,1)S(1)} %collective-permute-done.cy_ref, s16[1552,128]{1,0:T(8,128)(2,1)S(1)} %collective-permute-done.1.cx_ref, ...), custom_call_target="tpu_custom_call" | custom-call | flops 20000000000 | bytes 8388608 | tf_op jit(solution)/shard_map/join_llama/pallas_call | solution.py:360
  30.9 3.0 %collective-permute-start.5 = (f32[8,128]{1,0:T(8,128)S(1)}, f32[8,128]{1,0:T(8,128)S(1)}, u32[]{:S(2)}, u32[]{:S(2)}) collective-permute-start(f32[8,128]{1,0:T(8,128)S(1)} %get-tuple-element.47.refs_0_), channel_id=1, source_target_pairs={{0,2},{2,0},{4,6},{6,4},{8,10},{10,8},{12,14},{14,12},{1,3},{3,1},... | collective-permute-start | bytes 12296 | tf_op jit(solution)/shard_map/ppermute | solution.py:466
  33.9 0.8 %collective-permute-done.5.refs_1_ = f32[8,128]{1,0:T(8,128)S(1)} collective-permute-done((f32[8,128]{1,0:T(8,128)S(1)}, f32[8,128]{1,0:T(8,128)S(1)}, u32[]{:S(2)}, u32[]{:S(2)}) %collective-permute-start.5) | collective-permute-done | bytes 4128 | tf_op jit(solution)/shard_map/ppermute | solution.py:466
  35.1 2.1 %collective-permute-start.8 = (f32[16,128]{1,0:T(8,128)S(1)}, f32[16,128]{1,0:T(8,128)S(1)}, u32[]{:S(2)}, u32[]{:S(2)}) collective-permute-start(f32[16,128]{1,0:T(8,128)S(1)} %constant_dynamic-update-slice_fusion), channel_id=1, source_target_pairs={{0,12},{2,14},{4,8},{6,10},{8,4},{10,6},{12,0},{14,2},{1,13},{3,15... | collective-permute-start | bytes 24584 | tf_op jit(solution)/shard_map/ppermute | solution.py:466
  37.1 0.9 %collective-permute-start.7 = (f32[16,128]{1,0:T(8,128)S(1)}, f32[16,128]{1,0:T(8,128)S(1)}, u32[]{:S(2)}, u32[]{:S(2)}) collective-permute-start(f32[16,128]{1,0:T(8,128)S(1)} %constant_dynamic-update-slice_fusion), channel_id=1, source_target_pairs={{0,8},{2,10},{4,12},{6,14},{8,0},{10,2},{12,4},{14,6},{1,9},{3,11}... | collective-permute-start | bytes 24584 | tf_op jit(solution)/shard_map/ppermute | solution.py:466
  38.1 1.3 %collective-permute-start.6 = (f32[16,128]{1,0:T(8,128)S(1)}, f32[16,128]{1,0:T(8,128)S(1)}, u32[]{:S(2)}, u32[]{:S(2)}) collective-permute-start(f32[16,128]{1,0:T(8,128)S(1)} %constant_dynamic-update-slice_fusion), channel_id=1, source_target_pairs={{0,4},{2,6},{4,0},{6,2},{8,12},{10,14},{12,8},{14,10},{1,5},{3,7},... | collective-permute-start | bytes 24584 | tf_op jit(solution)/shard_map/ppermute | solution.py:466
  39.5 1.4 %map_parts.1 = (f32[128,1536]{1,0:T(8,128)S(1)}, f32[128,128]{1,0:T(8,128)S(1)}) custom-call(s32[11]{0:T(128)S(1)} %concatenate.6.meta_ref, bf16[128,1664]{1,0:T(8,128)(2,1)S(1)} %get-tuple-element.49.u_ref, bf16[128,1664]{1,0:T(8,128)(2,1)S(1)} %collective-permute-done.9.near_ref, bf16[128,1664]{1,0:T(8,128)(2,1)S(1)} %collective-permute-done.10.far_ref, ...), custom_call_target="tpu_custom_call" | custom-call | flops 268435456 | bytes 2097152 | tf_op jit(solution)/shard_map/map_parts/pallas_call | solution.py:408
  40.9 0.8 %collective-permute-done.7.refs_3_ = f32[16,128]{1,0:T(8,128)S(1)} collective-permute-done((f32[16,128]{1,0:T(8,128)S(1)}, f32[16,128]{1,0:T(8,128)S(1)}, u32[]{:S(2)}, u32[]{:S(2)}) %collective-permute-start.7) | collective-permute-done | bytes 8224 | tf_op jit(solution)/shard_map/ppermute | solution.py:466
  41.8 1.3 %finish.1 = (f32[128,1536]{1,0:T(8,128)}, f32[1,128]{1,0:T(1,128)}) custom-call(f32[8,128]{1,0:T(8,128)S(1)} %get-tuple-element.47.refs_0_, f32[8,128]{1,0:T(8,128)S(1)} %collective-permute-done.5.refs_1_, f32[16,128]{1,0:T(8,128)S(1)} %collective-permute-done.6.refs_2_, f32[16,128]{1,0:T(8,128)S(1)} %collective-permute-done.7.refs_3_, ...), custom_call_target="tpu_custom_call" | custom-call | flops 3932160 | bytes 2359296 | tf_op jit(solution)/shard_map/finish/pallas_call | solution.py:446
  (23 shorter events, 1.3 us)
Async XLA Ops:
  6.3 20.1 %collective-permute-start.2 = (s16[1552,128]{1,0:T(8,128)(2,1)S(1)}, s16[1552,128]{1,0:T(8,128)(2,1)S(1)}, u32[]{:S(2)}, u32[]{:S(2)}) collective-permute-start(s16[1552,128]{1,0:T(8,128)(2,1)S(1)} %encode_parts.3), channel_id=1, source_target_pairs={{0,17},{1,16},{16,1},{17,0},{2,19},{3,18},{18,3},{19,2},{4,21},{5,... | collective-permute-start | bytes 1191944 | tf_op jit(solution)/shard_map/ppermute | solution.py:493
  12.4 15.7 %collective-permute-start = (s16[1552,128]{1,0:T(8,128)(2,1)S(1)}, s16[1552,128]{1,0:T(8,128)(2,1)S(1)}, u32[]{:S(2)}, u32[]{:S(2)}) collective-permute-start(s16[1552,128]{1,0:T(8,128)(2,1)S(1)} %encode_parts.4), channel_id=1, source_target_pairs={{0,1},{1,0},{2,3},{3,2},{4,5},{5,4},{6,7},{7,6},{8,9},{9,8},{10,11... | collective-permute-start | bytes 1191944 | tf_op jit(solution)/shard_map/ppermute | solution.py:496
  13.0 3.0 %copy-start.2 = (s32[4]{0:T(128)S(1)}, s32[4]{0:T(128)}, u32[]{:S(2)}) copy-start(s32[4]{0:T(128)} %param.11) | copy-start | bytes 52
  13.0 3.0 %copy-start.3 = (s32[4]{0:T(128)S(1)}, s32[4]{0:T(128)}, u32[]{:S(2)}) copy-start(s32[4]{0:T(128)} %param.12) | copy-start | bytes 52
  13.0 3.2 %copy-start.1 = (s32[128]{0:T(128)S(1)}, s32[128]{0:T(128)}, u32[]{:S(2)}) copy-start(s32[128]{0:T(128)} %param.15) | copy-start | bytes 1540
  15.3 12.9 %collective-permute-start.1 = (s16[1552,128]{1,0:T(8,128)(2,1)S(1)}, s16[1552,128]{1,0:T(8,128)(2,1)S(1)}, u32[]{:S(2)}, u32[]{:S(2)}) collective-permute-start(s16[1552,128]{1,0:T(8,128)(2,1)S(1)} %encode_parts.5), channel_id=1, source_target_pairs={{0,16},{16,0},{1,17},{17,1},{2,18},{18,2},{3,19},{19,3},{4,20},{20... | collective-permute-start | bytes 1191944 | tf_op jit(solution)/shard_map/ppermute | solution.py:499
  20.4 9.3 %collective-permute-start.4 = (bf16[144,1536]{1,0:T(8,128)(2,1)S(1)}, bf16[144,1536]{1,0:T(8,128)(2,1)S(1)}, u32[]{:S(2)}, u32[]{:S(2)}) collective-permute-start(bf16[144,1536]{1,0:T(8,128)(2,1)S(1)} %get-tuple-element.45), channel_id=1, source_target_pairs={{2,4},{4,2},{6,8},{8,6},{10,12},{12,10},{3,5},{5,3},{7,9},{9,7},{1... | collective-permute-start | bytes 1327112 | tf_op jit(solution)/shard_map/ppermute | solution.py:507
  22.9 6.8 %collective-permute-start.3 = (bf16[160,1536]{1,0:T(8,128)(2,1)S(1)}, bf16[160,1536]{1,0:T(8,128)(2,1)S(1)}, u32[]{:S(2)}, u32[]{:S(2)}) collective-permute-start(bf16[160,1536]{1,0:T(8,128)(2,1)S(1)} %get-tuple-element.43), channel_id=1, source_target_pairs={{0,2},{2,0},{4,6},{6,4},{8,10},{10,8},{12,14},{14,12},{1,3},{3,1},... | collective-permute-start | bytes 1474568 | tf_op jit(solution)/shard_map/ppermute | solution.py:506
  29.0 10.4 %collective-permute-start.10 = (bf16[128,1664]{1,0:T(8,128)(2,1)S(1)}, bf16[128,1664]{1,0:T(8,128)(2,1)S(1)}, u32[]{:S(2)}, u32[]{:S(2)}) collective-permute-start(bf16[128,1664]{1,0:T(8,128)(2,1)S(1)} %get-tuple-element.49.u_ref), channel_id=1, source_target_pairs={{2,4},{4,2},{6,8},{8,6},{10,12},{12,10},{3,5},{5,3},{7,9},{9,7},{1... | collective-permute-start | bytes 1277960 | tf_op jit(solution)/shard_map/ppermute | solution.py:511
  29.8 9.7 %copy-start = (bf16[4,512,512]{2,1,0:T(8,128)(2,1)S(1)}, bf16[4,512,512]{2,1,0:T(8,128)(2,1)}, u32[]{:S(2)}) copy-start(bf16[4,512,512]{2,1,0:T(8,128)(2,1)} %w_ref.3) | copy-start | bytes 6291460
  30.9 3.8 %collective-permute-start.5 = (f32[8,128]{1,0:T(8,128)S(1)}, f32[8,128]{1,0:T(8,128)S(1)}, u32[]{:S(2)}, u32[]{:S(2)}) collective-permute-start(f32[8,128]{1,0:T(8,128)S(1)} %get-tuple-element.47.refs_0_), channel_id=1, source_target_pairs={{0,2},{2,0},{4,6},{6,4},{8,10},{10,8},{12,14},{14,12},{1,3},{3,1},... | collective-permute-start | bytes 12296 | tf_op jit(solution)/shard_map/ppermute | solution.py:466
  34.7 4.7 %collective-permute-start.9 = (bf16[128,1664]{1,0:T(8,128)(2,1)S(1)}, bf16[128,1664]{1,0:T(8,128)(2,1)S(1)}, u32[]{:S(2)}, u32[]{:S(2)}) collective-permute-start(bf16[128,1664]{1,0:T(8,128)(2,1)S(1)} %get-tuple-element.49.u_ref), channel_id=1, source_target_pairs={{0,2},{2,0},{4,6},{6,4},{8,10},{10,8},{12,14},{14,12},{1,3},{3,1},... | collective-permute-start | bytes 1277960 | tf_op jit(solution)/shard_map/ppermute | solution.py:517
  35.1 5.8 %collective-permute-start.8 = (f32[16,128]{1,0:T(8,128)S(1)}, f32[16,128]{1,0:T(8,128)S(1)}, u32[]{:S(2)}, u32[]{:S(2)}) collective-permute-start(f32[16,128]{1,0:T(8,128)S(1)} %constant_dynamic-update-slice_fusion), channel_id=1, source_target_pairs={{0,12},{2,14},{4,8},{6,10},{8,4},{10,6},{12,0},{14,2},{1,13},{3,15... | collective-permute-start | bytes 24584 | tf_op jit(solution)/shard_map/ppermute | solution.py:466
  37.1 4.5 %collective-permute-start.7 = (f32[16,128]{1,0:T(8,128)S(1)}, f32[16,128]{1,0:T(8,128)S(1)}, u32[]{:S(2)}, u32[]{:S(2)}) collective-permute-start(f32[16,128]{1,0:T(8,128)S(1)} %constant_dynamic-update-slice_fusion), channel_id=1, source_target_pairs={{0,8},{2,10},{4,12},{6,14},{8,0},{10,2},{12,4},{14,6},{1,9},{3,11}... | collective-permute-start | bytes 24584 | tf_op jit(solution)/shard_map/ppermute | solution.py:466
  38.1 3.7 %collective-permute-start.6 = (f32[16,128]{1,0:T(8,128)S(1)}, f32[16,128]{1,0:T(8,128)S(1)}, u32[]{:S(2)}, u32[]{:S(2)}) collective-permute-start(f32[16,128]{1,0:T(8,128)S(1)} %constant_dynamic-update-slice_fusion), channel_id=1, source_target_pairs={{0,4},{2,6},{4,0},{6,2},{8,12},{10,14},{12,8},{14,10},{1,5},{3,7},... | collective-permute-start | bytes 24584 | tf_op jit(solution)/shard_map/ppermute | solution.py:466

commit v6 on v5

--- a/solution.py
+++ b/solution.py
@@ -143,6 +143,31 @@
     return outs[:count], outs[count : 2 * count], outs[2 * count]
 
 
+def rows_kernel(which, hidden_ref, gain_ref, left_ref, squares_ref, held, sem):
+    rows = held.shape[0]
+    quarter = jnp.bitwise_xor(2 * lax.axis_index("mp") + lax.axis_index("rows"), which)
+    at = pl.ds(pl.multiple_of(quarter * rows, rows), rows)
+    hidden_copy = pltpu.make_async_copy(hidden_ref.at[at, :], held, sem)
+    hidden_copy.start()
+    hidden_copy.wait()
+    squares = prepare(held[...], gain_ref[...].astype(f32), left_ref, 0)
+    squares_ref[...] = jnp.broadcast_to(squares, (rows, LANES))
+
+
+def prep_rows(hidden, gain, which):
+    rows, feats = hidden.shape[0] // 4, hidden.shape[1]
+    vmem = pl.BlockSpec(memory_space=pltpu.VMEM)
+    return pl.pallas_call(
+        functools.partial(rows_kernel, which),
+        in_specs=[pl.BlockSpec(memory_space=pltpu.HBM), vmem],
+        out_shape=[jax.ShapeDtypeStruct((2 * rows, feats), bf16), jax.ShapeDtypeStruct((rows, LANES), f32)],
+        scratch_shapes=[pltpu.VMEM((rows, feats), bf16), pltpu.SemaphoreType.DMA],
+        compiler_params=params(),
+        cost_estimate=pl.CostEstimate(flops=1, bytes_accessed=6 * rows * feats, transcendentals=0),
+        name="prep_rows",
+    )(hidden, gain)
+
+
 def encode_kernel(count, both_ref, *refs):
     square_refs, outs = refs[:count], refs[count:]
     rows, cols = both_ref.shape[0] // count // 2, both_ref.shape[1]
@@ -172,10 +197,13 @@
     return jnp.dot(left, head, preferred_element_type=f32)
 
 
-def side_kernel(width, blocks, own_which, meta_ref, quarter_ref, token_ref, hidden_ref, gain_ref, w_ref, head_ref, near_ref, own_ref, far_ref, left_ref, squares_ref, head_out, held, gain_held, w_held, sum_ref, sem, gain_sem, w_sems, head_sem):
+def side_kernel(width, blocks, lists_ref, token_ref, hidden_ref, gain_ref, w_ref, head_ref, near_ref, own_ref, far_ref, left_ref, squares_ref, head_out, held, gain_held, w_held, sum_ref, meta_ref, sem, gain_sem, w_sems, head_sem, meta_sem):
     rows = token_ref.shape[1]
     slots = w_ref.shape[0]
-    at = pl.ds(pl.multiple_of(quarter_ref[own_which] * rows, rows), rows)
+    meta_copy = pltpu.make_async_copy(lists_ref, meta_ref, meta_sem)
+    meta_copy.start()
+    quarter = 2 * lax.axis_index("mp") + lax.axis_index("rows")
+    at = pl.ds(pl.multiple_of(quarter * rows, rows), rows)
     hidden_copy = pltpu.make_async_copy(hidden_ref.at[at, :], held, sem)
     gain_copy = pltpu.make_async_copy(gain_ref, gain_held, gain_sem)
     w_copies = [pltpu.make_async_copy(w_ref.at[k], w_held.at[k], w_sems.at[k]) for k in range(slots)]
@@ -185,7 +213,7 @@
         copy.start()
     head_copy = pltpu.make_async_copy(head_ref, head_out, head_sem)
     head_copy.start()
-    shard = meta_ref[1]
+    shard = lax.axis_index("vocab")
     near_at = jnp.where(shard % 2 == 0, 2, 0)
     token = jnp.transpose(jnp.broadcast_to(token_ref[...].astype(f32), (8, rows)))[:, :1].astype(i32)
     place = lax.broadcasted_iota(i32, (rows, width), 1)
@@ -194,13 +222,14 @@
     hidden_copy.wait()
     squares = prepare(held[...], gain_held[...].astype(f32), left_ref, 0)
     squares_ref[...] = jnp.broadcast_to(squares, (rows, LANES))
+    meta_copy.wait()
     for slot in range(slots):
         w_copies[slot].wait()
 
-        @pl.when(slot < meta_ref[2 + 2 * slots])
+        @pl.when(slot < meta_ref[2 * slots])
         def _():
-            source = jnp.clip(meta_ref[2 + slot] - (shard - 1) * blocks, 0, 3 * blocks - 1)
-            hits = (token - meta_ref[2 + slots + slot] * width == place).astype(bf16)
+            source = jnp.clip(meta_ref[slot] - (shard - 1) * blocks, 0, 3 * blocks - 1)
+            hits = (token - meta_ref[slots + slot] * width == place).astype(bf16)
             left = jnp.concatenate([hits, jnp.ones((EXTRA, width), bf16)], axis=0)
             found = lax.dot_general(
                 left, w_held[slot], (((1,), (1,)), ((), ())), preferred_element_type=f32
@@ -221,13 +250,12 @@
     head_copy.wait()
 
 
-def side_parts(meta, quarters, token, hidden, gain, weights, head, width):
+def side_parts(lists, token, hidden, gain, weights, head, width):
     rows, feats, cols = token.shape[1], hidden.shape[1], head.shape[1]
-    smem = pl.BlockSpec(memory_space=pltpu.SMEM)
     hbm = pl.BlockSpec(memory_space=pltpu.HBM)
     outs = pl.pallas_call(
-        functools.partial(side_kernel, width, cols // width, 0),
-        in_specs=[smem, smem, pl.BlockSpec(memory_space=pltpu.VMEM), hbm, hbm, hbm, hbm],
+        functools.partial(side_kernel, width, cols // width),
+        in_specs=[pl.BlockSpec(memory_space=pl.ANY), pl.BlockSpec(memory_space=pltpu.VMEM), hbm, hbm, hbm, hbm],
         out_shape=[jax.ShapeDtypeStruct((rows + many * EXTRA, cols), bf16) for many in (2, 1, 1)]
         + [jax.ShapeDtypeStruct((2 * rows, feats), bf16), jax.ShapeDtypeStruct((rows, LANES), f32)]
         + [jax.ShapeDtypeStruct(head.shape, head.dtype)],
@@ -236,15 +264,17 @@
             pltpu.VMEM(gain.shape, bf16),
             pltpu.VMEM(weights.shape, bf16),
             pltpu.VMEM((3, rows + EXTRA, cols), f32),
+            pltpu.SMEM(lists.shape, i32),
             pltpu.SemaphoreType.DMA,
             pltpu.SemaphoreType.DMA,
             pltpu.SemaphoreType.DMA((weights.shape[0],)),
             pltpu.SemaphoreType.DMA,
+            pltpu.SemaphoreType.DMA,
         ],
         compiler_params=params(),
         cost_estimate=pl.CostEstimate(flops=1, bytes_accessed=1, transcendentals=0),
         name="side_parts",
-    )(meta, quarters, token, hidden, gain, weights, head)
+    )(lists, token, hidden, gain, weights, head)
     return outs[:3], outs[3], outs[4], outs[5]
 
 
@@ -367,10 +397,12 @@
     )(own, squares, *codes, token, u, *columns, stats)
 
 
-def map_kernel(width, blocks, shards, meta_ref, u_ref, near_ref, far_ref, w_ref, m_ref, top_ref, all_ref, scale_ref):
+def map_kernel(width, blocks, shards, lists_ref, u_ref, near_ref, far_ref, w_ref, m_ref, top_ref, all_ref, scale_ref, meta_ref, meta_sem):
     rows = u_ref.shape[0]
     body = blocks * width
-    shard = meta_ref[1]
+    meta_copy = pltpu.make_async_copy(lists_ref, meta_ref, meta_sem)
+    meta_copy.start()
+    shard = lax.axis_index("vocab")
     slots = w_ref.shape[0]
     near_at = jnp.where(shard % 2 == 0, 2, 0)
 
@@ -386,12 +418,13 @@
         all_ref[k] = ref[:, :body]
         scale_ref[k] = jnp.broadcast_to(jnp.exp(peak - top), (rows, LANES))
     m_ref[...] = jnp.zeros_like(m_ref)
+    meta_copy.wait()
     for slot in range(slots):
 
-        @pl.when(slot < meta_ref[2 + 2 * slots])
+        @pl.when(slot < meta_ref[2 * slots])
         def _():
-            source = jnp.clip(meta_ref[2 + slot] - (shard - 1) * blocks, 0, 3 * blocks - 1)
-            target = jnp.clip(meta_ref[2 + slots + slot] - shard * blocks, 0, blocks - 1)
+            source = jnp.clip(meta_ref[slot] - (shard - 1) * blocks, 0, 3 * blocks - 1)
+            target = jnp.clip(meta_ref[slots + slot] - shard * blocks, 0, blocks - 1)
             inside = pl.multiple_of(source % blocks * width, width)
             picked = all_ref[source // blocks, :, pl.ds(inside, width)]
             term = jnp.dot(picked, w_ref[slot], preferred_element_type=f32)
@@ -401,21 +434,22 @@
     top_ref[...] = jnp.broadcast_to(top, (rows, LANES))
 
 
-def map_parts(meta, u, near, far, weights, width, shards):
+def map_parts(lists, u, near, far, weights, width, shards):
     rows, cols = u.shape[0], u.shape[1] - LANES
     blocks = cols // width
     whole = pl.BlockSpec(memory_space=pltpu.VMEM)
     return pl.pallas_call(
         functools.partial(map_kernel, width, blocks, shards),
-        in_specs=[pl.BlockSpec(memory_space=pltpu.SMEM)] + [whole] * 4,
+        in_specs=[pl.BlockSpec(memory_space=pl.ANY)] + [whole] * 4,
         out_shape=[jax.ShapeDtypeStruct((rows, cols), f32), jax.ShapeDtypeStruct((rows, LANES), f32)],
-        scratch_shapes=[pltpu.VMEM((3, rows, cols), bf16), pltpu.VMEM((3, rows, LANES), f32)],
+        scratch_shapes=[pltpu.VMEM((3, rows, cols), bf16), pltpu.VMEM((3, rows, LANES), f32)]
+        + [pltpu.SMEM(lists.shape, i32), pltpu.SemaphoreType.DMA],
         compiler_params=params(),
         cost_estimate=pl.CostEstimate(
             flops=2 * rows * weights.size, bytes_accessed=2 * weights.size, transcendentals=0
         ),
         name="map_parts",
-    )(meta, u, near, far, weights)
+    )(lists, u, near, far, weights)
 
 
 def finish_kernel(pieces, *refs):
@@ -481,25 +515,23 @@
     held_head = pltpu.with_memory_space_constraint(head, pltpu.HBM)
     width = pair_weight.shape[1]
     features = hidden.shape[1] * row_groups
-    model, shard, side = (lax.axis_index(name).astype(i32) for name in ("mp", "vocab", "rows"))
-    mine = 2 * model + side
-    quarters = jnp.stack([mine, mine ^ 1, mine ^ 2, mine ^ 3])
-    meta = jnp.concatenate([jnp.stack([model, shard]), pair_source, pair_target, pair_count])
+    lists = jnp.concatenate([pair_source, pair_target, pair_count])
 
     inside = [(i, i ^ 1) for i in range(shards)]
     across = [(i, i + 1 if i % 2 else i - 1) for i in range(1, shards - 1)]
-    lefts, squares, head = first_prep(held_hidden, held_gain, held_head, (3, 1, 2))
+    lefts, squares, head = first_prep(held_hidden, held_gain, held_head, (3, 1))
     (to_d,) = encode_parts(product(lefts[0], head), squares[:1])
     from_d = lax.ppermute(to_d, ("mp", "rows"), [(0, 3), (1, 2), (2, 1), (3, 0)])
     left_y, _ = lax.optimization_barrier((lefts[1], to_d))
     (to_y,) = encode_parts(product(left_y, head), squares[1:2])
     from_y = lax.ppermute(to_y, "rows", [(0, 1), (1, 0)])
-    left_x, _ = lax.optimization_barrier((lefts[2], to_y))
-    (to_x,) = encode_parts(product(left_x, head), squares[2:])
+    late_gain, _ = lax.optimization_barrier((norm_gain, to_y))
+    left_x, squares_x = prep_rows(held_hidden, late_gain, 2)
+    (to_x,) = encode_parts(product(left_x, head), [squares_x])
     from_x = lax.ppermute(to_x, "mp", [(0, 1), (1, 0)])
-    early, _ = lax.optimization_barrier((meta, to_x))
+    early, _ = lax.optimization_barrier((lists, to_x))
     (to_near, columns, to_far), left_own, squares_own, head = side_parts(
-        early, quarters, token, held_hidden, held_gain, held_weight, held_head, width
+        early, token, held_hidden, held_gain, held_weight, held_head, width
     )
     own = product(left_own, head)
     to_near, _ = lax.optimization_barrier((to_near, own))
@@ -515,7 +547,7 @@
     pieces, last = gather_pieces(stats, shards)
     late_u, _ = lax.optimization_barrier((u, last))
     near = lax.ppermute(late_u, "vocab", inside)
-    m, m_top = map_parts(meta, u, near, far, pair_weight, width, shards)
+    m, m_top = map_parts(lists, u, near, far, pair_weight, width, shards)
     out, nll = finish(pieces, e, m, m_top)
     return out, nll[0]
 

time: 43.4 us -> 44.2 us (1.018)
  Pallas kernels: 13.7 us -> 15.4 us
  waiting for transfers between devices: 3.62 us -> 2.73 us
    ppermute x1, waiting for transfers between devices: 1.82 us -> 0.29 us  [on_device(): from_x = lax.ppermute(to_x, 'mp', [(0, 1), (1, 0)])]
    pallas_call x1 -> x2, Pallas kernels: 4.23 us -> 5.18 us  [the longest x1 3.7 us: side_parts(): pl.pallas_call(functools.partial(side_kernel, width, cols // width), in_s...]
    ppermute x1, waiting for transfers between devices: 0.01 us -> 0.53 us  [on_device(): from_y = lax.ppermute(to_y, 'rows', [(0, 1), (1, 0)])]
  transfers between devices with their start and end apart: 11 -> 11, of which waited for: 5 -> 4; matrix products, arithmetic and copies ran while one was open for 13% -> 13% of each run, Pallas kernels for 20% -> 22%
where the time goes in v6:
time: 44.2 us; the launch traced here: 44 us
  starting transfers between devices  17.1 us (39%)
  Pallas kernels  15.4 us (35%)
  matrix products  7.24 us (16%)
  waiting for transfers between devices  2.73 us (6%)
  between operations  1.45 us (3%)
    ppermute x4, starting transfers between devices, gather_pieces(): lax.ppermute(sent, 'vocab', [(i, i ^ turn * step) for i in range(shards)])  7.34 us
    dot_general x4, matrix products, product(): return jnp.dot(left, head, preferred_element_type=f32)  7.24 us
    ppermute x1, starting transfers between devices, on_device(): lax.ppermute(to_d, ('mp', 'rows'), [(0, 3), (1, 2), (2, 1), (3, 0)])  3.93 us
    pallas_call x1, Pallas kernels, first_prep(): pl.pallas_call(functools.partial(first_kernel, kinds, rows), in_specs=[hb...  3.77 us
    pallas_call x1, Pallas kernels, side_parts(): pl.pallas_call(functools.partial(side_kernel, width, cols // width), in_s...  3.7 us
    ppermute x1, starting transfers between devices, on_device(): near_columns = lax.ppermute(to_near, 'vocab', inside)  3.43 us
    ppermute x4, waiting for transfers between devices, gather_pieces(): lax.ppermute(sent, 'vocab', [(i, i ^ turn * step) for i in range(shards)])  1.89 us
    pallas_call x1, Pallas kernels, map_parts(): pl.pallas_call(functools.partial(map_kernel, width, blocks, shards), in_s...  1.65 us
  transfers between devices with their start and end apart: 11, of which 4 were waited for; matrix products, arithmetic and copies ran while one was open for 13% of the time, Pallas kernels for 22%

profile of v6, /device:TPU:0, one launch (start us, length us, event | category | flops | bytes accessed | tf_op | source)
XLA Modules:
  0.0 44.0 jit_solution(3215602474552175286)
XLA Ops:
  0.6 3.8 %first_prep.1 = (bf16[256,2048]{1,0:T(8,128)(2,1)S(1)}, bf16[256,2048]{1,0:T(8,128)(2,1)S(1)}, f32[128,128]{1,0:T(8,128)S(1)}, f32[128,128]{1,0:T(8,128)S(1)}, bf16[2048,1536]{1,0:T(8,128)(2,1)S(1)}) custom-call(bf16[512,2048]{1,0:T(8,128)(2,1)} %bitcast.16, bf16[1,2048]{1,0:T(2,128)(2,1)} %gain_ref.4, bf16[2048,1536]{1,0:T(8,128)(2,1)} %bitcast.14), custom_call_target="tpu_custom_call" | custom-call | flops 4194304 | bytes 6291456 | tf_op jit(solution)/shard_map/first_prep/pallas_call | solution.py:124
  4.4 1.8 %fusion.both_ref = f32[256,1536]{1,0:T(8,128)S(1)} fusion(bf16[256,2048]{1,0:T(8,128)(2,1)S(1)} %get-tuple-element.29, bf16[2048,1536]{1,0:T(8,128)(2,1)S(1)} %get-tuple-element.30), kind=kOutput, calls=%fused_computation.3 | convolution fusion | flops 1610612736 | bytes 8912896 | tf_op jit(solution)/shard_map/dot_general | solution.py:197
  6.2 0.5 %encode_parts.3 = s16[1552,128]{1,0:T(8,128)(2,1)S(1)} custom-call(f32[256,1536]{1,0:T(8,128)S(1)} %fusion.both_ref, f32[128,128]{1,0:T(8,128)S(1)} %get-tuple-element.31.refs_0_), custom_call_target="tpu_custom_call" | custom-call | flops 3932160 | bytes 1966080 | tf_op jit(solution)/shard_map/encode_parts/pallas_call | solution.py:185
  6.7 3.9 %collective-permute-start.2 = (s16[1552,128]{1,0:T(8,128)(2,1)S(1)}, s16[1552,128]{1,0:T(8,128)(2,1)S(1)}, u32[]{:S(2)}, u32[]{:S(2)}) collective-permute-start(s16[1552,128]{1,0:T(8,128)(2,1)S(1)} %encode_parts.3), channel_id=1, source_target_pairs={{0,17},{1,16},{16,1},{17,0},{2,19},{3,18},{18,3},{19,2},{4,21},{5,... | collective-permute-start | bytes 1191944 | tf_op jit(solution)/shard_map/ppermute | solution.py:524
  10.6 1.8 %fusion.1.both_ref = f32[256,1536]{1,0:T(8,128)S(1)} fusion(bf16[256,2048]{1,0:T(8,128)(2,1)S(1)} %get-tuple-element.32, bf16[2048,1536]{1,0:T(8,128)(2,1)S(1)} %get-tuple-element.30), kind=kOutput, calls=%fused_computation.4 | convolution fusion | flops 1610612736 | bytes 8912896 | tf_op jit(solution)/shard_map/dot_general | solution.py:197
  12.4 0.5 %encode_parts.4 = s16[1552,128]{1,0:T(8,128)(2,1)S(1)} custom-call(f32[256,1536]{1,0:T(8,128)S(1)} %fusion.1.both_ref, f32[128,128]{1,0:T(8,128)S(1)} %get-tuple-element.33.refs_0_), custom_call_target="tpu_custom_call" | custom-call | flops 3932160 | bytes 1966080 | tf_op jit(solution)/shard_map/encode_parts/pallas_call | solution.py:185
  12.9 0.5 %collective-permute-start = (s16[1552,128]{1,0:T(8,128)(2,1)S(1)}, s16[1552,128]{1,0:T(8,128)(2,1)S(1)}, u32[]{:S(2)}, u32[]{:S(2)}) collective-permute-start(s16[1552,128]{1,0:T(8,128)(2,1)S(1)} %encode_parts.4), channel_id=1, source_target_pairs={{0,1},{1,0},{2,3},{3,2},{4,5},{5,4},{6,7},{7,6},{8,9},{9,8},{10,11... | collective-permute-start | bytes 1191944 | tf_op jit(solution)/shard_map/ppermute | solution.py:527
  13.5 1.5 %prep_rows.1 = (bf16[256,2048]{1,0:T(8,128)(2,1)S(1)}, f32[128,128]{1,0:T(8,128)S(1)}) custom-call(bf16[512,2048]{1,0:T(8,128)(2,1)} %bitcast.17, bf16[1,2048]{1,0:T(2,128)(2,1)S(1)} %copy-done.1), custom_call_target="tpu_custom_call" | custom-call | flops 1 | bytes 1572864 | tf_op jit(solution)/shard_map/prep_rows/pallas_call | solution.py:160
  15.0 1.8 %fusion.2.both_ref = f32[256,1536]{1,0:T(8,128)S(1)} fusion(bf16[256,2048]{1,0:T(8,128)(2,1)S(1)} %get-tuple-element.35, bf16[2048,1536]{1,0:T(8,128)(2,1)S(1)} %get-tuple-element.30), kind=kOutput, calls=%fused_computation.5 | convolution fusion | flops 1610612736 | bytes 8912896 | tf_op jit(solution)/shard_map/dot_general | solution.py:197
  18.2 3.7 %side_parts.1 = (bf16[160,1536]{1,0:T(8,128)(2,1)S(1)}, bf16[144,1536]{1,0:T(8,128)(2,1)S(1)}, bf16[144,1536]{1,0:T(8,128)(2,1)S(1)}, bf16[256,2048]{1,0:T(8,128...) custom-call(s32[9]{0:T(128)S(1)} %pad_add_fusion.lists_ref, s32[1,128]{1,0:T(1,128)S(1)} %bitcast.12, ...), custom_call_target="tpu_custom_call" | custom-call | flops 1 | bytes 1 | tf_op jit(solution)/shard_map/side_parts/pallas_call | solution.py:256
  21.9 0.7 %collective-permute-start.4 = (bf16[144,1536]{1,0:T(8,128)(2,1)S(1)}, bf16[144,1536]{1,0:T(8,128)(2,1)S(1)}, u32[]{:S(2)}, u32[]{:S(2)}) collective-permute-start(bf16[144,1536]{1,0:T(8,128)(2,1)S(1)} %get-tuple-element.45), channel_id=1, source_target_pairs={{2,4},{4,2},{6,8},{8,6},{10,12},{12,10},{3,5},{5,3},{7,9},{9,7},{1... | collective-permute-start | bytes 1327112 | tf_op jit(solution)/shard_map/ppermute | solution.py:539
  22.6 1.8 %fusion.3.own_ref = f32[256,1536]{1,0:T(8,128)S(1)} fusion(bf16[256,2048]{1,0:T(8,128)(2,1)S(1)} %get-tuple-element.38, bf16[2048,1536]{1,0:T(8,128)(2,1)S(1)} %get-tuple-element.39), kind=kOutput, calls=%fused_computation.6 | convolution fusion | flops 1610612736 | bytes 8912896 | tf_op jit(solution)/shard_map/dot_general | solution.py:197
  24.4 3.4 %collective-permute-start.3 = (bf16[160,1536]{1,0:T(8,128)(2,1)S(1)}, bf16[160,1536]{1,0:T(8,128)(2,1)S(1)}, u32[]{:S(2)}, u32[]{:S(2)}) collective-permute-start(bf16[160,1536]{1,0:T(8,128)(2,1)S(1)} %get-tuple-element.43), channel_id=1, source_target_pairs={{0,2},{2,0},{4,6},{6,4},{8,10},{10,8},{12,14},{14,12},{1,3},{3,1},... | collective-permute-start | bytes 1474568 | tf_op jit(solution)/shard_map/ppermute | solution.py:538
  27.8 0.5 %collective-permute-done.cy_ref = s16[1552,128]{1,0:T(8,128)(2,1)S(1)} collective-permute-done((s16[1552,128]{1,0:T(8,128)(2,1)S(1)}, s16[1552,128]{1,0:T(8,128)(2,1)S(1)}, u32[]{:S(2)}, u32[]{:S(2)}) %collective-permute-start) | collective-permute-done | bytes 397344 | tf_op jit(solution)/shard_map/ppermute | solution.py:527
  28.6 0.8 %join_qwen.1 = (bf16[128,1664]{1,0:T(8,128)(2,1)S(1)}, f32[128,128]{1,0:T(8,128)S(1)}) custom-call(f32[256,1536]{1,0:T(8,128)S(1)} %fusion.3.own_ref, f32[128,128]{1,0:T(8,128)S(1)} %get-tuple-element.40.squares_ref, s16[1552,128]{1,0:T(8,128)(2,1)S(1)} %collective-permute-done.cy_ref, s16[1552,128]{1,0:T(8,128)(2,1)S(1)} %collective-permute-done.1.cx_ref, ...), custom_call_target="tpu_custom_call" | custom-call | flops 20000000000 | bytes 8388608 | tf_op jit(solution)/shard_map/join_qwen/pallas_call | solution.py:345
  29.5 0.7 %collective-permute-start.10 = (bf16[128,1664]{1,0:T(8,128)(2,1)S(1)}, bf16[128,1664]{1,0:T(8,128)(2,1)S(1)}, u32[]{:S(2)}, u32[]{:S(2)}) collective-permute-start(bf16[128,1664]{1,0:T(8,128)(2,1)S(1)} %get-tuple-element.49.u_ref), channel_id=1, source_target_pairs={{2,4},{4,2},{6,8},{8,6},{10,12},{12,10},{3,5},{5,3},{7,9},{9,7},{1... | collective-permute-start | bytes 1277960 | tf_op jit(solution)/shard_map/ppermute | solution.py:543
  30.2 1.2 %join_llama.1 = (f32[128,1536]{1,0:T(8,128)S(1)}, f32[8,128]{1,0:T(8,128)S(1)}) custom-call(f32[256,1536]{1,0:T(8,128)S(1)} %fusion.3.own_ref, f32[128,128]{1,0:T(8,128)S(1)} %get-tuple-element.40.squares_ref, s16[1552,128]{1,0:T(8,128)(2,1)S(1)} %collective-permute-done.cy_ref, s16[1552,128]{1,0:T(8,128)(2,1)S(1)} %collective-permute-done.1.cx_ref, ...), custom_call_target="tpu_custom_call" | custom-call | flops 20000000000 | bytes 8388608 | tf_op jit(solution)/shard_map/join_llama/pallas_call | solution.py:390
  31.4 3.0 %collective-permute-start.5 = (f32[8,128]{1,0:T(8,128)S(1)}, f32[8,128]{1,0:T(8,128)S(1)}, u32[]{:S(2)}, u32[]{:S(2)}) collective-permute-start(f32[8,128]{1,0:T(8,128)S(1)} %get-tuple-element.47.refs_0_), channel_id=1, source_target_pairs={{0,2},{2,0},{4,6},{6,4},{8,10},{10,8},{12,14},{14,12},{1,3},{3,1},... | collective-permute-start | bytes 12296 | tf_op jit(solution)/shard_map/ppermute | solution.py:500
  34.3 0.8 %collective-permute-done.5.refs_1_ = f32[8,128]{1,0:T(8,128)S(1)} collective-permute-done((f32[8,128]{1,0:T(8,128)S(1)}, f32[8,128]{1,0:T(8,128)S(1)}, u32[]{:S(2)}, u32[]{:S(2)}) %collective-permute-start.5) | collective-permute-done | bytes 4128 | tf_op jit(solution)/shard_map/ppermute | solution.py:500
  35.5 2.6 %collective-permute-start.8 = (f32[16,128]{1,0:T(8,128)S(1)}, f32[16,128]{1,0:T(8,128)S(1)}, u32[]{:S(2)}, u32[]{:S(2)}) collective-permute-start(f32[16,128]{1,0:T(8,128)S(1)} %constant_dynamic-update-slice_fusion), channel_id=1, source_target_pairs={{0,12},{2,14},{4,8},{6,10},{8,4},{10,6},{12,0},{14,2},{1,13},{3,15... | collective-permute-start | bytes 24584 | tf_op jit(solution)/shard_map/ppermute | solution.py:500
  38.6 1.3 %collective-permute-start.6 = (f32[16,128]{1,0:T(8,128)S(1)}, f32[16,128]{1,0:T(8,128)S(1)}, u32[]{:S(2)}, u32[]{:S(2)}) collective-permute-start(f32[16,128]{1,0:T(8,128)S(1)} %constant_dynamic-update-slice_fusion), channel_id=1, source_target_pairs={{0,4},{2,6},{4,0},{6,2},{8,12},{10,14},{12,8},{14,10},{1,5},{3,7},... | collective-permute-start | bytes 24584 | tf_op jit(solution)/shard_map/ppermute | solution.py:500
  39.9 1.7 %map_parts.1 = (f32[128,1536]{1,0:T(8,128)S(1)}, f32[128,128]{1,0:T(8,128)S(1)}) custom-call(s32[9]{0:T(128)S(1)} %pad_add_fusion.lists_ref, bf16[128,1664]{1,0:T(8,128)(2,1)S(1)} %get-tuple-element.49.u_ref, bf16[128,1664]{1,0:T(8,128)(2,1)S(1)} %collective-permute-done.9.near_ref, bf16[128,1664]{1,0:T(8,128)(2,1)S(1)} %collective-permute-done.10.far_ref, ...), custom_call_target="tpu_custom_call" | custom-call | flops 268435456 | bytes 2097152 | tf_op jit(solution)/shard_map/map_parts/pallas_call | solution.py:441
  41.6 1.1 %collective-permute-done.7.refs_3_ = f32[16,128]{1,0:T(8,128)S(1)} collective-permute-done((f32[16,128]{1,0:T(8,128)S(1)}, f32[16,128]{1,0:T(8,128)S(1)}, u32[]{:S(2)}, u32[]{:S(2)}) %collective-permute-start.7) | collective-permute-done | bytes 8224 | tf_op jit(solution)/shard_map/ppermute | solution.py:500
  42.7 1.3 %finish.1 = (f32[128,1536]{1,0:T(8,128)}, f32[1,128]{1,0:T(1,128)}) custom-call(f32[8,128]{1,0:T(8,128)S(1)} %get-tuple-element.47.refs_0_, f32[8,128]{1,0:T(8,128)S(1)} %collective-permute-done.5.refs_1_, f32[16,128]{1,0:T(8,128)S(1)} %collective-permute-done.6.refs_2_, f32[16,128]{1,0:T(8,128)S(1)} %collective-permute-done.7.refs_3_, ...), custom_call_target="tpu_custom_call" | custom-call | flops 3932160 | bytes 2359296 | tf_op jit(solution)/shard_map/finish/pallas_call | solution.py:480
  (25 shorter events, 1.8 us)
Async XLA Ops:
  6.7 21.1 %collective-permute-start.2 = (s16[1552,128]{1,0:T(8,128)(2,1)S(1)}, s16[1552,128]{1,0:T(8,128)(2,1)S(1)}, u32[]{:S(2)}, u32[]{:S(2)}) collective-permute-start(s16[1552,128]{1,0:T(8,128)(2,1)S(1)} %encode_parts.3), channel_id=1, source_target_pairs={{0,17},{1,16},{16,1},{17,0},{2,19},{3,18},{18,3},{19,2},{4,21},{5,... | collective-permute-start | bytes 1191944 | tf_op jit(solution)/shard_map/ppermute | solution.py:524
  10.6 2.8 %copy-start.1 = (bf16[1,2048]{1,0:T(2,128)(2,1)S(1)}, bf16[1,2048]{1,0:T(2,128)(2,1)}, u32[]{:S(2)}) copy-start(bf16[1,2048]{1,0:T(2,128)(2,1)} %gain_ref.4) | copy-start | bytes 12292
  12.9 15.4 %collective-permute-start = (s16[1552,128]{1,0:T(8,128)(2,1)S(1)}, s16[1552,128]{1,0:T(8,128)(2,1)S(1)}, u32[]{:S(2)}, u32[]{:S(2)}) collective-permute-start(s16[1552,128]{1,0:T(8,128)(2,1)S(1)} %encode_parts.4), channel_id=1, source_target_pairs={{0,1},{1,0},{2,3},{3,2},{4,5},{5,4},{6,7},{7,6},{8,9},{9,8},{10,11... | collective-permute-start | bytes 1191944 | tf_op jit(solution)/shard_map/ppermute | solution.py:527
  15.0 3.1 %copy-start.3 = (s32[4]{0:T(128)S(1)}, s32[4]{0:T(128)}, u32[]{:S(2)}) copy-start(s32[4]{0:T(128)} %param.12) | copy-start | bytes 52
  15.0 3.1 %copy-start.4 = (s32[4]{0:T(128)S(1)}, s32[4]{0:T(128)}, u32[]{:S(2)}) copy-start(s32[4]{0:T(128)} %param.11) | copy-start | bytes 52
  15.0 3.2 %copy-start.2 = (s32[128]{0:T(128)S(1)}, s32[128]{0:T(128)}, u32[]{:S(2)}) copy-start(s32[128]{0:T(128)} %param.15) | copy-start | bytes 1540
  17.3 11.4 %collective-permute-start.1 = (s16[1552,128]{1,0:T(8,128)(2,1)S(1)}, s16[1552,128]{1,0:T(8,128)(2,1)S(1)}, u32[]{:S(2)}, u32[]{:S(2)}) collective-permute-start(s16[1552,128]{1,0:T(8,128)(2,1)S(1)} %encode_parts.5), channel_id=1, source_target_pairs={{0,16},{16,0},{1,17},{17,1},{2,18},{18,2},{3,19},{19,3},{4,20},{20... | collective-permute-start | bytes 1191944 | tf_op jit(solution)/shard_map/ppermute | solution.py:531
  21.9 8.3 %collective-permute-start.4 = (bf16[144,1536]{1,0:T(8,128)(2,1)S(1)}, bf16[144,1536]{1,0:T(8,128)(2,1)S(1)}, u32[]{:S(2)}, u32[]{:S(2)}) collective-permute-start(bf16[144,1536]{1,0:T(8,128)(2,1)S(1)} %get-tuple-element.45), channel_id=1, source_target_pairs={{2,4},{4,2},{6,8},{8,6},{10,12},{12,10},{3,5},{5,3},{7,9},{9,7},{1... | collective-permute-start | bytes 1327112 | tf_op jit(solution)/shard_map/ppermute | solution.py:539
  24.4 5.8 %collective-permute-start.3 = (bf16[160,1536]{1,0:T(8,128)(2,1)S(1)}, bf16[160,1536]{1,0:T(8,128)(2,1)S(1)}, u32[]{:S(2)}, u32[]{:S(2)}) collective-permute-start(bf16[160,1536]{1,0:T(8,128)(2,1)S(1)} %get-tuple-element.43), channel_id=1, source_target_pairs={{0,2},{2,0},{4,6},{6,4},{8,10},{10,8},{12,14},{14,12},{1,3},{3,1},... | collective-permute-start | bytes 1474568 | tf_op jit(solution)/shard_map/ppermute | solution.py:538
  29.5 10.4 %collective-permute-start.10 = (bf16[128,1664]{1,0:T(8,128)(2,1)S(1)}, bf16[128,1664]{1,0:T(8,128)(2,1)S(1)}, u32[]{:S(2)}, u32[]{:S(2)}) collective-permute-start(bf16[128,1664]{1,0:T(8,128)(2,1)S(1)} %get-tuple-element.49.u_ref), channel_id=1, source_target_pairs={{2,4},{4,2},{6,8},{8,6},{10,12},{12,10},{3,5},{5,3},{7,9},{9,7},{1... | collective-permute-start | bytes 1277960 | tf_op jit(solution)/shard_map/ppermute | solution.py:543
  30.2 9.7 %copy-start = (bf16[4,512,512]{2,1,0:T(8,128)(2,1)S(1)}, bf16[4,512,512]{2,1,0:T(8,128)(2,1)}, u32[]{:S(2)}) copy-start(bf16[4,512,512]{2,1,0:T(8,128)(2,1)} %w_ref.3) | copy-start | bytes 6291460
  31.4 3.8 %collective-permute-start.5 = (f32[8,128]{1,0:T(8,128)S(1)}, f32[8,128]{1,0:T(8,128)S(1)}, u32[]{:S(2)}, u32[]{:S(2)}) collective-permute-start(f32[8,128]{1,0:T(8,128)S(1)} %get-tuple-element.47.refs_0_), channel_id=1, source_target_pairs={{0,2},{2,0},{4,6},{6,4},{8,10},{10,8},{12,14},{14,12},{1,3},{3,1},... | collective-permute-start | bytes 12296 | tf_op jit(solution)/shard_map/ppermute | solution.py:500
  35.2 4.7 %collective-permute-start.9 = (bf16[128,1664]{1,0:T(8,128)(2,1)S(1)}, bf16[128,1664]{1,0:T(8,128)(2,1)S(1)}, u32[]{:S(2)}, u32[]{:S(2)}) collective-permute-start(bf16[128,1664]{1,0:T(8,128)(2,1)S(1)} %get-tuple-element.49.u_ref), channel_id=1, source_target_pairs={{0,2},{2,0},{4,6},{6,4},{8,10},{10,8},{12,14},{14,12},{1,3},{3,1},... | collective-permute-start | bytes 1277960 | tf_op jit(solution)/shard_map/ppermute | solution.py:549
  35.5 6.1 %collective-permute-start.8 = (f32[16,128]{1,0:T(8,128)S(1)}, f32[16,128]{1,0:T(8,128)S(1)}, u32[]{:S(2)}, u32[]{:S(2)}) collective-permute-start(f32[16,128]{1,0:T(8,128)S(1)} %constant_dynamic-update-slice_fusion), channel_id=1, source_target_pairs={{0,12},{2,14},{4,8},{6,10},{8,4},{10,6},{12,0},{14,2},{1,13},{3,15... | collective-permute-start | bytes 24584 | tf_op jit(solution)/shard_map/ppermute | solution.py:500
  38.1 4.6 %collective-permute-start.7 = (f32[16,128]{1,0:T(8,128)S(1)}, f32[16,128]{1,0:T(8,128)S(1)}, u32[]{:S(2)}, u32[]{:S(2)}) collective-permute-start(f32[16,128]{1,0:T(8,128)S(1)} %constant_dynamic-update-slice_fusion), channel_id=1, source_target_pairs={{0,8},{2,10},{4,12},{6,14},{8,0},{10,2},{12,4},{14,6},{1,9},{3,11}... | collective-permute-start | bytes 24584 | tf_op jit(solution)/shard_map/ppermute | solution.py:500
  38.6 4.1 %collective-permute-start.6 = (f32[16,128]{1,0:T(8,128)S(1)}, f32[16,128]{1,0:T(8,128)S(1)}, u32[]{:S(2)}, u32[]{:S(2)}) collective-permute-start(f32[16,128]{1,0:T(8,128)S(1)} %constant_dynamic-update-slice_fusion), channel_id=1, source_target_pairs={{0,4},{2,6},{4,0},{6,2},{8,12},{10,14},{12,8},{14,10},{1,5},{3,7},... | collective-permute-start | bytes 24584 | tf_op jit(solution)/shard_map/ppermute | solution.py:500

commit v7 on v6

--- a/solution.py
+++ b/solution.py
@@ -141,31 +141,6 @@
         name="first_prep",
     )(hidden, gain, head)
     return outs[:count], outs[count : 2 * count], outs[2 * count]
-
-
-def rows_kernel(which, hidden_ref, gain_ref, left_ref, squares_ref, held, sem):
-    rows = held.shape[0]
-    quarter = jnp.bitwise_xor(2 * lax.axis_index("mp") + lax.axis_index("rows"), which)
-    at = pl.ds(pl.multiple_of(quarter * rows, rows), rows)
-    hidden_copy = pltpu.make_async_copy(hidden_ref.at[at, :], held, sem)
-    hidden_copy.start()
-    hidden_copy.wait()
-    squares = prepare(held[...], gain_ref[...].astype(f32), left_ref, 0)
-    squares_ref[...] = jnp.broadcast_to(squares, (rows, LANES))
-
-
-def prep_rows(hidden, gain, which):
-    rows, feats = hidden.shape[0] // 4, hidden.shape[1]
-    vmem = pl.BlockSpec(memory_space=pltpu.VMEM)
-    return pl.pallas_call(
-        functools.partial(rows_kernel, which),
-        in_specs=[pl.BlockSpec(memory_space=pltpu.HBM), vmem],
-        out_shape=[jax.ShapeDtypeStruct((2 * rows, feats), bf16), jax.ShapeDtypeStruct((rows, LANES), f32)],
-        scratch_shapes=[pltpu.VMEM((rows, feats), bf16), pltpu.SemaphoreType.DMA],
-        compiler_params=params(),
-        cost_estimate=pl.CostEstimate(flops=1, bytes_accessed=6 * rows * feats, transcendentals=0),
-        name="prep_rows",
-    )(hidden, gain)
 
 
 def encode_kernel(count, both_ref, *refs):
@@ -519,15 +494,14 @@
 
     inside = [(i, i ^ 1) for i in range(shards)]
     across = [(i, i + 1 if i % 2 else i - 1) for i in range(1, shards - 1)]
-    lefts, squares, head = first_prep(held_hidden, held_gain, held_head, (3, 1))
+    lefts, squares, head = first_prep(held_hidden, held_gain, held_head, (3, 1, 2))
     (to_d,) = encode_parts(product(lefts[0], head), squares[:1])
     from_d = lax.ppermute(to_d, ("mp", "rows"), [(0, 3), (1, 2), (2, 1), (3, 0)])
     left_y, _ = lax.optimization_barrier((lefts[1], to_d))
     (to_y,) = encode_parts(product(left_y, head), squares[1:2])
     from_y = lax.ppermute(to_y, "rows", [(0, 1), (1, 0)])
-    late_gain, _ = lax.optimization_barrier((norm_gain, to_y))
-    left_x, squares_x = prep_rows(held_hidden, late_gain, 2)
-    (to_x,) = encode_parts(product(left_x, head), [squares_x])
+    left_x, _ = lax.optimization_barrier((lefts[2], to_y))
+    (to_x,) = encode_parts(product(left_x, head), squares[2:])
     from_x = lax.ppermute(to_x, "mp", [(0, 1), (1, 0)])
     early, _ = lax.optimization_barrier((lists, to_x))
     (to_near, columns, to_far), left_own, squares_own, head = side_parts(

time: 44.2 us -> 43.4 us (0.982)
  Pallas kernels: 15.4 us -> 13.5 us
  waiting for transfers between devices: 2.73 us -> 3.93 us
    ppermute x1, waiting for transfers between devices: 0.29 us -> 2.43 us  [on_device(): from_x = lax.ppermute(to_x, 'mp', [(0, 1), (1, 0)])]
    pallas_call x1 -> x0, Pallas kernels: 1.47 us -> none  [prep_rows(): pl.pallas_call(functools.partial(rows_kernel, which), in_specs=[pl.BlockS...]
    ppermute x1, waiting for transfers between devices: 0.53 us -> 0.01 us  [on_device(): from_y = lax.ppermute(to_y, 'rows', [(0, 1), (1, 0)])]
  transfers between devices with their start and end apart: 11 -> 11, of which waited for: 4 -> 4; matrix products, arithmetic and copies ran while one was open for 13% -> 13% of each run, Pallas kernels for 22% -> 19%
where the time goes in v7:
time: 43.4 us; the launch traced here: 43.1 us
  starting transfers between devices  17.1 us (39%)
  Pallas kernels  13.5 us (31%)
  matrix products  7.11 us (16%)
  waiting for transfers between devices  3.93 us (9%)
  between operations  1.42 us (3%)
    ppermute x4, starting transfers between devices, gather_pieces(): lax.ppermute(sent, 'vocab', [(i, i ^ turn * step) for i in range(shards)])  7.34 us
    dot_general x4, matrix products, product(): return jnp.dot(left, head, preferred_element_type=f32)  7.11 us
    ppermute x1, starting transfers between devices, on_device(): lax.ppermute(to_d, ('mp', 'rows'), [(0, 3), (1, 2), (2, 1), (3, 0)])  3.93 us
    pallas_call x1, Pallas kernels, side_parts(): pl.pallas_call(functools.partial(side_kernel, width, cols // width), in_s...  3.7 us
    ppermute x1, starting transfers between devices, on_device(): near_columns = lax.ppermute(to_near, 'vocab', inside)  3.44 us
    pallas_call x1, Pallas kernels, first_prep(): pl.pallas_call(functools.partial(first_kernel, kinds, rows), in_specs=[hb...  3.35 us
    ppermute x1, waiting for transfers between devices, on_device(): from_x = lax.ppermute(to_x, 'mp', [(0, 1), (1, 0)])  2.43 us
    pallas_call x1, Pallas kernels, map_parts(): pl.pallas_call(functools.partial(map_kernel, width, blocks, shards), in_s...  1.65 us
  transfers between devices with their start and end apart: 11, of which 4 were waited for; matrix products, arithmetic and copies ran while one was open for 13% of the time, Pallas kernels for 19%

profile of v7, /device:TPU:0, one launch (start us, length us, event | category | flops | bytes accessed | tf_op | source)
XLA Modules:
  0.0 43.1 jit_solution(8367713555371846724)
XLA Ops:
  0.6 3.4 %first_prep.1 = (bf16[256,2048]{1,0:T(8,128)(2,1)S(1)}, bf16[256,2048]{1,0:T(8,128)(2,1)S(1)}, bf16[256,2048]{1,0:T(8,128)(2,1)S(1)}, f32[128,128]{1,0:T(8,128)S...) custom-call(bf16[512,2048]{1,0:T(8,128)(2,1)} %bitcast.16, ...), custom_call_target="tpu_custom_call" | custom-call | flops 6291456 | bytes 6291456 | tf_op jit(solution)/shard_map/first_prep/pallas_call | solution.py:124
  4.0 1.8 %fusion.both_ref = f32[256,1536]{1,0:T(8,128)S(1)} fusion(bf16[256,2048]{1,0:T(8,128)(2,1)S(1)} %get-tuple-element.30, bf16[2048,1536]{1,0:T(8,128)(2,1)S(1)} %get-tuple-element.31), kind=kOutput, calls=%fused_computation.3 | convolution fusion | flops 1610612736 | bytes 8912896 | tf_op jit(solution)/shard_map/dot_general | solution.py:172
  5.8 0.5 %encode_parts.3 = s16[1552,128]{1,0:T(8,128)(2,1)S(1)} custom-call(f32[256,1536]{1,0:T(8,128)S(1)} %fusion.both_ref, f32[128,128]{1,0:T(8,128)S(1)} %get-tuple-element.32.refs_0_), custom_call_target="tpu_custom_call" | custom-call | flops 3932160 | bytes 1966080 | tf_op jit(solution)/shard_map/encode_parts/pallas_call | solution.py:160
  6.3 3.9 %collective-permute-start.2 = (s16[1552,128]{1,0:T(8,128)(2,1)S(1)}, s16[1552,128]{1,0:T(8,128)(2,1)S(1)}, u32[]{:S(2)}, u32[]{:S(2)}) collective-permute-start(s16[1552,128]{1,0:T(8,128)(2,1)S(1)} %encode_parts.3), channel_id=1, source_target_pairs={{0,17},{1,16},{16,1},{17,0},{2,19},{3,18},{18,3},{19,2},{4,21},{5,... | collective-permute-start | bytes 1191944 | tf_op jit(solution)/shard_map/ppermute | solution.py:499
  10.2 1.8 %fusion.1.both_ref = f32[256,1536]{1,0:T(8,128)S(1)} fusion(bf16[256,2048]{1,0:T(8,128)(2,1)S(1)} %get-tuple-element.33, bf16[2048,1536]{1,0:T(8,128)(2,1)S(1)} %get-tuple-element.31), kind=kOutput, calls=%fused_computation.4 | convolution fusion | flops 1610612736 | bytes 8912896 | tf_op jit(solution)/shard_map/dot_general | solution.py:172
  12.0 0.5 %encode_parts.4 = s16[1552,128]{1,0:T(8,128)(2,1)S(1)} custom-call(f32[256,1536]{1,0:T(8,128)S(1)} %fusion.1.both_ref, f32[128,128]{1,0:T(8,128)S(1)} %get-tuple-element.34.refs_0_), custom_call_target="tpu_custom_call" | custom-call | flops 3932160 | bytes 1966080 | tf_op jit(solution)/shard_map/encode_parts/pallas_call | solution.py:160
  12.4 0.5 %collective-permute-start = (s16[1552,128]{1,0:T(8,128)(2,1)S(1)}, s16[1552,128]{1,0:T(8,128)(2,1)S(1)}, u32[]{:S(2)}, u32[]{:S(2)}) collective-permute-start(s16[1552,128]{1,0:T(8,128)(2,1)S(1)} %encode_parts.4), channel_id=1, source_target_pairs={{0,1},{1,0},{2,3},{3,2},{4,5},{5,4},{6,7},{7,6},{8,9},{9,8},{10,11... | collective-permute-start | bytes 1191944 | tf_op jit(solution)/shard_map/ppermute | solution.py:502
  13.0 1.8 %fusion.2.both_ref = f32[256,1536]{1,0:T(8,128)S(1)} fusion(bf16[256,2048]{1,0:T(8,128)(2,1)S(1)} %get-tuple-element.35, bf16[2048,1536]{1,0:T(8,128)(2,1)S(1)} %get-tuple-element.31), kind=kOutput, calls=%fused_computation.5 | convolution fusion | flops 1610612736 | bytes 8912896 | tf_op jit(solution)/shard_map/dot_general | solution.py:172
  16.1 3.7 %side_parts.1 = (bf16[160,1536]{1,0:T(8,128)(2,1)S(1)}, bf16[144,1536]{1,0:T(8,128)(2,1)S(1)}, bf16[144,1536]{1,0:T(8,128)(2,1)S(1)}, bf16[256,2048]{1,0:T(8,128...) custom-call(s32[9]{0:T(128)S(1)} %pad_add_fusion.lists_ref, s32[1,128]{1,0:T(1,128)S(1)} %bitcast.12, ...), custom_call_target="tpu_custom_call" | custom-call | flops 1 | bytes 1 | tf_op jit(solution)/shard_map/side_parts/pallas_call | solution.py:231
  19.8 0.7 %collective-permute-start.4 = (bf16[144,1536]{1,0:T(8,128)(2,1)S(1)}, bf16[144,1536]{1,0:T(8,128)(2,1)S(1)}, u32[]{:S(2)}, u32[]{:S(2)}) collective-permute-start(bf16[144,1536]{1,0:T(8,128)(2,1)S(1)} %get-tuple-element.45), channel_id=1, source_target_pairs={{2,4},{4,2},{6,8},{8,6},{10,12},{12,10},{3,5},{5,3},{7,9},{9,7},{1... | collective-permute-start | bytes 1327112 | tf_op jit(solution)/shard_map/ppermute | solution.py:513
  20.5 1.8 %fusion.3.own_ref = f32[256,1536]{1,0:T(8,128)S(1)} fusion(bf16[256,2048]{1,0:T(8,128)(2,1)S(1)} %get-tuple-element.38, bf16[2048,1536]{1,0:T(8,128)(2,1)S(1)} %get-tuple-element.39), kind=kOutput, calls=%fused_computation.6 | convolution fusion | flops 1610612736 | bytes 8912896 | tf_op jit(solution)/shard_map/dot_general | solution.py:172
  22.3 3.4 %collective-permute-start.3 = (bf16[160,1536]{1,0:T(8,128)(2,1)S(1)}, bf16[160,1536]{1,0:T(8,128)(2,1)S(1)}, u32[]{:S(2)}, u32[]{:S(2)}) collective-permute-start(bf16[160,1536]{1,0:T(8,128)(2,1)S(1)} %get-tuple-element.43), channel_id=1, source_target_pairs={{0,2},{2,0},{4,6},{6,4},{8,10},{10,8},{12,14},{14,12},{1,3},{3,1},... | collective-permute-start | bytes 1474568 | tf_op jit(solution)/shard_map/ppermute | solution.py:512
  25.8 2.4 %collective-permute-done.1.cx_ref = s16[1552,128]{1,0:T(8,128)(2,1)S(1)} collective-permute-done((s16[1552,128]{1,0:T(8,128)(2,1)S(1)}, s16[1552,128]{1,0:T(8,128)(2,1)S(1)}, u32[]{:S(2)}, u32[]{:S(2)}) %collective-permute-start.1) | collective-permute-done | bytes 397344 | tf_op jit(solution)/shard_map/ppermute | solution.py:505
  28.2 0.8 %join_qwen.1 = (bf16[128,1664]{1,0:T(8,128)(2,1)S(1)}, f32[128,128]{1,0:T(8,128)S(1)}) custom-call(f32[256,1536]{1,0:T(8,128)S(1)} %fusion.3.own_ref, f32[128,128]{1,0:T(8,128)S(1)} %get-tuple-element.40.squares_ref, s16[1552,128]{1,0:T(8,128)(2,1)S(1)} %collective-permute-done.cy_ref, s16[1552,128]{1,0:T(8,128)(2,1)S(1)} %collective-permute-done.1.cx_ref, ...), custom_call_target="tpu_custom_call" | custom-call | flops 20000000000 | bytes 8388608 | tf_op jit(solution)/shard_map/join_qwen/pallas_call | solution.py:320
  29.0 0.7 %collective-permute-start.10 = (bf16[128,1664]{1,0:T(8,128)(2,1)S(1)}, bf16[128,1664]{1,0:T(8,128)(2,1)S(1)}, u32[]{:S(2)}, u32[]{:S(2)}) collective-permute-start(bf16[128,1664]{1,0:T(8,128)(2,1)S(1)} %get-tuple-element.49.u_ref), channel_id=1, source_target_pairs={{2,4},{4,2},{6,8},{8,6},{10,12},{12,10},{3,5},{5,3},{7,9},{9,7},{1... | collective-permute-start | bytes 1277960 | tf_op jit(solution)/shard_map/ppermute | solution.py:517
  29.8 1.2 %join_llama.1 = (f32[128,1536]{1,0:T(8,128)S(1)}, f32[8,128]{1,0:T(8,128)S(1)}) custom-call(f32[256,1536]{1,0:T(8,128)S(1)} %fusion.3.own_ref, f32[128,128]{1,0:T(8,128)S(1)} %get-tuple-element.40.squares_ref, s16[1552,128]{1,0:T(8,128)(2,1)S(1)} %collective-permute-done.cy_ref, s16[1552,128]{1,0:T(8,128)(2,1)S(1)} %collective-permute-done.1.cx_ref, ...), custom_call_target="tpu_custom_call" | custom-call | flops 20000000000 | bytes 8388608 | tf_op jit(solution)/shard_map/join_llama/pallas_call | solution.py:365
  30.9 3.0 %collective-permute-start.5 = (f32[8,128]{1,0:T(8,128)S(1)}, f32[8,128]{1,0:T(8,128)S(1)}, u32[]{:S(2)}, u32[]{:S(2)}) collective-permute-start(f32[8,128]{1,0:T(8,128)S(1)} %get-tuple-element.47.refs_0_), channel_id=1, source_target_pairs={{0,2},{2,0},{4,6},{6,4},{8,10},{10,8},{12,14},{14,12},{1,3},{3,1},... | collective-permute-start | bytes 12296 | tf_op jit(solution)/shard_map/ppermute | solution.py:475
  33.9 0.8 %collective-permute-done.5.refs_1_ = f32[8,128]{1,0:T(8,128)S(1)} collective-permute-done((f32[8,128]{1,0:T(8,128)S(1)}, f32[8,128]{1,0:T(8,128)S(1)}, u32[]{:S(2)}, u32[]{:S(2)}) %collective-permute-start.5) | collective-permute-done | bytes 4128 | tf_op jit(solution)/shard_map/ppermute | solution.py:475
  35.1 2.1 %collective-permute-start.8 = (f32[16,128]{1,0:T(8,128)S(1)}, f32[16,128]{1,0:T(8,128)S(1)}, u32[]{:S(2)}, u32[]{:S(2)}) collective-permute-start(f32[16,128]{1,0:T(8,128)S(1)} %constant_dynamic-update-slice_fusion), channel_id=1, source_target_pairs={{0,12},{2,14},{4,8},{6,10},{8,4},{10,6},{12,0},{14,2},{1,13},{3,15... | collective-permute-start | bytes 24584 | tf_op jit(solution)/shard_map/ppermute | solution.py:475
  37.1 0.9 %collective-permute-start.7 = (f32[16,128]{1,0:T(8,128)S(1)}, f32[16,128]{1,0:T(8,128)S(1)}, u32[]{:S(2)}, u32[]{:S(2)}) collective-permute-start(f32[16,128]{1,0:T(8,128)S(1)} %constant_dynamic-update-slice_fusion), channel_id=1, source_target_pairs={{0,8},{2,10},{4,12},{6,14},{8,0},{10,2},{12,4},{14,6},{1,9},{3,11}... | collective-permute-start | bytes 24584 | tf_op jit(solution)/shard_map/ppermute | solution.py:475
  38.1 1.3 %collective-permute-start.6 = (f32[16,128]{1,0:T(8,128)S(1)}, f32[16,128]{1,0:T(8,128)S(1)}, u32[]{:S(2)}, u32[]{:S(2)}) collective-permute-start(f32[16,128]{1,0:T(8,128)S(1)} %constant_dynamic-update-slice_fusion), channel_id=1, source_target_pairs={{0,4},{2,6},{4,0},{6,2},{8,12},{10,14},{12,8},{14,10},{1,5},{3,7},... | collective-permute-start | bytes 24584 | tf_op jit(solution)/shard_map/ppermute | solution.py:475
  39.5 1.7 %map_parts.1 = (f32[128,1536]{1,0:T(8,128)S(1)}, f32[128,128]{1,0:T(8,128)S(1)}) custom-call(s32[9]{0:T(128)S(1)} %pad_add_fusion.lists_ref, bf16[128,1664]{1,0:T(8,128)(2,1)S(1)} %get-tuple-element.49.u_ref, bf16[128,1664]{1,0:T(8,128)(2,1)S(1)} %collective-permute-done.9.near_ref, bf16[128,1664]{1,0:T(8,128)(2,1)S(1)} %collective-permute-done.10.far_ref, ...), custom_call_target="tpu_custom_call" | custom-call | flops 268435456 | bytes 2097152 | tf_op jit(solution)/shard_map/map_parts/pallas_call | solution.py:416
  41.1 0.6 %collective-permute-done.7.refs_3_ = f32[16,128]{1,0:T(8,128)S(1)} collective-permute-done((f32[16,128]{1,0:T(8,128)S(1)}, f32[16,128]{1,0:T(8,128)S(1)}, u32[]{:S(2)}, u32[]{:S(2)}) %collective-permute-start.7) | collective-permute-done | bytes 8224 | tf_op jit(solution)/shard_map/ppermute | solution.py:475
  41.8 1.3 %finish.1 = (f32[128,1536]{1,0:T(8,128)}, f32[1,128]{1,0:T(1,128)}) custom-call(f32[8,128]{1,0:T(8,128)S(1)} %get-tuple-element.47.refs_0_, f32[8,128]{1,0:T(8,128)S(1)} %collective-permute-done.5.refs_1_, f32[16,128]{1,0:T(8,128)S(1)} %collective-permute-done.6.refs_2_, f32[16,128]{1,0:T(8,128)S(1)} %collective-permute-done.7.refs_3_, ...), custom_call_target="tpu_custom_call" | custom-call | flops 3932160 | bytes 2359296 | tf_op jit(solution)/shard_map/finish/pallas_call | solution.py:455
  (22 shorter events, 1.1 us)
Async XLA Ops:
  6.3 19.5 %collective-permute-start.2 = (s16[1552,128]{1,0:T(8,128)(2,1)S(1)}, s16[1552,128]{1,0:T(8,128)(2,1)S(1)}, u32[]{:S(2)}, u32[]{:S(2)}) collective-permute-start(s16[1552,128]{1,0:T(8,128)(2,1)S(1)} %encode_parts.3), channel_id=1, source_target_pairs={{0,17},{1,16},{16,1},{17,0},{2,19},{3,18},{18,3},{19,2},{4,21},{5,... | collective-permute-start | bytes 1191944 | tf_op jit(solution)/shard_map/ppermute | solution.py:499
  12.4 15.7 %collective-permute-start = (s16[1552,128]{1,0:T(8,128)(2,1)S(1)}, s16[1552,128]{1,0:T(8,128)(2,1)S(1)}, u32[]{:S(2)}, u32[]{:S(2)}) collective-permute-start(s16[1552,128]{1,0:T(8,128)(2,1)S(1)} %encode_parts.4), channel_id=1, source_target_pairs={{0,1},{1,0},{2,3},{3,2},{4,5},{5,4},{6,7},{7,6},{8,9},{9,8},{10,11... | collective-permute-start | bytes 1191944 | tf_op jit(solution)/shard_map/ppermute | solution.py:502
  13.0 3.0 %copy-start.2 = (s32[4]{0:T(128)S(1)}, s32[4]{0:T(128)}, u32[]{:S(2)}) copy-start(s32[4]{0:T(128)} %param.12) | copy-start | bytes 52
  13.0 3.0 %copy-start.3 = (s32[4]{0:T(128)S(1)}, s32[4]{0:T(128)}, u32[]{:S(2)}) copy-start(s32[4]{0:T(128)} %param.11) | copy-start | bytes 52
  13.0 3.1 %copy-start.1 = (s32[128]{0:T(128)S(1)}, s32[128]{0:T(128)}, u32[]{:S(2)}) copy-start(s32[128]{0:T(128)} %param.15) | copy-start | bytes 1540
  15.3 12.9 %collective-permute-start.1 = (s16[1552,128]{1,0:T(8,128)(2,1)S(1)}, s16[1552,128]{1,0:T(8,128)(2,1)S(1)}, u32[]{:S(2)}, u32[]{:S(2)}) collective-permute-start(s16[1552,128]{1,0:T(8,128)(2,1)S(1)} %encode_parts.5), channel_id=1, source_target_pairs={{0,16},{16,0},{1,17},{17,1},{2,18},{18,2},{3,19},{19,3},{4,20},{20... | collective-permute-start | bytes 1191944 | tf_op jit(solution)/shard_map/ppermute | solution.py:505
  19.8 9.9 %collective-permute-start.4 = (bf16[144,1536]{1,0:T(8,128)(2,1)S(1)}, bf16[144,1536]{1,0:T(8,128)(2,1)S(1)}, u32[]{:S(2)}, u32[]{:S(2)}) collective-permute-start(bf16[144,1536]{1,0:T(8,128)(2,1)S(1)} %get-tuple-element.45), channel_id=1, source_target_pairs={{2,4},{4,2},{6,8},{8,6},{10,12},{12,10},{3,5},{5,3},{7,9},{9,7},{1... | collective-permute-start | bytes 1327112 | tf_op jit(solution)/shard_map/ppermute | solution.py:513
  22.3 7.4 %collective-permute-start.3 = (bf16[160,1536]{1,0:T(8,128)(2,1)S(1)}, bf16[160,1536]{1,0:T(8,128)(2,1)S(1)}, u32[]{:S(2)}, u32[]{:S(2)}) collective-permute-start(bf16[160,1536]{1,0:T(8,128)(2,1)S(1)} %get-tuple-element.43), channel_id=1, source_target_pairs={{0,2},{2,0},{4,6},{6,4},{8,10},{10,8},{12,14},{14,12},{1,3},{3,1},... | collective-permute-start | bytes 1474568 | tf_op jit(solution)/shard_map/ppermute | solution.py:512
  29.0 10.4 %collective-permute-start.10 = (bf16[128,1664]{1,0:T(8,128)(2,1)S(1)}, bf16[128,1664]{1,0:T(8,128)(2,1)S(1)}, u32[]{:S(2)}, u32[]{:S(2)}) collective-permute-start(bf16[128,1664]{1,0:T(8,128)(2,1)S(1)} %get-tuple-element.49.u_ref), channel_id=1, source_target_pairs={{2,4},{4,2},{6,8},{8,6},{10,12},{12,10},{3,5},{5,3},{7,9},{9,7},{1... | collective-permute-start | bytes 1277960 | tf_op jit(solution)/shard_map/ppermute | solution.py:517
  29.8 9.7 %copy-start = (bf16[4,512,512]{2,1,0:T(8,128)(2,1)S(1)}, bf16[4,512,512]{2,1,0:T(8,128)(2,1)}, u32[]{:S(2)}) copy-start(bf16[4,512,512]{2,1,0:T(8,128)(2,1)} %w_ref.3) | copy-start | bytes 6291460
  30.9 3.8 %collective-permute-start.5 = (f32[8,128]{1,0:T(8,128)S(1)}, f32[8,128]{1,0:T(8,128)S(1)}, u32[]{:S(2)}, u32[]{:S(2)}) collective-permute-start(f32[8,128]{1,0:T(8,128)S(1)} %get-tuple-element.47.refs_0_), channel_id=1, source_target_pairs={{0,2},{2,0},{4,6},{6,4},{8,10},{10,8},{12,14},{14,12},{1,3},{3,1},... | collective-permute-start | bytes 12296 | tf_op jit(solution)/shard_map/ppermute | solution.py:475
  34.7 4.7 %collective-permute-start.9 = (bf16[128,1664]{1,0:T(8,128)(2,1)S(1)}, bf16[128,1664]{1,0:T(8,128)(2,1)S(1)}, u32[]{:S(2)}, u32[]{:S(2)}) collective-permute-start(bf16[128,1664]{1,0:T(8,128)(2,1)S(1)} %get-tuple-element.49.u_ref), channel_id=1, source_target_pairs={{0,2},{2,0},{4,6},{6,4},{8,10},{10,8},{12,14},{14,12},{1,3},{3,1},... | collective-permute-start | bytes 1277960 | tf_op jit(solution)/shard_map/ppermute | solution.py:523
  35.1 6.1 %collective-permute-start.8 = (f32[16,128]{1,0:T(8,128)S(1)}, f32[16,128]{1,0:T(8,128)S(1)}, u32[]{:S(2)}, u32[]{:S(2)}) collective-permute-start(f32[16,128]{1,0:T(8,128)S(1)} %constant_dynamic-update-slice_fusion), channel_id=1, source_target_pairs={{0,12},{2,14},{4,8},{6,10},{8,4},{10,6},{12,0},{14,2},{1,13},{3,15... | collective-permute-start | bytes 24584 | tf_op jit(solution)/shard_map/ppermute | solution.py:475
  37.1 4.5 %collective-permute-start.7 = (f32[16,128]{1,0:T(8,128)S(1)}, f32[16,128]{1,0:T(8,128)S(1)}, u32[]{:S(2)}, u32[]{:S(2)}) collective-permute-start(f32[16,128]{1,0:T(8,128)S(1)} %constant_dynamic-update-slice_fusion), channel_id=1, source_target_pairs={{0,8},{2,10},{4,12},{6,14},{8,0},{10,2},{12,4},{14,6},{1,9},{3,11}... | collective-permute-start | bytes 24584 | tf_op jit(solution)/shard_map/ppermute | solution.py:475
  38.1 3.7 %collective-permute-start.6 = (f32[16,128]{1,0:T(8,128)S(1)}, f32[16,128]{1,0:T(8,128)S(1)}, u32[]{:S(2)}, u32[]{:S(2)}) collective-permute-start(f32[16,128]{1,0:T(8,128)S(1)} %constant_dynamic-update-slice_fusion), channel_id=1, source_target_pairs={{0,4},{2,6},{4,0},{6,2},{8,12},{10,14},{12,8},{14,10},{1,5},{3,7},... | collective-permute-start | bytes 24584 | tf_op jit(solution)/shard_map/ppermute | solution.py:475

commit v8 on v7

--- a/solution.py
+++ b/solution.py
@@ -305,12 +305,16 @@
     for j in range(blocks):
         at = pl.ds(j * width, width)
         qwen = jnp.exp(q_ref[:, at] - peak)
-        u_ref[:, at] = qwen.astype(bf16)
+        held = qwen.astype(bf16)
+        for k in range(width // LANES):
+            slab = j * (width // LANES) + k
+            u_ref[pl.ds(slab * rows, rows), :] = held[:, k * LANES : (k + 1) * LANES]
         total += jnp.sum(qwen, axis=1, keepdims=True)
     first = peak.astype(bf16).astype(f32)
     second = (peak - first).astype(bf16).astype(f32)
     third = peak - first - second
-    u_ref[:, body:] = columns_to_lanes([first, second, third], rows).astype(bf16)
+    parts = jnp.transpose(columns_to_lanes([first, second, third], rows))[:EXTRA]
+    u_ref[pl.ds(body // LANES * rows, EXTRA), :] = parts.astype(bf16)
     stats_ref[...] = columns_to_lanes([peak, total], rows)
 
 
@@ -321,7 +325,7 @@
         functools.partial(qwen_kernel, width, cols // width, features),
         in_specs=[whole] * 5,
         out_shape=[
-            jax.ShapeDtypeStruct((rows, cols + LANES), bf16),
+            jax.ShapeDtypeStruct((cols // LANES * rows + EXTRA, LANES), bf16),
             jax.ShapeDtypeStruct((rows, LANES), f32),
         ],
         scratch_shapes=[pltpu.VMEM((rows, cols), f32)],
@@ -349,7 +353,8 @@
         total += jnp.sum(llama, axis=1, keepdims=True)
         hit = lax.broadcasted_iota(i32, (rows, width), 1) + j * width == token
         pick_e += jnp.sum(jnp.where(hit, llama, 0.0), axis=1, keepdims=True)
-        held = u_ref[:, at].astype(f32)
+        slabs = range(j * (width // LANES), (j + 1) * (width // LANES))
+        held = jnp.concatenate([u_ref[pl.ds(slab * rows, rows), :] for slab in slabs], axis=1).astype(f32)
         columns = functools.reduce(jnp.add, [ref[pl.ds(0, rows), at].astype(f32) for ref in columns_refs])
         pick_m += jnp.sum(held * columns, axis=1, keepdims=True)
         sums = functools.reduce(jnp.add, [ref[pl.ds(rows, EXTRA), at].astype(f32) for ref in columns_refs])
@@ -373,7 +378,7 @@
 
 
 def map_kernel(width, blocks, shards, lists_ref, u_ref, near_ref, far_ref, w_ref, m_ref, top_ref, all_ref, scale_ref, meta_ref, meta_sem):
-    rows = u_ref.shape[0]
+    rows = m_ref.shape[0]
     body = blocks * width
     meta_copy = pltpu.make_async_copy(lists_ref, meta_ref, meta_sem)
     meta_copy.start()
@@ -382,7 +387,7 @@
     near_at = jnp.where(shard % 2 == 0, 2, 0)
 
     def peak_of(ref):
-        lanes = ref[:, body:].astype(f32)
+        lanes = jnp.transpose(ref[pl.ds(body // LANES * rows, EXTRA), :].astype(f32))
         return lanes[:, 0:1] + lanes[:, 1:2] + lanes[:, 2:3]
 
     own_peak = peak_of(u_ref)
@@ -390,7 +395,8 @@
     far_peak = jnp.where((shard > 0) & (shard < shards - 1), peak_of(far_ref), own_peak)
     top = jnp.maximum(jnp.maximum(near_peak, far_peak), own_peak)
     for k, ref, peak in ((near_at, near_ref, near_peak), (1, u_ref, own_peak), (2 - near_at, far_ref, far_peak)):
-        all_ref[k] = ref[:, :body]
+        for slab in range(body // LANES):
+            all_ref[k, :, pl.ds(slab * LANES, LANES)] = ref[pl.ds(slab * rows, rows), :]
         scale_ref[k] = jnp.broadcast_to(jnp.exp(peak - top), (rows, LANES))
     m_ref[...] = jnp.zeros_like(m_ref)
     meta_copy.wait()
@@ -409,8 +415,8 @@
     top_ref[...] = jnp.broadcast_to(top, (rows, LANES))
 
 
-def map_parts(lists, u, near, far, weights, width, shards):
-    rows, cols = u.shape[0], u.shape[1] - LANES
+def map_parts(lists, u, near, far, weights, width, shards, rows):
+    cols = (u.shape[0] - EXTRA) // rows * LANES
     blocks = cols // width
     whole = pl.BlockSpec(memory_space=pltpu.VMEM)
     return pl.pallas_call(
@@ -521,7 +527,7 @@
     pieces, last = gather_pieces(stats, shards)
     late_u, _ = lax.optimization_barrier((u, last))
     near = lax.ppermute(late_u, "vocab", inside)
-    m, m_top = map_parts(lists, u, near, far, pair_weight, width, shards)
+    m, m_top = map_parts(lists, u, near, far, pair_weight, width, shards, e.shape[0])
     out, nll = finish(pieces, e, m, m_top)
     return out, nll[0]
 

time: 43.4 us -> 43.3 us (level)
  transfers between devices with their start and end apart: 11 -> 11, of which waited for: 4 -> 4; matrix products, arithmetic and copies ran while one was open for 13% -> 13% of each run, Pallas kernels for 19% -> 20%
where the time goes in v8:
time: 43.3 us; the launch traced here: 43.1 us
  starting transfers between devices  17.1 us (39%)
  Pallas kernels  13.6 us (31%)
  matrix products  7.11 us (16%)
  waiting for transfers between devices  3.8 us (9%)
  between operations  1.41 us (3%)
    ppermute x4, starting transfers between devices, gather_pieces(): lax.ppermute(sent, 'vocab', [(i, i ^ turn * step) for i in range(shards)])  7.34 us
    dot_general x4, matrix products, product(): return jnp.dot(left, head, preferred_element_type=f32)  7.11 us
    ppermute x1, starting transfers between devices, on_device(): lax.ppermute(to_d, ('mp', 'rows'), [(0, 3), (1, 2), (2, 1), (3, 0)])  3.93 us
    pallas_call x1, Pallas kernels, side_parts(): pl.pallas_call(functools.partial(side_kernel, width, cols // width), in_s...  3.7 us
    ppermute x1, starting transfers between devices, on_device(): near_columns = lax.ppermute(to_near, 'vocab', inside)  3.44 us
    pallas_call x1, Pallas kernels, first_prep(): pl.pallas_call(functools.partial(first_kernel, kinds, rows), in_specs=[hb...  3.35 us
    ppermute x1, waiting for transfers between devices, on_device(): from_x = lax.ppermute(to_x, 'mp', [(0, 1), (1, 0)])  2.43 us
    pallas_call x1, Pallas kernels, map_parts(): pl.pallas_call(functools.partial(map_kernel, width, blocks, shards), in_s...  1.78 us
  transfers between devices with their start and end apart: 11, of which 4 were waited for; matrix products, arithmetic and copies ran while one was open for 13% of the time, Pallas kernels for 20%

profile of v8, /device:TPU:0, one launch (start us, length us, event | category | flops | bytes accessed | tf_op | source)
XLA Modules:
  0.0 43.1 jit_solution(13405224716402582271)
XLA Ops:
  0.6 3.4 %first_prep.1 = (bf16[256,2048]{1,0:T(8,128)(2,1)S(1)}, bf16[256,2048]{1,0:T(8,128)(2,1)S(1)}, bf16[256,2048]{1,0:T(8,128)(2,1)S(1)}, f32[128,128]{1,0:T(8,128)S...) custom-call(bf16[512,2048]{1,0:T(8,128)(2,1)} %bitcast.16, ...), custom_call_target="tpu_custom_call" | custom-call | flops 6291456 | bytes 6291456 | tf_op jit(solution)/shard_map/first_prep/pallas_call | solution.py:124
  4.0 1.8 %fusion.both_ref = f32[256,1536]{1,0:T(8,128)S(1)} fusion(bf16[256,2048]{1,0:T(8,128)(2,1)S(1)} %get-tuple-element.30, bf16[2048,1536]{1,0:T(8,128)(2,1)S(1)} %get-tuple-element.31), kind=kOutput, calls=%fused_computation.3 | convolution fusion | flops 1610612736 | bytes 8912896 | tf_op jit(solution)/shard_map/dot_general | solution.py:172
  5.8 0.5 %encode_parts.3 = s16[1552,128]{1,0:T(8,128)(2,1)S(1)} custom-call(f32[256,1536]{1,0:T(8,128)S(1)} %fusion.both_ref, f32[128,128]{1,0:T(8,128)S(1)} %get-tuple-element.32.refs_0_), custom_call_target="tpu_custom_call" | custom-call | flops 3932160 | bytes 1966080 | tf_op jit(solution)/shard_map/encode_parts/pallas_call | solution.py:160
  6.3 3.9 %collective-permute-start.2 = (s16[1552,128]{1,0:T(8,128)(2,1)S(1)}, s16[1552,128]{1,0:T(8,128)(2,1)S(1)}, u32[]{:S(2)}, u32[]{:S(2)}) collective-permute-start(s16[1552,128]{1,0:T(8,128)(2,1)S(1)} %encode_parts.3), channel_id=1, source_target_pairs={{0,17},{1,16},{16,1},{17,0},{2,19},{3,18},{18,3},{19,2},{4,21},{5,... | collective-permute-start | bytes 1191944 | tf_op jit(solution)/shard_map/ppermute | solution.py:505
  10.2 1.8 %fusion.1.both_ref = f32[256,1536]{1,0:T(8,128)S(1)} fusion(bf16[256,2048]{1,0:T(8,128)(2,1)S(1)} %get-tuple-element.33, bf16[2048,1536]{1,0:T(8,128)(2,1)S(1)} %get-tuple-element.31), kind=kOutput, calls=%fused_computation.4 | convolution fusion | flops 1610612736 | bytes 8912896 | tf_op jit(solution)/shard_map/dot_general | solution.py:172
  12.0 0.5 %encode_parts.4 = s16[1552,128]{1,0:T(8,128)(2,1)S(1)} custom-call(f32[256,1536]{1,0:T(8,128)S(1)} %fusion.1.both_ref, f32[128,128]{1,0:T(8,128)S(1)} %get-tuple-element.34.refs_0_), custom_call_target="tpu_custom_call" | custom-call | flops 3932160 | bytes 1966080 | tf_op jit(solution)/shard_map/encode_parts/pallas_call | solution.py:160
  12.4 0.5 %collective-permute-start = (s16[1552,128]{1,0:T(8,128)(2,1)S(1)}, s16[1552,128]{1,0:T(8,128)(2,1)S(1)}, u32[]{:S(2)}, u32[]{:S(2)}) collective-permute-start(s16[1552,128]{1,0:T(8,128)(2,1)S(1)} %encode_parts.4), channel_id=1, source_target_pairs={{0,1},{1,0},{2,3},{3,2},{4,5},{5,4},{6,7},{7,6},{8,9},{9,8},{10,11... | collective-permute-start | bytes 1191944 | tf_op jit(solution)/shard_map/ppermute | solution.py:508
  13.0 1.8 %fusion.2.both_ref = f32[256,1536]{1,0:T(8,128)S(1)} fusion(bf16[256,2048]{1,0:T(8,128)(2,1)S(1)} %get-tuple-element.35, bf16[2048,1536]{1,0:T(8,128)(2,1)S(1)} %get-tuple-element.31), kind=kOutput, calls=%fused_computation.5 | convolution fusion | flops 1610612736 | bytes 8912896 | tf_op jit(solution)/shard_map/dot_general | solution.py:172
  14.8 0.5 %encode_parts.5 = s16[1552,128]{1,0:T(8,128)(2,1)S(1)} custom-call(f32[256,1536]{1,0:T(8,128)S(1)} %fusion.2.both_ref, f32[128,128]{1,0:T(8,128)S(1)} %get-tuple-element.36.refs_0_), custom_call_target="tpu_custom_call" | custom-call | flops 3932160 | bytes 1966080 | tf_op jit(solution)/shard_map/encode_parts/pallas_call | solution.py:160
  16.1 3.7 %side_parts.1 = (bf16[160,1536]{1,0:T(8,128)(2,1)S(1)}, bf16[144,1536]{1,0:T(8,128)(2,1)S(1)}, bf16[144,1536]{1,0:T(8,128)(2,1)S(1)}, bf16[256,2048]{1,0:T(8,128...) custom-call(s32[9]{0:T(128)S(1)} %pad_add_fusion.lists_ref, s32[1,128]{1,0:T(1,128)S(1)} %bitcast.12, ...), custom_call_target="tpu_custom_call" | custom-call | flops 1 | bytes 1 | tf_op jit(solution)/shard_map/side_parts/pallas_call | solution.py:231
  19.8 0.7 %collective-permute-start.4 = (bf16[144,1536]{1,0:T(8,128)(2,1)S(1)}, bf16[144,1536]{1,0:T(8,128)(2,1)S(1)}, u32[]{:S(2)}, u32[]{:S(2)}) collective-permute-start(bf16[144,1536]{1,0:T(8,128)(2,1)S(1)} %get-tuple-element.45), channel_id=1, source_target_pairs={{2,4},{4,2},{6,8},{8,6},{10,12},{12,10},{3,5},{5,3},{7,9},{9,7},{1... | collective-permute-start | bytes 1327112 | tf_op jit(solution)/shard_map/ppermute | solution.py:519
  20.5 1.8 %fusion.3.own_ref = f32[256,1536]{1,0:T(8,128)S(1)} fusion(bf16[256,2048]{1,0:T(8,128)(2,1)S(1)} %get-tuple-element.38, bf16[2048,1536]{1,0:T(8,128)(2,1)S(1)} %get-tuple-element.39), kind=kOutput, calls=%fused_computation.6 | convolution fusion | flops 1610612736 | bytes 8912896 | tf_op jit(solution)/shard_map/dot_general | solution.py:172
  22.3 3.4 %collective-permute-start.3 = (bf16[160,1536]{1,0:T(8,128)(2,1)S(1)}, bf16[160,1536]{1,0:T(8,128)(2,1)S(1)}, u32[]{:S(2)}, u32[]{:S(2)}) collective-permute-start(bf16[160,1536]{1,0:T(8,128)(2,1)S(1)} %get-tuple-element.43), channel_id=1, source_target_pairs={{0,2},{2,0},{4,6},{6,4},{8,10},{10,8},{12,14},{14,12},{1,3},{3,1},... | collective-permute-start | bytes 1474568 | tf_op jit(solution)/shard_map/ppermute | solution.py:518
  25.8 2.4 %collective-permute-done.1.cx_ref = s16[1552,128]{1,0:T(8,128)(2,1)S(1)} collective-permute-done((s16[1552,128]{1,0:T(8,128)(2,1)S(1)}, s16[1552,128]{1,0:T(8,128)(2,1)S(1)}, u32[]{:S(2)}, u32[]{:S(2)}) %collective-permute-start.1) | collective-permute-done | bytes 397344 | tf_op jit(solution)/shard_map/ppermute | solution.py:511
  28.2 0.8 %join_qwen.1 = (bf16[1552,128]{1,0:T(8,128)(2,1)S(1)}, f32[128,128]{1,0:T(8,128)S(1)}) custom-call(f32[256,1536]{1,0:T(8,128)S(1)} %fusion.3.own_ref, f32[128,128]{1,0:T(8,128)S(1)} %get-tuple-element.40.squares_ref, s16[1552,128]{1,0:T(8,128)(2,1)S(1)} %collective-permute-done.cy_ref, s16[1552,128]{1,0:T(8,128)(2,1)S(1)} %collective-permute-done.1.cx_ref, ...), custom_call_target="tpu_custom_call" | custom-call | flops 20000000000 | bytes 8388608 | tf_op jit(solution)/shard_map/join_qwen/pallas_call | solution.py:324
  29.0 0.7 %collective-permute-start.10 = (bf16[1552,128]{1,0:T(8,128)(2,1)S(1)}, bf16[1552,128]{1,0:T(8,128)(2,1)S(1)}, u32[]{:S(2)}, u32[]{:S(2)}) collective-permute-start(bf16[1552,128]{1,0:T(8,128)(2,1)S(1)} %get-tuple-element.49.u_ref), channel_id=1, source_target_pairs={{2,4},{4,2},{6,8},{8,6},{10,12},{12,10},{3,5},{5,3},{7,9},{9,7},{1... | collective-permute-start | bytes 1191944 | tf_op jit(solution)/shard_map/ppermute | solution.py:523
  29.7 1.2 %join_llama.1 = (f32[128,1536]{1,0:T(8,128)S(1)}, f32[8,128]{1,0:T(8,128)S(1)}) custom-call(f32[256,1536]{1,0:T(8,128)S(1)} %fusion.3.own_ref, f32[128,128]{1,0:T(8,128)S(1)} %get-tuple-element.40.squares_ref, s16[1552,128]{1,0:T(8,128)(2,1)S(1)} %collective-permute-done.cy_ref, s16[1552,128]{1,0:T(8,128)(2,1)S(1)} %collective-permute-done.1.cx_ref, ...), custom_call_target="tpu_custom_call" | custom-call | flops 20000000000 | bytes 8388608 | tf_op jit(solution)/shard_map/join_llama/pallas_call | solution.py:370
  30.9 3.0 %collective-permute-start.5 = (f32[8,128]{1,0:T(8,128)S(1)}, f32[8,128]{1,0:T(8,128)S(1)}, u32[]{:S(2)}, u32[]{:S(2)}) collective-permute-start(f32[8,128]{1,0:T(8,128)S(1)} %get-tuple-element.47.refs_0_), channel_id=1, source_target_pairs={{0,2},{2,0},{4,6},{6,4},{8,10},{10,8},{12,14},{14,12},{1,3},{3,1},... | collective-permute-start | bytes 12296 | tf_op jit(solution)/shard_map/ppermute | solution.py:481
  33.9 0.8 %collective-permute-done.5.refs_1_ = f32[8,128]{1,0:T(8,128)S(1)} collective-permute-done((f32[8,128]{1,0:T(8,128)S(1)}, f32[8,128]{1,0:T(8,128)S(1)}, u32[]{:S(2)}, u32[]{:S(2)}) %collective-permute-start.5) | collective-permute-done | bytes 4128 | tf_op jit(solution)/shard_map/ppermute | solution.py:481
  35.0 2.1 %collective-permute-start.8 = (f32[16,128]{1,0:T(8,128)S(1)}, f32[16,128]{1,0:T(8,128)S(1)}, u32[]{:S(2)}, u32[]{:S(2)}) collective-permute-start(f32[16,128]{1,0:T(8,128)S(1)} %constant_dynamic-update-slice_fusion), channel_id=1, source_target_pairs={{0,12},{2,14},{4,8},{6,10},{8,4},{10,6},{12,0},{14,2},{1,13},{3,15... | collective-permute-start | bytes 24584 | tf_op jit(solution)/shard_map/ppermute | solution.py:481
  37.1 0.9 %collective-permute-start.7 = (f32[16,128]{1,0:T(8,128)S(1)}, f32[16,128]{1,0:T(8,128)S(1)}, u32[]{:S(2)}, u32[]{:S(2)}) collective-permute-start(f32[16,128]{1,0:T(8,128)S(1)} %constant_dynamic-update-slice_fusion), channel_id=1, source_target_pairs={{0,8},{2,10},{4,12},{6,14},{8,0},{10,2},{12,4},{14,6},{1,9},{3,11}... | collective-permute-start | bytes 24584 | tf_op jit(solution)/shard_map/ppermute | solution.py:481
  38.1 1.3 %collective-permute-start.6 = (f32[16,128]{1,0:T(8,128)S(1)}, f32[16,128]{1,0:T(8,128)S(1)}, u32[]{:S(2)}, u32[]{:S(2)}) collective-permute-start(f32[16,128]{1,0:T(8,128)S(1)} %constant_dynamic-update-slice_fusion), channel_id=1, source_target_pairs={{0,4},{2,6},{4,0},{6,2},{8,12},{10,14},{12,8},{14,10},{1,5},{3,7},... | collective-permute-start | bytes 24584 | tf_op jit(solution)/shard_map/ppermute | solution.py:481
  39.4 1.8 %map_parts.1 = (f32[128,1536]{1,0:T(8,128)S(1)}, f32[128,128]{1,0:T(8,128)S(1)}) custom-call(s32[9]{0:T(128)S(1)} %pad_add_fusion.lists_ref, bf16[1552,128]{1,0:T(8,128)(2,1)S(1)} %get-tuple-element.49.u_ref, bf16[1552,128]{1,0:T(8,128)(2,1)S(1)} %collective-permute-done.9.near_ref, bf16[1552,128]{1,0:T(8,128)(2,1)S(1)} %collective-permute-done.10.far_ref, ...), custom_call_target="tpu_custom_call" | custom-call | flops 268435456 | bytes 2097152 | tf_op jit(solution)/shard_map/map_parts/pallas_call | solution.py:422
  41.8 1.3 %finish.1 = (f32[128,1536]{1,0:T(8,128)}, f32[1,128]{1,0:T(1,128)}) custom-call(f32[8,128]{1,0:T(8,128)S(1)} %get-tuple-element.47.refs_0_, f32[8,128]{1,0:T(8,128)S(1)} %collective-permute-done.5.refs_1_, f32[16,128]{1,0:T(8,128)S(1)} %collective-permute-done.6.refs_2_, f32[16,128]{1,0:T(8,128)S(1)} %collective-permute-done.7.refs_3_, ...), custom_call_target="tpu_custom_call" | custom-call | flops 3932160 | bytes 2359296 | tf_op jit(solution)/shard_map/finish/pallas_call | solution.py:461
  (22 shorter events, 1.1 us)
Async XLA Ops:
  6.3 19.5 %collective-permute-start.2 = (s16[1552,128]{1,0:T(8,128)(2,1)S(1)}, s16[1552,128]{1,0:T(8,128)(2,1)S(1)}, u32[]{:S(2)}, u32[]{:S(2)}) collective-permute-start(s16[1552,128]{1,0:T(8,128)(2,1)S(1)} %encode_parts.3), channel_id=1, source_target_pairs={{0,17},{1,16},{16,1},{17,0},{2,19},{3,18},{18,3},{19,2},{4,21},{5,... | collective-permute-start | bytes 1191944 | tf_op jit(solution)/shard_map/ppermute | solution.py:505
  12.4 15.7 %collective-permute-start = (s16[1552,128]{1,0:T(8,128)(2,1)S(1)}, s16[1552,128]{1,0:T(8,128)(2,1)S(1)}, u32[]{:S(2)}, u32[]{:S(2)}) collective-permute-start(s16[1552,128]{1,0:T(8,128)(2,1)S(1)} %encode_parts.4), channel_id=1, source_target_pairs={{0,1},{1,0},{2,3},{3,2},{4,5},{5,4},{6,7},{7,6},{8,9},{9,8},{10,11... | collective-permute-start | bytes 1191944 | tf_op jit(solution)/shard_map/ppermute | solution.py:508
  13.0 3.0 %copy-start.2 = (s32[4]{0:T(128)S(1)}, s32[4]{0:T(128)}, u32[]{:S(2)}) copy-start(s32[4]{0:T(128)} %param.12) | copy-start | bytes 52
  13.0 3.0 %copy-start.3 = (s32[4]{0:T(128)S(1)}, s32[4]{0:T(128)}, u32[]{:S(2)}) copy-start(s32[4]{0:T(128)} %param.11) | copy-start | bytes 52
  13.0 3.1 %copy-start.1 = (s32[128]{0:T(128)S(1)}, s32[128]{0:T(128)}, u32[]{:S(2)}) copy-start(s32[128]{0:T(128)} %param.15) | copy-start | bytes 1540
  15.3 12.9 %collective-permute-start.1 = (s16[1552,128]{1,0:T(8,128)(2,1)S(1)}, s16[1552,128]{1,0:T(8,128)(2,1)S(1)}, u32[]{:S(2)}, u32[]{:S(2)}) collective-permute-start(s16[1552,128]{1,0:T(8,128)(2,1)S(1)} %encode_parts.5), channel_id=1, source_target_pairs={{0,16},{16,0},{1,17},{17,1},{2,18},{18,2},{3,19},{19,3},{4,20},{20... | collective-permute-start | bytes 1191944 | tf_op jit(solution)/shard_map/ppermute | solution.py:511
  19.8 9.9 %collective-permute-start.4 = (bf16[144,1536]{1,0:T(8,128)(2,1)S(1)}, bf16[144,1536]{1,0:T(8,128)(2,1)S(1)}, u32[]{:S(2)}, u32[]{:S(2)}) collective-permute-start(bf16[144,1536]{1,0:T(8,128)(2,1)S(1)} %get-tuple-element.45), channel_id=1, source_target_pairs={{2,4},{4,2},{6,8},{8,6},{10,12},{12,10},{3,5},{5,3},{7,9},{9,7},{1... | collective-permute-start | bytes 1327112 | tf_op jit(solution)/shard_map/ppermute | solution.py:519
  22.3 7.4 %collective-permute-start.3 = (bf16[160,1536]{1,0:T(8,128)(2,1)S(1)}, bf16[160,1536]{1,0:T(8,128)(2,1)S(1)}, u32[]{:S(2)}, u32[]{:S(2)}) collective-permute-start(bf16[160,1536]{1,0:T(8,128)(2,1)S(1)} %get-tuple-element.43), channel_id=1, source_target_pairs={{0,2},{2,0},{4,6},{6,4},{8,10},{10,8},{12,14},{14,12},{1,3},{3,1},... | collective-permute-start | bytes 1474568 | tf_op jit(solution)/shard_map/ppermute | solution.py:518
  29.0 10.4 %collective-permute-start.10 = (bf16[1552,128]{1,0:T(8,128)(2,1)S(1)}, bf16[1552,128]{1,0:T(8,128)(2,1)S(1)}, u32[]{:S(2)}, u32[]{:S(2)}) collective-permute-start(bf16[1552,128]{1,0:T(8,128)(2,1)S(1)} %get-tuple-element.49.u_ref), channel_id=1, source_target_pairs={{2,4},{4,2},{6,8},{8,6},{10,12},{12,10},{3,5},{5,3},{7,9},{9,7},{1... | collective-permute-start | bytes 1191944 | tf_op jit(solution)/shard_map/ppermute | solution.py:523
  29.7 9.7 %copy-start = (bf16[4,512,512]{2,1,0:T(8,128)(2,1)S(1)}, bf16[4,512,512]{2,1,0:T(8,128)(2,1)}, u32[]{:S(2)}) copy-start(bf16[4,512,512]{2,1,0:T(8,128)(2,1)} %w_ref.3) | copy-start | bytes 6291460
  30.9 3.8 %collective-permute-start.5 = (f32[8,128]{1,0:T(8,128)S(1)}, f32[8,128]{1,0:T(8,128)S(1)}, u32[]{:S(2)}, u32[]{:S(2)}) collective-permute-start(f32[8,128]{1,0:T(8,128)S(1)} %get-tuple-element.47.refs_0_), channel_id=1, source_target_pairs={{0,2},{2,0},{4,6},{6,4},{8,10},{10,8},{12,14},{14,12},{1,3},{3,1},... | collective-permute-start | bytes 12296 | tf_op jit(solution)/shard_map/ppermute | solution.py:481
  34.7 4.7 %collective-permute-start.9 = (bf16[1552,128]{1,0:T(8,128)(2,1)S(1)}, bf16[1552,128]{1,0:T(8,128)(2,1)S(1)}, u32[]{:S(2)}, u32[]{:S(2)}) collective-permute-start(bf16[1552,128]{1,0:T(8,128)(2,1)S(1)} %get-tuple-element.49.u_ref), channel_id=1, source_target_pairs={{0,2},{2,0},{4,6},{6,4},{8,10},{10,8},{12,14},{14,12},{1,3},{3,1},... | collective-permute-start | bytes 1191944 | tf_op jit(solution)/shard_map/ppermute | solution.py:529
  35.0 6.2 %collective-permute-start.8 = (f32[16,128]{1,0:T(8,128)S(1)}, f32[16,128]{1,0:T(8,128)S(1)}, u32[]{:S(2)}, u32[]{:S(2)}) collective-permute-start(f32[16,128]{1,0:T(8,128)S(1)} %constant_dynamic-update-slice_fusion), channel_id=1, source_target_pairs={{0,12},{2,14},{4,8},{6,10},{8,4},{10,6},{12,0},{14,2},{1,13},{3,15... | collective-permute-start | bytes 24584 | tf_op jit(solution)/shard_map/ppermute | solution.py:481
  37.1 4.5 %collective-permute-start.7 = (f32[16,128]{1,0:T(8,128)S(1)}, f32[16,128]{1,0:T(8,128)S(1)}, u32[]{:S(2)}, u32[]{:S(2)}) collective-permute-start(f32[16,128]{1,0:T(8,128)S(1)} %constant_dynamic-update-slice_fusion), channel_id=1, source_target_pairs={{0,8},{2,10},{4,12},{6,14},{8,0},{10,2},{12,4},{14,6},{1,9},{3,11}... | collective-permute-start | bytes 24584 | tf_op jit(solution)/shard_map/ppermute | solution.py:481
  38.1 3.7 %collective-permute-start.6 = (f32[16,128]{1,0:T(8,128)S(1)}, f32[16,128]{1,0:T(8,128)S(1)}, u32[]{:S(2)}, u32[]{:S(2)}) collective-permute-start(f32[16,128]{1,0:T(8,128)S(1)} %constant_dynamic-update-slice_fusion), channel_id=1, source_target_pairs={{0,4},{2,6},{4,0},{6,2},{8,12},{10,14},{12,8},{14,10},{1,5},{3,7},... | collective-permute-start | bytes 24584 | tf_op jit(solution)/shard_map/ppermute | solution.py:481

commit v9 on v8

--- a/solution.py
+++ b/solution.py
@@ -477,7 +477,7 @@
     while step < shards:
         radix = 4 if step > 1 and 4 * step <= shards else 2
         sent = pieces[0] if len(pieces) == 1 else jnp.concatenate(pieces, axis=0)
-        for turn in range(1, radix):
+        for turn in (1, 3, 2)[: radix - 1] if radix == 4 else (1,):
             pieces.append(lax.ppermute(sent, "vocab", [(i, i ^ (turn * step)) for i in range(shards)]))
         step *= radix
     return pieces, sent

time: 43.3 us -> 44.6 us (1.030)
  waiting for transfers between devices: 3.8 us -> 5.33 us
  starting transfers between devices: 17.1 us -> 16.6 us
    ppermute x4, waiting for transfers between devices: 1.36 us -> 2.88 us  [gather_pieces(): lax.ppermute(sent, 'vocab', [(i, i ^ turn * step) for i in range(shards)])]
    ppermute x4, starting transfers between devices: 7.34 us -> 6.89 us  [gather_pieces(): lax.ppermute(sent, 'vocab', [(i, i ^ turn * step) for i in range(shards)])]
  transfers between devices with their start and end apart: 11 -> 11, of which waited for: 4 -> 3; matrix products, arithmetic and copies ran while one was open for 13% -> 12% of each run, Pallas kernels for 20% -> 19%
where the time goes in v9:
time: 44.6 us; the launch traced here: 44.4 us
  starting transfers between devices  16.6 us (37%)
  Pallas kernels  13.8 us (31%)
  matrix products  7.11 us (16%)
  waiting for transfers between devices  5.33 us (12%)
  between operations  1.42 us (3%)
    dot_general x4, matrix products, product(): return jnp.dot(left, head, preferred_element_type=f32)  7.11 us
    ppermute x4, starting transfers between devices, gather_pieces(): lax.ppermute(sent, 'vocab', [(i, i ^ turn * step) for i in range(shards)])  6.89 us
    ppermute x1, starting transfers between devices, on_device(): lax.ppermute(to_d, ('mp', 'rows'), [(0, 3), (1, 2), (2, 1), (3, 0)])  3.93 us
    pallas_call x1, Pallas kernels, side_parts(): pl.pallas_call(functools.partial(side_kernel, width, cols // width), in_s...  3.7 us
    ppermute x1, starting transfers between devices, on_device(): near_columns = lax.ppermute(to_near, 'vocab', inside)  3.44 us
    pallas_call x1, Pallas kernels, first_prep(): pl.pallas_call(functools.partial(first_kernel, kinds, rows), in_specs=[hb...  3.35 us
    ppermute x4, waiting for transfers between devices, gather_pieces(): lax.ppermute(sent, 'vocab', [(i, i ^ turn * step) for i in range(shards)])  2.88 us
    ppermute x1, waiting for transfers between devices, on_device(): from_x = lax.ppermute(to_x, 'mp', [(0, 1), (1, 0)])  2.43 us
  transfers between devices with their start and end apart: 11, of which 3 were waited for; matrix products, arithmetic and copies ran while one was open for 12% of the time, Pallas kernels for 19%

profile of v9, /device:TPU:0, one launch (start us, length us, event | category | flops | bytes accessed | tf_op | source)
XLA Modules:
  0.0 44.4 jit_solution(8624093396085846672)
XLA Ops:
  0.6 3.4 %first_prep.1 = (bf16[256,2048]{1,0:T(8,128)(2,1)S(1)}, bf16[256,2048]{1,0:T(8,128)(2,1)S(1)}, bf16[256,2048]{1,0:T(8,128)(2,1)S(1)}, f32[128,128]{1,0:T(8,128)S...) custom-call(bf16[512,2048]{1,0:T(8,128)(2,1)} %bitcast.16, ...), custom_call_target="tpu_custom_call" | custom-call | flops 6291456 | bytes 6291456 | tf_op jit(solution)/shard_map/first_prep/pallas_call | solution.py:124
  4.0 1.8 %fusion.both_ref = f32[256,1536]{1,0:T(8,128)S(1)} fusion(bf16[256,2048]{1,0:T(8,128)(2,1)S(1)} %get-tuple-element.30, bf16[2048,1536]{1,0:T(8,128)(2,1)S(1)} %get-tuple-element.31), kind=kOutput, calls=%fused_computation.3 | convolution fusion | flops 1610612736 | bytes 8912896 | tf_op jit(solution)/shard_map/dot_general | solution.py:172
  5.8 0.5 %encode_parts.3 = s16[1552,128]{1,0:T(8,128)(2,1)S(1)} custom-call(f32[256,1536]{1,0:T(8,128)S(1)} %fusion.both_ref, f32[128,128]{1,0:T(8,128)S(1)} %get-tuple-element.32.refs_0_), custom_call_target="tpu_custom_call" | custom-call | flops 3932160 | bytes 1966080 | tf_op jit(solution)/shard_map/encode_parts/pallas_call | solution.py:160
  6.3 3.9 %collective-permute-start.2 = (s16[1552,128]{1,0:T(8,128)(2,1)S(1)}, s16[1552,128]{1,0:T(8,128)(2,1)S(1)}, u32[]{:S(2)}, u32[]{:S(2)}) collective-permute-start(s16[1552,128]{1,0:T(8,128)(2,1)S(1)} %encode_parts.3), channel_id=1, source_target_pairs={{0,17},{1,16},{16,1},{17,0},{2,19},{3,18},{18,3},{19,2},{4,21},{5,... | collective-permute-start | bytes 1191944 | tf_op jit(solution)/shard_map/ppermute | solution.py:505
  10.2 1.8 %fusion.1.both_ref = f32[256,1536]{1,0:T(8,128)S(1)} fusion(bf16[256,2048]{1,0:T(8,128)(2,1)S(1)} %get-tuple-element.33, bf16[2048,1536]{1,0:T(8,128)(2,1)S(1)} %get-tuple-element.31), kind=kOutput, calls=%fused_computation.4 | convolution fusion | flops 1610612736 | bytes 8912896 | tf_op jit(solution)/shard_map/dot_general | solution.py:172
  12.0 0.5 %encode_parts.4 = s16[1552,128]{1,0:T(8,128)(2,1)S(1)} custom-call(f32[256,1536]{1,0:T(8,128)S(1)} %fusion.1.both_ref, f32[128,128]{1,0:T(8,128)S(1)} %get-tuple-element.34.refs_0_), custom_call_target="tpu_custom_call" | custom-call | flops 3932160 | bytes 1966080 | tf_op jit(solution)/shard_map/encode_parts/pallas_call | solution.py:160
  12.4 0.5 %collective-permute-start = (s16[1552,128]{1,0:T(8,128)(2,1)S(1)}, s16[1552,128]{1,0:T(8,128)(2,1)S(1)}, u32[]{:S(2)}, u32[]{:S(2)}) collective-permute-start(s16[1552,128]{1,0:T(8,128)(2,1)S(1)} %encode_parts.4), channel_id=1, source_target_pairs={{0,1},{1,0},{2,3},{3,2},{4,5},{5,4},{6,7},{7,6},{8,9},{9,8},{10,11... | collective-permute-start | bytes 1191944 | tf_op jit(solution)/shard_map/ppermute | solution.py:508
  13.0 1.8 %fusion.2.both_ref = f32[256,1536]{1,0:T(8,128)S(1)} fusion(bf16[256,2048]{1,0:T(8,128)(2,1)S(1)} %get-tuple-element.35, bf16[2048,1536]{1,0:T(8,128)(2,1)S(1)} %get-tuple-element.31), kind=kOutput, calls=%fused_computation.5 | convolution fusion | flops 1610612736 | bytes 8912896 | tf_op jit(solution)/shard_map/dot_general | solution.py:172
  14.8 0.5 %encode_parts.5 = s16[1552,128]{1,0:T(8,128)(2,1)S(1)} custom-call(f32[256,1536]{1,0:T(8,128)S(1)} %fusion.2.both_ref, f32[128,128]{1,0:T(8,128)S(1)} %get-tuple-element.36.refs_0_), custom_call_target="tpu_custom_call" | custom-call | flops 3932160 | bytes 1966080 | tf_op jit(solution)/shard_map/encode_parts/pallas_call | solution.py:160
  16.1 3.7 %side_parts.1 = (bf16[160,1536]{1,0:T(8,128)(2,1)S(1)}, bf16[144,1536]{1,0:T(8,128)(2,1)S(1)}, bf16[144,1536]{1,0:T(8,128)(2,1)S(1)}, bf16[256,2048]{1,0:T(8,128...) custom-call(s32[9]{0:T(128)S(1)} %pad_add_fusion.lists_ref, s32[1,128]{1,0:T(1,128)S(1)} %bitcast.12, ...), custom_call_target="tpu_custom_call" | custom-call | flops 1 | bytes 1 | tf_op jit(solution)/shard_map/side_parts/pallas_call | solution.py:231
  19.8 0.7 %collective-permute-start.4 = (bf16[144,1536]{1,0:T(8,128)(2,1)S(1)}, bf16[144,1536]{1,0:T(8,128)(2,1)S(1)}, u32[]{:S(2)}, u32[]{:S(2)}) collective-permute-start(bf16[144,1536]{1,0:T(8,128)(2,1)S(1)} %get-tuple-element.45), channel_id=1, source_target_pairs={{2,4},{4,2},{6,8},{8,6},{10,12},{12,10},{3,5},{5,3},{7,9},{9,7},{1... | collective-permute-start | bytes 1327112 | tf_op jit(solution)/shard_map/ppermute | solution.py:519
  20.5 1.8 %fusion.3.own_ref = f32[256,1536]{1,0:T(8,128)S(1)} fusion(bf16[256,2048]{1,0:T(8,128)(2,1)S(1)} %get-tuple-element.38, bf16[2048,1536]{1,0:T(8,128)(2,1)S(1)} %get-tuple-element.39), kind=kOutput, calls=%fused_computation.6 | convolution fusion | flops 1610612736 | bytes 8912896 | tf_op jit(solution)/shard_map/dot_general | solution.py:172
  22.3 3.4 %collective-permute-start.3 = (bf16[160,1536]{1,0:T(8,128)(2,1)S(1)}, bf16[160,1536]{1,0:T(8,128)(2,1)S(1)}, u32[]{:S(2)}, u32[]{:S(2)}) collective-permute-start(bf16[160,1536]{1,0:T(8,128)(2,1)S(1)} %get-tuple-element.43), channel_id=1, source_target_pairs={{0,2},{2,0},{4,6},{6,4},{8,10},{10,8},{12,14},{14,12},{1,3},{3,1},... | collective-permute-start | bytes 1474568 | tf_op jit(solution)/shard_map/ppermute | solution.py:518
  25.8 2.4 %collective-permute-done.1.cx_ref = s16[1552,128]{1,0:T(8,128)(2,1)S(1)} collective-permute-done((s16[1552,128]{1,0:T(8,128)(2,1)S(1)}, s16[1552,128]{1,0:T(8,128)(2,1)S(1)}, u32[]{:S(2)}, u32[]{:S(2)}) %collective-permute-start.1) | collective-permute-done | bytes 397344 | tf_op jit(solution)/shard_map/ppermute | solution.py:511
  28.2 0.8 %join_qwen.1 = (bf16[1552,128]{1,0:T(8,128)(2,1)S(1)}, f32[128,128]{1,0:T(8,128)S(1)}) custom-call(f32[256,1536]{1,0:T(8,128)S(1)} %fusion.3.own_ref, f32[128,128]{1,0:T(8,128)S(1)} %get-tuple-element.40.squares_ref, s16[1552,128]{1,0:T(8,128)(2,1)S(1)} %collective-permute-done.cy_ref, s16[1552,128]{1,0:T(8,128)(2,1)S(1)} %collective-permute-done.1.cx_ref, ...), custom_call_target="tpu_custom_call" | custom-call | flops 20000000000 | bytes 8388608 | tf_op jit(solution)/shard_map/join_qwen/pallas_call | solution.py:324
  29.0 0.7 %collective-permute-start.10 = (bf16[1552,128]{1,0:T(8,128)(2,1)S(1)}, bf16[1552,128]{1,0:T(8,128)(2,1)S(1)}, u32[]{:S(2)}, u32[]{:S(2)}) collective-permute-start(bf16[1552,128]{1,0:T(8,128)(2,1)S(1)} %get-tuple-element.49.u_ref), channel_id=1, source_target_pairs={{2,4},{4,2},{6,8},{8,6},{10,12},{12,10},{3,5},{5,3},{7,9},{9,7},{1... | collective-permute-start | bytes 1191944 | tf_op jit(solution)/shard_map/ppermute | solution.py:523
  29.7 1.2 %join_llama.1 = (f32[128,1536]{1,0:T(8,128)S(1)}, f32[8,128]{1,0:T(8,128)S(1)}) custom-call(f32[256,1536]{1,0:T(8,128)S(1)} %fusion.3.own_ref, f32[128,128]{1,0:T(8,128)S(1)} %get-tuple-element.40.squares_ref, s16[1552,128]{1,0:T(8,128)(2,1)S(1)} %collective-permute-done.cy_ref, s16[1552,128]{1,0:T(8,128)(2,1)S(1)} %collective-permute-done.1.cx_ref, ...), custom_call_target="tpu_custom_call" | custom-call | flops 20000000000 | bytes 8388608 | tf_op jit(solution)/shard_map/join_llama/pallas_call | solution.py:370
  30.9 3.0 %collective-permute-start.5 = (f32[8,128]{1,0:T(8,128)S(1)}, f32[8,128]{1,0:T(8,128)S(1)}, u32[]{:S(2)}, u32[]{:S(2)}) collective-permute-start(f32[8,128]{1,0:T(8,128)S(1)} %get-tuple-element.47.refs_0_), channel_id=1, source_target_pairs={{0,2},{2,0},{4,6},{6,4},{8,10},{10,8},{12,14},{14,12},{1,3},{3,1},... | collective-permute-start | bytes 12296 | tf_op jit(solution)/shard_map/ppermute | solution.py:481
  33.9 0.8 %collective-permute-done.5.refs_1_ = f32[8,128]{1,0:T(8,128)S(1)} collective-permute-done((f32[8,128]{1,0:T(8,128)S(1)}, f32[8,128]{1,0:T(8,128)S(1)}, u32[]{:S(2)}, u32[]{:S(2)}) %collective-permute-start.5) | collective-permute-done | bytes 4128 | tf_op jit(solution)/shard_map/ppermute | solution.py:481
  35.0 2.6 %collective-permute-start.8 = (f32[16,128]{1,0:T(8,128)S(1)}, f32[16,128]{1,0:T(8,128)S(1)}, u32[]{:S(2)}, u32[]{:S(2)}) collective-permute-start(f32[16,128]{1,0:T(8,128)S(1)} %constant_dynamic-update-slice_fusion), channel_id=1, source_target_pairs={{0,8},{2,10},{4,12},{6,14},{8,0},{10,2},{12,4},{14,6},{1,9},{3,11}... | collective-permute-start | bytes 24584 | tf_op jit(solution)/shard_map/ppermute | solution.py:481
  37.6 1.3 %collective-permute-start.7 = (f32[16,128]{1,0:T(8,128)S(1)}, f32[16,128]{1,0:T(8,128)S(1)}, u32[]{:S(2)}, u32[]{:S(2)}) collective-permute-start(f32[16,128]{1,0:T(8,128)S(1)} %constant_dynamic-update-slice_fusion), channel_id=1, source_target_pairs={{0,12},{2,14},{4,8},{6,10},{8,4},{10,6},{12,0},{14,2},{1,13},{3,15... | collective-permute-start | bytes 24584 | tf_op jit(solution)/shard_map/ppermute | solution.py:481
  39.0 2.0 %map_parts.1 = (f32[128,1536]{1,0:T(8,128)S(1)}, f32[128,128]{1,0:T(8,128)S(1)}) custom-call(s32[9]{0:T(128)S(1)} %pad_add_fusion.lists_ref, bf16[1552,128]{1,0:T(8,128)(2,1)S(1)} %get-tuple-element.49.u_ref, bf16[1552,128]{1,0:T(8,128)(2,1)S(1)} %collective-permute-done.9.near_ref, bf16[1552,128]{1,0:T(8,128)(2,1)S(1)} %collective-permute-done.10.far_ref, ...), custom_call_target="tpu_custom_call" | custom-call | flops 268435456 | bytes 2097152 | tf_op jit(solution)/shard_map/map_parts/pallas_call | solution.py:422
  41.0 2.1 %collective-permute-done.7.refs_3_ = f32[16,128]{1,0:T(8,128)S(1)} collective-permute-done((f32[16,128]{1,0:T(8,128)S(1)}, f32[16,128]{1,0:T(8,128)S(1)}, u32[]{:S(2)}, u32[]{:S(2)}) %collective-permute-start.7) | collective-permute-done | bytes 8224 | tf_op jit(solution)/shard_map/ppermute | solution.py:481
  43.1 1.3 %finish.1 = (f32[128,1536]{1,0:T(8,128)}, f32[1,128]{1,0:T(1,128)}) custom-call(f32[8,128]{1,0:T(8,128)S(1)} %get-tuple-element.47.refs_0_, f32[8,128]{1,0:T(8,128)S(1)} %collective-permute-done.5.refs_1_, f32[16,128]{1,0:T(8,128)S(1)} %collective-permute-done.6.refs_2_, f32[16,128]{1,0:T(8,128)S(1)} %collective-permute-done.7.refs_3_, ...), custom_call_target="tpu_custom_call" | custom-call | flops 3932160 | bytes 2359296 | tf_op jit(solution)/shard_map/finish/pallas_call | solution.py:461
  (22 shorter events, 0.6 us)
Async XLA Ops:
  6.3 19.5 %collective-permute-start.2 = (s16[1552,128]{1,0:T(8,128)(2,1)S(1)}, s16[1552,128]{1,0:T(8,128)(2,1)S(1)}, u32[]{:S(2)}, u32[]{:S(2)}) collective-permute-start(s16[1552,128]{1,0:T(8,128)(2,1)S(1)} %encode_parts.3), channel_id=1, source_target_pairs={{0,17},{1,16},{16,1},{17,0},{2,19},{3,18},{18,3},{19,2},{4,21},{5,... | collective-permute-start | bytes 1191944 | tf_op jit(solution)/shard_map/ppermute | solution.py:505
  12.4 15.7 %collective-permute-start = (s16[1552,128]{1,0:T(8,128)(2,1)S(1)}, s16[1552,128]{1,0:T(8,128)(2,1)S(1)}, u32[]{:S(2)}, u32[]{:S(2)}) collective-permute-start(s16[1552,128]{1,0:T(8,128)(2,1)S(1)} %encode_parts.4), channel_id=1, source_target_pairs={{0,1},{1,0},{2,3},{3,2},{4,5},{5,4},{6,7},{7,6},{8,9},{9,8},{10,11... | collective-permute-start | bytes 1191944 | tf_op jit(solution)/shard_map/ppermute | solution.py:508
  13.0 3.0 %copy-start.2 = (s32[4]{0:T(128)S(1)}, s32[4]{0:T(128)}, u32[]{:S(2)}) copy-start(s32[4]{0:T(128)} %param.12) | copy-start | bytes 52
  13.0 3.0 %copy-start.3 = (s32[4]{0:T(128)S(1)}, s32[4]{0:T(128)}, u32[]{:S(2)}) copy-start(s32[4]{0:T(128)} %param.11) | copy-start | bytes 52
  13.0 3.1 %copy-start.1 = (s32[128]{0:T(128)S(1)}, s32[128]{0:T(128)}, u32[]{:S(2)}) copy-start(s32[128]{0:T(128)} %param.15) | copy-start | bytes 1540
  15.3 12.9 %collective-permute-start.1 = (s16[1552,128]{1,0:T(8,128)(2,1)S(1)}, s16[1552,128]{1,0:T(8,128)(2,1)S(1)}, u32[]{:S(2)}, u32[]{:S(2)}) collective-permute-start(s16[1552,128]{1,0:T(8,128)(2,1)S(1)} %encode_parts.5), channel_id=1, source_target_pairs={{0,16},{16,0},{1,17},{17,1},{2,18},{18,2},{3,19},{19,3},{4,20},{20... | collective-permute-start | bytes 1191944 | tf_op jit(solution)/shard_map/ppermute | solution.py:511
  19.8 9.9 %collective-permute-start.4 = (bf16[144,1536]{1,0:T(8,128)(2,1)S(1)}, bf16[144,1536]{1,0:T(8,128)(2,1)S(1)}, u32[]{:S(2)}, u32[]{:S(2)}) collective-permute-start(bf16[144,1536]{1,0:T(8,128)(2,1)S(1)} %get-tuple-element.45), channel_id=1, source_target_pairs={{2,4},{4,2},{6,8},{8,6},{10,12},{12,10},{3,5},{5,3},{7,9},{9,7},{1... | collective-permute-start | bytes 1327112 | tf_op jit(solution)/shard_map/ppermute | solution.py:519
  22.3 7.4 %collective-permute-start.3 = (bf16[160,1536]{1,0:T(8,128)(2,1)S(1)}, bf16[160,1536]{1,0:T(8,128)(2,1)S(1)}, u32[]{:S(2)}, u32[]{:S(2)}) collective-permute-start(bf16[160,1536]{1,0:T(8,128)(2,1)S(1)} %get-tuple-element.43), channel_id=1, source_target_pairs={{0,2},{2,0},{4,6},{6,4},{8,10},{10,8},{12,14},{14,12},{1,3},{3,1},... | collective-permute-start | bytes 1474568 | tf_op jit(solution)/shard_map/ppermute | solution.py:518
  29.0 9.9 %collective-permute-start.10 = (bf16[1552,128]{1,0:T(8,128)(2,1)S(1)}, bf16[1552,128]{1,0:T(8,128)(2,1)S(1)}, u32[]{:S(2)}, u32[]{:S(2)}) collective-permute-start(bf16[1552,128]{1,0:T(8,128)(2,1)S(1)} %get-tuple-element.49.u_ref), channel_id=1, source_target_pairs={{2,4},{4,2},{6,8},{8,6},{10,12},{12,10},{3,5},{5,3},{7,9},{9,7},{1... | collective-permute-start | bytes 1191944 | tf_op jit(solution)/shard_map/ppermute | solution.py:523
  29.7 9.2 %copy-start = (bf16[4,512,512]{2,1,0:T(8,128)(2,1)S(1)}, bf16[4,512,512]{2,1,0:T(8,128)(2,1)}, u32[]{:S(2)}) copy-start(bf16[4,512,512]{2,1,0:T(8,128)(2,1)} %w_ref.3) | copy-start | bytes 6291460
  30.9 3.8 %collective-permute-start.5 = (f32[8,128]{1,0:T(8,128)S(1)}, f32[8,128]{1,0:T(8,128)S(1)}, u32[]{:S(2)}, u32[]{:S(2)}) collective-permute-start(f32[8,128]{1,0:T(8,128)S(1)} %get-tuple-element.47.refs_0_), channel_id=1, source_target_pairs={{0,2},{2,0},{4,6},{6,4},{8,10},{10,8},{12,14},{14,12},{1,3},{3,1},... | collective-permute-start | bytes 12296 | tf_op jit(solution)/shard_map/ppermute | solution.py:481
  34.7 4.3 %collective-permute-start.9 = (bf16[1552,128]{1,0:T(8,128)(2,1)S(1)}, bf16[1552,128]{1,0:T(8,128)(2,1)S(1)}, u32[]{:S(2)}, u32[]{:S(2)}) collective-permute-start(bf16[1552,128]{1,0:T(8,128)(2,1)S(1)} %get-tuple-element.49.u_ref), channel_id=1, source_target_pairs={{0,2},{2,0},{4,6},{6,4},{8,10},{10,8},{12,14},{14,12},{1,3},{3,1},... | collective-permute-start | bytes 1191944 | tf_op jit(solution)/shard_map/ppermute | solution.py:529
  35.0 6.0 %collective-permute-start.8 = (f32[16,128]{1,0:T(8,128)S(1)}, f32[16,128]{1,0:T(8,128)S(1)}, u32[]{:S(2)}, u32[]{:S(2)}) collective-permute-start(f32[16,128]{1,0:T(8,128)S(1)} %constant_dynamic-update-slice_fusion), channel_id=1, source_target_pairs={{0,8},{2,10},{4,12},{6,14},{8,0},{10,2},{12,4},{14,6},{1,9},{3,11}... | collective-permute-start | bytes 24584 | tf_op jit(solution)/shard_map/ppermute | solution.py:481
  37.6 5.4 %collective-permute-start.7 = (f32[16,128]{1,0:T(8,128)S(1)}, f32[16,128]{1,0:T(8,128)S(1)}, u32[]{:S(2)}, u32[]{:S(2)}) collective-permute-start(f32[16,128]{1,0:T(8,128)S(1)} %constant_dynamic-update-slice_fusion), channel_id=1, source_target_pairs={{0,12},{2,14},{4,8},{6,10},{8,4},{10,6},{12,0},{14,2},{1,13},{3,15... | collective-permute-start | bytes 24584 | tf_op jit(solution)/shard_map/ppermute | solution.py:481
  39.0 4.1 %collective-permute-start.6 = (f32[16,128]{1,0:T(8,128)S(1)}, f32[16,128]{1,0:T(8,128)S(1)}, u32[]{:S(2)}, u32[]{:S(2)}) collective-permute-start(f32[16,128]{1,0:T(8,128)S(1)} %constant_dynamic-update-slice_fusion), channel_id=1, source_target_pairs={{0,4},{2,6},{4,0},{6,2},{8,12},{10,14},{12,8},{14,10},{1,5},{3,7},... | collective-permute-start | bytes 24584 | tf_op jit(solution)/shard_map/ppermute | solution.py:481

commit v10 on v8

--- a/solution.py
+++ b/solution.py
@@ -261,13 +261,18 @@
     return at[:groups], decode_scalar(*at[groups:])
 
 
-def model_logits(mine, features, own_ref, squares_ref, cy_ref, cx_ref, cd_ref, out_ref):
+def model_logits(mine, features, own_ref, squares_ref, cy_ref, cx_ref, cd_ref, out_ref, peak_ref=None):
     rows = squares_ref.shape[0]
     cols = own_ref.shape[1]
 
     def run(scale, at_slab):
+        peak = jnp.full((rows, LANES), -jnp.inf, f32)
         for slab in range(cols // LANES):
-            out_ref[:, pl.ds(slab * LANES, LANES)] = at_slab(slab) * scale
+            logits = at_slab(slab) * scale
+            out_ref[:, pl.ds(slab * LANES, LANES)] = logits
+            peak = jnp.maximum(peak, logits)
+        if peak_ref is not None:
+            peak_ref[...] = peak
 
     @pl.when(mine)
     def _():
@@ -291,16 +296,18 @@
 
         run(lax.rsqrt((squares_x + squares_d) / features + 1e-05), at_slab)
 
+    if peak_ref is not None:
+        return jnp.max(peak_ref[...], axis=1, keepdims=True)
     peak = jnp.full((rows, LANES), -jnp.inf, f32)
     for slab in range(cols // LANES):
         peak = jnp.maximum(peak, out_ref[:, pl.ds(slab * LANES, LANES)])
     return jnp.max(peak, axis=1, keepdims=True)
 
 
-def qwen_kernel(width, blocks, features, own_ref, squares_ref, cy_ref, cx_ref, cd_ref, u_ref, stats_ref, q_ref):
+def qwen_kernel(width, blocks, features, own_ref, squares_ref, cy_ref, cx_ref, cd_ref, u_ref, stats_ref, q_ref, peak_ref):
     rows = squares_ref.shape[0]
     body = blocks * width
-    peak = model_logits(lax.axis_index("mp") == 1, features, own_ref, squares_ref, cy_ref, cx_ref, cd_ref, q_ref)
+    peak = model_logits(lax.axis_index("mp") == 1, features, own_ref, squares_ref, cy_ref, cx_ref, cd_ref, q_ref, peak_ref)
     total = jnp.zeros((rows, 1), f32)
     for j in range(blocks):
         at = pl.ds(j * width, width)
@@ -328,7 +335,7 @@
             jax.ShapeDtypeStruct((cols // LANES * rows + EXTRA, LANES), bf16),
             jax.ShapeDtypeStruct((rows, LANES), f32),
         ],
-        scratch_shapes=[pltpu.VMEM((rows, cols), f32)],
+        scratch_shapes=[pltpu.VMEM((rows, cols), f32), pltpu.VMEM((rows, LANES), f32)],
         compiler_params=params(),
         cost_estimate=pl.CostEstimate(flops=20000000000, bytes_accessed=8 * 1024 * 1024, transcendentals=0),
         name="join_qwen",

time: 43.3 us -> 43.3 us (level)
  no operation moved by 1% of the time
where the time goes in v10:
time: 43.3 us; the launch traced here: 43.1 us
  starting transfers between devices  17.1 us (39%)
  Pallas kernels  13.8 us (32%)
  matrix products  7.11 us (16%)
  waiting for transfers between devices  3.57 us (8%)
  between operations  1.41 us (3%)
    ppermute x4, starting transfers between devices, gather_pieces(): lax.ppermute(sent, 'vocab', [(i, i ^ turn * step) for i in range(shards)])  7.34 us
    dot_general x4, matrix products, product(): return jnp.dot(left, head, preferred_element_type=f32)  7.11 us
    ppermute x1, starting transfers between devices, on_device(): lax.ppermute(to_d, ('mp', 'rows'), [(0, 3), (1, 2), (2, 1), (3, 0)])  3.93 us
    pallas_call x1, Pallas kernels, side_parts(): pl.pallas_call(functools.partial(side_kernel, width, cols // width), in_s...  3.7 us
    ppermute x1, starting transfers between devices, on_device(): near_columns = lax.ppermute(to_near, 'vocab', inside)  3.44 us
    pallas_call x1, Pallas kernels, first_prep(): pl.pallas_call(functools.partial(first_kernel, kinds, rows), in_specs=[hb...  3.35 us
    ppermute x1, waiting for transfers between devices, on_device(): from_x = lax.ppermute(to_x, 'mp', [(0, 1), (1, 0)])  2.43 us
    pallas_call x1, Pallas kernels, map_parts(): pl.pallas_call(functools.partial(map_kernel, width, blocks, shards), in_s...  2.01 us
  transfers between devices with their start and end apart: 11, of which 4 were waited for; matrix products, arithmetic and copies ran while one was open for 13% of the time, Pallas kernels for 20%

profile of v10, /device:TPU:0, one launch (start us, length us, event | category | flops | bytes accessed | tf_op | source)
XLA Modules:
  0.0 43.1 jit_solution(9932608989318304688)
XLA Ops:
  0.6 3.4 %first_prep.1 = (bf16[256,2048]{1,0:T(8,128)(2,1)S(1)}, bf16[256,2048]{1,0:T(8,128)(2,1)S(1)}, bf16[256,2048]{1,0:T(8,128)(2,1)S(1)}, f32[128,128]{1,0:T(8,128)S...) custom-call(bf16[512,2048]{1,0:T(8,128)(2,1)} %bitcast.16, ...), custom_call_target="tpu_custom_call" | custom-call | flops 6291456 | bytes 6291456 | tf_op jit(solution)/shard_map/first_prep/pallas_call | solution.py:124
  4.0 1.8 %fusion.both_ref = f32[256,1536]{1,0:T(8,128)S(1)} fusion(bf16[256,2048]{1,0:T(8,128)(2,1)S(1)} %get-tuple-element.30, bf16[2048,1536]{1,0:T(8,128)(2,1)S(1)} %get-tuple-element.31), kind=kOutput, calls=%fused_computation.3 | convolution fusion | flops 1610612736 | bytes 8912896 | tf_op jit(solution)/shard_map/dot_general | solution.py:172
  5.8 0.5 %encode_parts.3 = s16[1552,128]{1,0:T(8,128)(2,1)S(1)} custom-call(f32[256,1536]{1,0:T(8,128)S(1)} %fusion.both_ref, f32[128,128]{1,0:T(8,128)S(1)} %get-tuple-element.32.refs_0_), custom_call_target="tpu_custom_call" | custom-call | flops 3932160 | bytes 1966080 | tf_op jit(solution)/shard_map/encode_parts/pallas_call | solution.py:160
  6.3 3.9 %collective-permute-start.2 = (s16[1552,128]{1,0:T(8,128)(2,1)S(1)}, s16[1552,128]{1,0:T(8,128)(2,1)S(1)}, u32[]{:S(2)}, u32[]{:S(2)}) collective-permute-start(s16[1552,128]{1,0:T(8,128)(2,1)S(1)} %encode_parts.3), channel_id=1, source_target_pairs={{0,17},{1,16},{16,1},{17,0},{2,19},{3,18},{18,3},{19,2},{4,21},{5,... | collective-permute-start | bytes 1191944 | tf_op jit(solution)/shard_map/ppermute | solution.py:512
  10.2 1.8 %fusion.1.both_ref = f32[256,1536]{1,0:T(8,128)S(1)} fusion(bf16[256,2048]{1,0:T(8,128)(2,1)S(1)} %get-tuple-element.33, bf16[2048,1536]{1,0:T(8,128)(2,1)S(1)} %get-tuple-element.31), kind=kOutput, calls=%fused_computation.4 | convolution fusion | flops 1610612736 | bytes 8912896 | tf_op jit(solution)/shard_map/dot_general | solution.py:172
  12.0 0.5 %encode_parts.4 = s16[1552,128]{1,0:T(8,128)(2,1)S(1)} custom-call(f32[256,1536]{1,0:T(8,128)S(1)} %fusion.1.both_ref, f32[128,128]{1,0:T(8,128)S(1)} %get-tuple-element.34.refs_0_), custom_call_target="tpu_custom_call" | custom-call | flops 3932160 | bytes 1966080 | tf_op jit(solution)/shard_map/encode_parts/pallas_call | solution.py:160
  12.4 0.5 %collective-permute-start = (s16[1552,128]{1,0:T(8,128)(2,1)S(1)}, s16[1552,128]{1,0:T(8,128)(2,1)S(1)}, u32[]{:S(2)}, u32[]{:S(2)}) collective-permute-start(s16[1552,128]{1,0:T(8,128)(2,1)S(1)} %encode_parts.4), channel_id=1, source_target_pairs={{0,1},{1,0},{2,3},{3,2},{4,5},{5,4},{6,7},{7,6},{8,9},{9,8},{10,11... | collective-permute-start | bytes 1191944 | tf_op jit(solution)/shard_map/ppermute | solution.py:515
  13.0 1.8 %fusion.2.both_ref = f32[256,1536]{1,0:T(8,128)S(1)} fusion(bf16[256,2048]{1,0:T(8,128)(2,1)S(1)} %get-tuple-element.35, bf16[2048,1536]{1,0:T(8,128)(2,1)S(1)} %get-tuple-element.31), kind=kOutput, calls=%fused_computation.5 | convolution fusion | flops 1610612736 | bytes 8912896 | tf_op jit(solution)/shard_map/dot_general | solution.py:172
  14.8 0.5 %encode_parts.5 = s16[1552,128]{1,0:T(8,128)(2,1)S(1)} custom-call(f32[256,1536]{1,0:T(8,128)S(1)} %fusion.2.both_ref, f32[128,128]{1,0:T(8,128)S(1)} %get-tuple-element.36.refs_0_), custom_call_target="tpu_custom_call" | custom-call | flops 3932160 | bytes 1966080 | tf_op jit(solution)/shard_map/encode_parts/pallas_call | solution.py:160
  16.1 3.7 %side_parts.1 = (bf16[160,1536]{1,0:T(8,128)(2,1)S(1)}, bf16[144,1536]{1,0:T(8,128)(2,1)S(1)}, bf16[144,1536]{1,0:T(8,128)(2,1)S(1)}, bf16[256,2048]{1,0:T(8,128...) custom-call(s32[9]{0:T(128)S(1)} %pad_add_fusion.lists_ref, s32[1,128]{1,0:T(1,128)S(1)} %bitcast.12, ...), custom_call_target="tpu_custom_call" | custom-call | flops 1 | bytes 1 | tf_op jit(solution)/shard_map/side_parts/pallas_call | solution.py:231
  19.8 0.7 %collective-permute-start.4 = (bf16[144,1536]{1,0:T(8,128)(2,1)S(1)}, bf16[144,1536]{1,0:T(8,128)(2,1)S(1)}, u32[]{:S(2)}, u32[]{:S(2)}) collective-permute-start(bf16[144,1536]{1,0:T(8,128)(2,1)S(1)} %get-tuple-element.45), channel_id=1, source_target_pairs={{2,4},{4,2},{6,8},{8,6},{10,12},{12,10},{3,5},{5,3},{7,9},{9,7},{1... | collective-permute-start | bytes 1327112 | tf_op jit(solution)/shard_map/ppermute | solution.py:526
  20.5 1.8 %fusion.3.own_ref = f32[256,1536]{1,0:T(8,128)S(1)} fusion(bf16[256,2048]{1,0:T(8,128)(2,1)S(1)} %get-tuple-element.38, bf16[2048,1536]{1,0:T(8,128)(2,1)S(1)} %get-tuple-element.39), kind=kOutput, calls=%fused_computation.6 | convolution fusion | flops 1610612736 | bytes 8912896 | tf_op jit(solution)/shard_map/dot_general | solution.py:172
  22.3 3.4 %collective-permute-start.3 = (bf16[160,1536]{1,0:T(8,128)(2,1)S(1)}, bf16[160,1536]{1,0:T(8,128)(2,1)S(1)}, u32[]{:S(2)}, u32[]{:S(2)}) collective-permute-start(bf16[160,1536]{1,0:T(8,128)(2,1)S(1)} %get-tuple-element.43), channel_id=1, source_target_pairs={{0,2},{2,0},{4,6},{6,4},{8,10},{10,8},{12,14},{14,12},{1,3},{3,1},... | collective-permute-start | bytes 1474568 | tf_op jit(solution)/shard_map/ppermute | solution.py:525
  25.8 2.4 %collective-permute-done.1.cx_ref = s16[1552,128]{1,0:T(8,128)(2,1)S(1)} collective-permute-done((s16[1552,128]{1,0:T(8,128)(2,1)S(1)}, s16[1552,128]{1,0:T(8,128)(2,1)S(1)}, u32[]{:S(2)}, u32[]{:S(2)}) %collective-permute-start.1) | collective-permute-done | bytes 397344 | tf_op jit(solution)/shard_map/ppermute | solution.py:518
  28.2 0.8 %join_qwen.1 = (bf16[1552,128]{1,0:T(8,128)(2,1)S(1)}, f32[128,128]{1,0:T(8,128)S(1)}) custom-call(f32[256,1536]{1,0:T(8,128)S(1)} %fusion.3.own_ref, f32[128,128]{1,0:T(8,128)S(1)} %get-tuple-element.40.squares_ref, s16[1552,128]{1,0:T(8,128)(2,1)S(1)} %collective-permute-done.cy_ref, s16[1552,128]{1,0:T(8,128)(2,1)S(1)} %collective-permute-done.1.cx_ref, ...), custom_call_target="tpu_custom_call" | custom-call | flops 20000000000 | bytes 8388608 | tf_op jit(solution)/shard_map/join_qwen/pallas_call | solution.py:331
  29.0 0.7 %collective-permute-start.10 = (bf16[1552,128]{1,0:T(8,128)(2,1)S(1)}, bf16[1552,128]{1,0:T(8,128)(2,1)S(1)}, u32[]{:S(2)}, u32[]{:S(2)}) collective-permute-start(bf16[1552,128]{1,0:T(8,128)(2,1)S(1)} %get-tuple-element.49.u_ref), channel_id=1, source_target_pairs={{2,4},{4,2},{6,8},{8,6},{10,12},{12,10},{3,5},{5,3},{7,9},{9,7},{1... | collective-permute-start | bytes 1191944 | tf_op jit(solution)/shard_map/ppermute | solution.py:530
  29.8 1.2 %join_llama.1 = (f32[128,1536]{1,0:T(8,128)S(1)}, f32[8,128]{1,0:T(8,128)S(1)}) custom-call(f32[256,1536]{1,0:T(8,128)S(1)} %fusion.3.own_ref, f32[128,128]{1,0:T(8,128)S(1)} %get-tuple-element.40.squares_ref, s16[1552,128]{1,0:T(8,128)(2,1)S(1)} %collective-permute-done.cy_ref, s16[1552,128]{1,0:T(8,128)(2,1)S(1)} %collective-permute-done.1.cx_ref, ...), custom_call_target="tpu_custom_call" | custom-call | flops 20000000000 | bytes 8388608 | tf_op jit(solution)/shard_map/join_llama/pallas_call | solution.py:377
  30.9 3.0 %collective-permute-start.5 = (f32[8,128]{1,0:T(8,128)S(1)}, f32[8,128]{1,0:T(8,128)S(1)}, u32[]{:S(2)}, u32[]{:S(2)}) collective-permute-start(f32[8,128]{1,0:T(8,128)S(1)} %get-tuple-element.47.refs_0_), channel_id=1, source_target_pairs={{0,2},{2,0},{4,6},{6,4},{8,10},{10,8},{12,14},{14,12},{1,3},{3,1},... | collective-permute-start | bytes 12296 | tf_op jit(solution)/shard_map/ppermute | solution.py:488
  33.9 0.8 %collective-permute-done.5.refs_1_ = f32[8,128]{1,0:T(8,128)S(1)} collective-permute-done((f32[8,128]{1,0:T(8,128)S(1)}, f32[8,128]{1,0:T(8,128)S(1)}, u32[]{:S(2)}, u32[]{:S(2)}) %collective-permute-start.5) | collective-permute-done | bytes 4128 | tf_op jit(solution)/shard_map/ppermute | solution.py:488
  35.0 2.1 %collective-permute-start.8 = (f32[16,128]{1,0:T(8,128)S(1)}, f32[16,128]{1,0:T(8,128)S(1)}, u32[]{:S(2)}, u32[]{:S(2)}) collective-permute-start(f32[16,128]{1,0:T(8,128)S(1)} %constant_dynamic-update-slice_fusion), channel_id=1, source_target_pairs={{0,12},{2,14},{4,8},{6,10},{8,4},{10,6},{12,0},{14,2},{1,13},{3,15... | collective-permute-start | bytes 24584 | tf_op jit(solution)/shard_map/ppermute | solution.py:488
  37.1 0.9 %collective-permute-start.7 = (f32[16,128]{1,0:T(8,128)S(1)}, f32[16,128]{1,0:T(8,128)S(1)}, u32[]{:S(2)}, u32[]{:S(2)}) collective-permute-start(f32[16,128]{1,0:T(8,128)S(1)} %constant_dynamic-update-slice_fusion), channel_id=1, source_target_pairs={{0,8},{2,10},{4,12},{6,14},{8,0},{10,2},{12,4},{14,6},{1,9},{3,11}... | collective-permute-start | bytes 24584 | tf_op jit(solution)/shard_map/ppermute | solution.py:488
  38.1 1.3 %collective-permute-start.6 = (f32[16,128]{1,0:T(8,128)S(1)}, f32[16,128]{1,0:T(8,128)S(1)}, u32[]{:S(2)}, u32[]{:S(2)}) collective-permute-start(f32[16,128]{1,0:T(8,128)S(1)} %constant_dynamic-update-slice_fusion), channel_id=1, source_target_pairs={{0,4},{2,6},{4,0},{6,2},{8,12},{10,14},{12,8},{14,10},{1,5},{3,7},... | collective-permute-start | bytes 24584 | tf_op jit(solution)/shard_map/ppermute | solution.py:488
  39.4 2.0 %map_parts.1 = (f32[128,1536]{1,0:T(8,128)S(1)}, f32[128,128]{1,0:T(8,128)S(1)}) custom-call(s32[9]{0:T(128)S(1)} %pad_add_fusion.lists_ref, bf16[1552,128]{1,0:T(8,128)(2,1)S(1)} %get-tuple-element.49.u_ref, bf16[1552,128]{1,0:T(8,128)(2,1)S(1)} %collective-permute-done.9.near_ref, bf16[1552,128]{1,0:T(8,128)(2,1)S(1)} %collective-permute-done.10.far_ref, ...), custom_call_target="tpu_custom_call" | custom-call | flops 268435456 | bytes 2097152 | tf_op jit(solution)/shard_map/map_parts/pallas_call | solution.py:429
  41.8 1.3 %finish.1 = (f32[128,1536]{1,0:T(8,128)}, f32[1,128]{1,0:T(1,128)}) custom-call(f32[8,128]{1,0:T(8,128)S(1)} %get-tuple-element.47.refs_0_, f32[8,128]{1,0:T(8,128)S(1)} %collective-permute-done.5.refs_1_, f32[16,128]{1,0:T(8,128)S(1)} %collective-permute-done.6.refs_2_, f32[16,128]{1,0:T(8,128)S(1)} %collective-permute-done.7.refs_3_, ...), custom_call_target="tpu_custom_call" | custom-call | flops 3932160 | bytes 2359296 | tf_op jit(solution)/shard_map/finish/pallas_call | solution.py:468
  (22 shorter events, 0.9 us)
Async XLA Ops:
  6.3 19.5 %collective-permute-start.2 = (s16[1552,128]{1,0:T(8,128)(2,1)S(1)}, s16[1552,128]{1,0:T(8,128)(2,1)S(1)}, u32[]{:S(2)}, u32[]{:S(2)}) collective-permute-start(s16[1552,128]{1,0:T(8,128)(2,1)S(1)} %encode_parts.3), channel_id=1, source_target_pairs={{0,17},{1,16},{16,1},{17,0},{2,19},{3,18},{18,3},{19,2},{4,21},{5,... | collective-permute-start | bytes 1191944 | tf_op jit(solution)/shard_map/ppermute | solution.py:512
  12.4 15.7 %collective-permute-start = (s16[1552,128]{1,0:T(8,128)(2,1)S(1)}, s16[1552,128]{1,0:T(8,128)(2,1)S(1)}, u32[]{:S(2)}, u32[]{:S(2)}) collective-permute-start(s16[1552,128]{1,0:T(8,128)(2,1)S(1)} %encode_parts.4), channel_id=1, source_target_pairs={{0,1},{1,0},{2,3},{3,2},{4,5},{5,4},{6,7},{7,6},{8,9},{9,8},{10,11... | collective-permute-start | bytes 1191944 | tf_op jit(solution)/shard_map/ppermute | solution.py:515
  13.0 3.0 %copy-start.2 = (s32[4]{0:T(128)S(1)}, s32[4]{0:T(128)}, u32[]{:S(2)}) copy-start(s32[4]{0:T(128)} %param.12) | copy-start | bytes 52
  13.0 3.0 %copy-start.3 = (s32[4]{0:T(128)S(1)}, s32[4]{0:T(128)}, u32[]{:S(2)}) copy-start(s32[4]{0:T(128)} %param.11) | copy-start | bytes 52
  13.0 3.1 %copy-start.1 = (s32[128]{0:T(128)S(1)}, s32[128]{0:T(128)}, u32[]{:S(2)}) copy-start(s32[128]{0:T(128)} %param.15) | copy-start | bytes 1540
  15.3 12.9 %collective-permute-start.1 = (s16[1552,128]{1,0:T(8,128)(2,1)S(1)}, s16[1552,128]{1,0:T(8,128)(2,1)S(1)}, u32[]{:S(2)}, u32[]{:S(2)}) collective-permute-start(s16[1552,128]{1,0:T(8,128)(2,1)S(1)} %encode_parts.5), channel_id=1, source_target_pairs={{0,16},{16,0},{1,17},{17,1},{2,18},{18,2},{3,19},{19,3},{4,20},{20... | collective-permute-start | bytes 1191944 | tf_op jit(solution)/shard_map/ppermute | solution.py:518
  19.8 9.9 %collective-permute-start.4 = (bf16[144,1536]{1,0:T(8,128)(2,1)S(1)}, bf16[144,1536]{1,0:T(8,128)(2,1)S(1)}, u32[]{:S(2)}, u32[]{:S(2)}) collective-permute-start(bf16[144,1536]{1,0:T(8,128)(2,1)S(1)} %get-tuple-element.45), channel_id=1, source_target_pairs={{2,4},{4,2},{6,8},{8,6},{10,12},{12,10},{3,5},{5,3},{7,9},{9,7},{1... | collective-permute-start | bytes 1327112 | tf_op jit(solution)/shard_map/ppermute | solution.py:526
  22.3 7.4 %collective-permute-start.3 = (bf16[160,1536]{1,0:T(8,128)(2,1)S(1)}, bf16[160,1536]{1,0:T(8,128)(2,1)S(1)}, u32[]{:S(2)}, u32[]{:S(2)}) collective-permute-start(bf16[160,1536]{1,0:T(8,128)(2,1)S(1)} %get-tuple-element.43), channel_id=1, source_target_pairs={{0,2},{2,0},{4,6},{6,4},{8,10},{10,8},{12,14},{14,12},{1,3},{3,1},... | collective-permute-start | bytes 1474568 | tf_op jit(solution)/shard_map/ppermute | solution.py:525
  29.0 10.4 %collective-permute-start.10 = (bf16[1552,128]{1,0:T(8,128)(2,1)S(1)}, bf16[1552,128]{1,0:T(8,128)(2,1)S(1)}, u32[]{:S(2)}, u32[]{:S(2)}) collective-permute-start(bf16[1552,128]{1,0:T(8,128)(2,1)S(1)} %get-tuple-element.49.u_ref), channel_id=1, source_target_pairs={{2,4},{4,2},{6,8},{8,6},{10,12},{12,10},{3,5},{5,3},{7,9},{9,7},{1... | collective-permute-start | bytes 1191944 | tf_op jit(solution)/shard_map/ppermute | solution.py:530
  29.8 9.7 %copy-start = (bf16[4,512,512]{2,1,0:T(8,128)(2,1)S(1)}, bf16[4,512,512]{2,1,0:T(8,128)(2,1)}, u32[]{:S(2)}) copy-start(bf16[4,512,512]{2,1,0:T(8,128)(2,1)} %w_ref.3) | copy-start | bytes 6291460
  30.9 3.8 %collective-permute-start.5 = (f32[8,128]{1,0:T(8,128)S(1)}, f32[8,128]{1,0:T(8,128)S(1)}, u32[]{:S(2)}, u32[]{:S(2)}) collective-permute-start(f32[8,128]{1,0:T(8,128)S(1)} %get-tuple-element.47.refs_0_), channel_id=1, source_target_pairs={{0,2},{2,0},{4,6},{6,4},{8,10},{10,8},{12,14},{14,12},{1,3},{3,1},... | collective-permute-start | bytes 12296 | tf_op jit(solution)/shard_map/ppermute | solution.py:488
  34.7 4.7 %collective-permute-start.9 = (bf16[1552,128]{1,0:T(8,128)(2,1)S(1)}, bf16[1552,128]{1,0:T(8,128)(2,1)S(1)}, u32[]{:S(2)}, u32[]{:S(2)}) collective-permute-start(bf16[1552,128]{1,0:T(8,128)(2,1)S(1)} %get-tuple-element.49.u_ref), channel_id=1, source_target_pairs={{0,2},{2,0},{4,6},{6,4},{8,10},{10,8},{12,14},{14,12},{1,3},{3,1},... | collective-permute-start | bytes 1191944 | tf_op jit(solution)/shard_map/ppermute | solution.py:536
  35.0 6.4 %collective-permute-start.8 = (f32[16,128]{1,0:T(8,128)S(1)}, f32[16,128]{1,0:T(8,128)S(1)}, u32[]{:S(2)}, u32[]{:S(2)}) collective-permute-start(f32[16,128]{1,0:T(8,128)S(1)} %constant_dynamic-update-slice_fusion), channel_id=1, source_target_pairs={{0,12},{2,14},{4,8},{6,10},{8,4},{10,6},{12,0},{14,2},{1,13},{3,15... | collective-permute-start | bytes 24584 | tf_op jit(solution)/shard_map/ppermute | solution.py:488
  37.1 4.5 %collective-permute-start.7 = (f32[16,128]{1,0:T(8,128)S(1)}, f32[16,128]{1,0:T(8,128)S(1)}, u32[]{:S(2)}, u32[]{:S(2)}) collective-permute-start(f32[16,128]{1,0:T(8,128)S(1)} %constant_dynamic-update-slice_fusion), channel_id=1, source_target_pairs={{0,8},{2,10},{4,12},{6,14},{8,0},{10,2},{12,4},{14,6},{1,9},{3,11}... | collective-permute-start | bytes 24584 | tf_op jit(solution)/shard_map/ppermute | solution.py:488
  38.1 3.7 %collective-permute-start.6 = (f32[16,128]{1,0:T(8,128)S(1)}, f32[16,128]{1,0:T(8,128)S(1)}, u32[]{:S(2)}, u32[]{:S(2)}) collective-permute-start(f32[16,128]{1,0:T(8,128)S(1)} %constant_dynamic-update-slice_fusion), channel_id=1, source_target_pairs={{0,4},{2,6},{4,0},{6,2},{8,12},{10,14},{12,8},{14,10},{1,5},{3,7},... | collective-permute-start | bytes 24584 | tf_op jit(solution)/shard_map/ppermute | solution.py:488
